TPU v7x, 32 devices: a whole 2x2x4 slice. The times are simulated.
32 devices in a mesh: section: 2 (over y), dp: 16 (over z, x, core).
Axes of the slice: x: 2, y: 2, z: 4, core: 2. Of those that a mesh axis runs over, the one named last changes fastest.
Arguments:
- tokens: bfloat16 [49152, 512], P('dp'), may hold values from -6 to 6
- cotangent: bfloat16 [49152, 512], P('dp'), may hold values from -6 to 6
- span_counts: int32 [32, 3], P('dp'), may hold values from 1 to 6, 12 in all within a row
- tail_lens: int32 [32, 3], P('dp'), may hold values from 1 to 128
- ln1_gain: float32 [2, 512], P('section'), may hold values from 0.1 to 1.9
- w_qkv: bfloat16 [2, 512, 1536], P('section'), may hold values from -0.25 to 0.25
- w_out: bfloat16 [2, 512, 512], P('section'), may hold values from -2 to 2
- ln2_gain: float32 [2, 512], P('section'), may hold values from 0.1 to 1.9
- w_up: bfloat16 [2, 512, 2048], P('section'), may hold values from -0.25 to 0.25
- w_down: bfloat16 [2, 2048, 512], P('section'), may hold values from -0.125 to 0.125
Outputs:
- activations: bfloat16 [2, 49152, 512], P('section', 'dp')
- input_grads: bfloat16 [2, 49152, 512], P('section', 'dp')
- grad_ln1: float32 [2, 512], P('section')
- grad_qkv: float32 [2, 512, 1536], P('section')
- grad_out: float32 [2, 512, 512], P('section')
- grad_ln2: float32 [2, 512], P('section')
- grad_up: float32 [2, 512, 2048], P('section')
- grad_down: float32 [2, 2048, 512], P('section')
Inputs may be any that keep to these rules, and one draw needn't show every extreme that they name: `span_counts`: in every row the 3 counts sum to 12 and the largest is exactly 6.
All inputs are finite; a program needn't handle non-finite values.
Results may differ from a plain program's by a relative error of at most 0.02.
Values may be sent and summed in bfloat16 or wider, within the bound.
No kernel may reach another device: no remote copies, remote signals or barrier semaphores. Data moves between devices by JAX's collectives and lax.ppermute only.
A program may use at most 320 MiB of HBM per device.

v0:
```python
import jax
import jax.numpy as jnp
from jax import lax
from jax.sharding import PartitionSpec as P

HEADS = 8
HEAD_DIM = 64
SPAN = 128
MB_BLK = 12


NEG_FILL = -1e30
EPSILON = 1e-05


def shifted(value, axis, by):
    size = lax.axis_size(axis)
    pairs = [(i, i + by) for i in range(size) if 0 <= i + by < size]
    return lax.ppermute(value, axis, pairs)


def norm_scale(values, gain):
    center = values - jnp.mean(values, axis=-1, keepdims=True)
    spread = jnp.mean(center * center, axis=-1, keepdims=True)
    return center * lax.rsqrt(spread + EPSILON) * gain


def gelu_exact(values):
    return jax.nn.gelu(values, approximate=False)


def block_tables(counts, tail_sizes, block_count, span_len):
    seq_ends = jnp.cumsum(counts)
    blocks = jnp.arange(block_count, dtype=jnp.int32)
    seq_of = jnp.sum((blocks[:, None] >= seq_ends[None, :]).astype(jnp.int32), axis=1)
    members = seq_of[:, None] == jnp.arange(counts.shape[0], dtype=jnp.int32)[None, :]
    end_of = jnp.sum(jnp.where(members, seq_ends[None, :], 0), axis=1)
    tail_of = jnp.sum(jnp.where(members, tail_sizes[None, :], 0), axis=1)
    filled = jnp.where(blocks == end_of - 1, tail_of, span_len)
    offsets = jnp.arange(span_len, dtype=jnp.int32)
    live_mask = offsets[None, :] < filled[:, None]
    earlier = (blocks[None, :] < blocks[:, None]) & (seq_of[None, :] == seq_of[:, None])
    return (live_mask, filled, earlier)


def split_heads(qkv_all):
    parts = qkv_all.reshape(MB_BLK, SPAN, 3, HEADS, HEAD_DIM)
    return (parts[:, :, 0], parts[:, :, 1], parts[:, :, 2])


def pooled(qkv_all, live_mask, filled):
    parts = qkv_all.reshape(MB_BLK, SPAN, 3, HEADS, HEAD_DIM)
    sums = jnp.einsum(
        "bsphe,bs->bphe",
        parts[:, :, 1:],
        live_mask.astype(jnp.bfloat16),
        preferred_element_type=jnp.float32,
    )
    means = (sums / filled.astype(jnp.float32)[:, None, None, None]).astype(jnp.bfloat16)
    return (means[:, 0], means[:, 1])


def joint_scores(queries, key_rows, key_sums, live_mask, earlier):
    scale_factor = HEAD_DIM ** (-0.5)
    offsets = jnp.arange(SPAN, dtype=jnp.int32)
    causal = offsets[:, None] >= offsets[None, :]
    local_raw = (
        jnp.einsum("bihe,bjhe->bhij", queries, key_rows, preferred_element_type=jnp.float32)
        * scale_factor
    )
    summary_raw = (
        jnp.einsum("bihe,che->bhic", queries, key_sums, preferred_element_type=jnp.float32)
        * scale_factor
    )
    local_scores = jnp.where(causal[None, None] & live_mask[:, None, None, :], local_raw, NEG_FILL)
    summary_scores = jnp.where(earlier[:, None, None, :], summary_raw, NEG_FILL)
    return (local_scores, summary_scores)


def layer_forward(layer_in, tables, params):
    gain_one, weight_qkv, weight_out, gain_two, weight_up, weight_down = params
    live_mask, filled, earlier = tables
    width = layer_in.shape[1]
    inputs = layer_in.astype(jnp.float32)
    normed = norm_scale(inputs, gain_one).astype(jnp.bfloat16)
    qkv_all = jnp.dot(normed, weight_qkv, preferred_element_type=jnp.float32).astype(jnp.bfloat16)
    key_sums, value_sums = pooled(qkv_all, live_mask, filled)
    queries, key_rows, value_rows = split_heads(qkv_all)
    local_scores, summary_scores = joint_scores(queries, key_rows, key_sums, live_mask, earlier)
    row_top = jnp.maximum(jnp.max(local_scores, axis=-1), jnp.max(summary_scores, axis=-1))[
        ..., None
    ]
    local_exp = jnp.exp(local_scores - row_top)
    summary_exp = jnp.exp(summary_scores - row_top)
    totals = jnp.sum(local_exp, axis=-1, keepdims=True) + jnp.sum(
        summary_exp, axis=-1, keepdims=True
    )
    log_total = row_top + jnp.log(totals)
    local_prob = (local_exp / totals).astype(jnp.bfloat16)
    summary_prob = (summary_exp / totals).astype(jnp.bfloat16)
    mixed = jnp.einsum(
        "bhij,bjhe->bihe", local_prob, value_rows, preferred_element_type=jnp.float32
    )
    mixed = mixed + jnp.einsum(
        "bhic,che->bihe", summary_prob, value_sums, preferred_element_type=jnp.float32
    )
    attended = mixed.reshape(-1, width).astype(jnp.bfloat16)
    hidden = inputs + jnp.dot(attended, weight_out, preferred_element_type=jnp.float32)
    second = norm_scale(hidden, gain_two).astype(jnp.bfloat16)
    upward = jnp.dot(second, weight_up, preferred_element_type=jnp.float32)
    activated = gelu_exact(upward).astype(jnp.bfloat16)
    layer_out = hidden + jnp.dot(activated, weight_down, preferred_element_type=jnp.float32)
    stash = {
        "layer_in": layer_in,
        "normed": normed,
        "qkv_all": qkv_all,
        "key_sums": key_sums,
        "value_sums": value_sums,
        "log_total": log_total,
        "attended": attended,
        "hidden": hidden,
        "second": second,
    }
    stash["upward"] = upward
    stash["activated"] = activated
    return (layer_out, stash)


def mlp_back(stash, grad_out, params):
    gain_two, weight_up, weight_down = (params[3], params[4], params[5])
    second = stash["second"]
    upward = stash["upward"]
    activated = stash["activated"]
    grad_low = grad_out.astype(jnp.bfloat16)
    grad_down = jnp.einsum("tf,td->fd", activated, grad_low, preferred_element_type=jnp.float32)
    grad_act = jnp.einsum("td,fd->tf", grad_low, weight_down, preferred_element_type=jnp.float32)
    gelu_back = jax.vjp(gelu_exact, upward)[1]
    grad_up_in = gelu_back(grad_act)[0].astype(jnp.bfloat16)
    grad_up = jnp.einsum("td,tf->df", second, grad_up_in, preferred_element_type=jnp.float32)
    grad_second = jnp.einsum("tf,df->td", grad_up_in, weight_up, preferred_element_type=jnp.float32)
    norm_back = jax.vjp(norm_scale, stash["hidden"], gain_two)[1]
    grad_hidden, grad_gain = norm_back(grad_second)
    return (grad_out + grad_hidden, (grad_gain, grad_up, grad_down))


def attn_back(stash, tables, grad_hidden, params):
    gain_one, weight_qkv, weight_out = (params[0], params[1], params[2])
    live_mask, filled, earlier = tables
    scale_factor = HEAD_DIM ** (-0.5)
    grad_low = grad_hidden.astype(jnp.bfloat16)
    grad_wout = jnp.einsum(
        "td,te->de", stash["attended"], grad_low, preferred_element_type=jnp.float32
    )
    grad_att = jnp.einsum(
        "te,de->td", grad_low, weight_out, preferred_element_type=jnp.float32
    ).astype(jnp.bfloat16)
    grad_att = grad_att.reshape(MB_BLK, SPAN, HEADS, HEAD_DIM)
    queries, key_rows, value_rows = split_heads(stash["qkv_all"])
    key_sums = stash["key_sums"]
    value_sums = stash["value_sums"]
    local_scores, summary_scores = joint_scores(queries, key_rows, key_sums, live_mask, earlier)
    local_prob = jnp.exp(local_scores - stash["log_total"])
    summary_prob = jnp.exp(summary_scores - stash["log_total"])
    grad_lp = jnp.einsum(
        "bihe,bjhe->bhij", grad_att, value_rows, preferred_element_type=jnp.float32
    )
    grad_sp = jnp.einsum("bihe,che->bhic", grad_att, value_sums, preferred_element_type=jnp.float32)
    grad_vr = jnp.einsum(
        "bhij,bihe->bjhe",
        local_prob.astype(jnp.bfloat16),
        grad_att,
        preferred_element_type=jnp.float32,
    )
    grad_vs = jnp.einsum(
        "bhic,bihe->che",
        summary_prob.astype(jnp.bfloat16),
        grad_att,
        preferred_element_type=jnp.float32,
    )
    row_dot = jnp.sum(local_prob * grad_lp, axis=-1, keepdims=True) + jnp.sum(
        summary_prob * grad_sp, axis=-1, keepdims=True
    )
    grad_ls = (local_prob * (grad_lp - row_dot)).astype(jnp.bfloat16)
    grad_ss = (summary_prob * (grad_sp - row_dot)).astype(jnp.bfloat16)
    grad_q = jnp.einsum("bhij,bjhe->bihe", grad_ls, key_rows, preferred_element_type=jnp.float32)
    grad_q = (
        grad_q + jnp.einsum("bhic,che->bihe", grad_ss, key_sums, preferred_element_type=jnp.float32)
    ) * scale_factor
    grad_k = (
        jnp.einsum("bhij,bihe->bjhe", grad_ls, queries, preferred_element_type=jnp.float32)
        * scale_factor
    )
    grad_ks = (
        jnp.einsum("bhic,bihe->che", grad_ss, queries, preferred_element_type=jnp.float32)
        * scale_factor
    )
    pooled_grads = jnp.stack([grad_ks, grad_vs], axis=1)
    spread_back = lax.optimization_barrier(pooled_grads.astype(jnp.bfloat16)).astype(jnp.float32)
    spread_back = spread_back / filled.astype(jnp.float32)[:, None, None, None]
    live_float = live_mask.astype(jnp.float32)[:, :, None, None]
    grad_k = grad_k + live_float * spread_back[:, None, 0]
    grad_v = grad_vr + live_float * spread_back[:, None, 1]
    grad_rows = jnp.stack([grad_q, grad_k, grad_v], axis=2).astype(jnp.bfloat16)
    grad_rows = grad_rows.reshape(grad_low.shape[0], 3 * grad_low.shape[1])
    grad_wqkv = jnp.einsum(
        "td,te->de", stash["normed"], grad_rows, preferred_element_type=jnp.float32
    )
    grad_normed = jnp.einsum("te,de->td", grad_rows, weight_qkv, preferred_element_type=jnp.float32)
    norm_back = jax.vjp(norm_scale, stash["layer_in"].astype(jnp.float32), gain_one)[1]
    grad_in, grad_gain = norm_back(grad_normed)
    return (grad_hidden + grad_in, (grad_gain, grad_wqkv, grad_wout))


def per_device(
    tokens, cotangent, span_counts, tail_lens, ln1_gain, w_qkv, w_out, ln2_gain, w_up, w_down
):
    section_idx = lax.axis_index("section")
    micro_count = span_counts.shape[0]
    width = tokens.shape[1]
    params = (ln1_gain[0], w_qkv[0], w_out[0], ln2_gain[0], w_up[0], w_down[0])
    token_blocks = tokens.reshape(micro_count, -1, width)
    grad_blocks = cotangent.reshape(micro_count, -1, width)
    received = jnp.zeros_like(token_blocks[0])
    kept = []
    layer_outs = []
    for step_num in range(micro_count + 1):
        own_rows = token_blocks[min(step_num, micro_count - 1)]
        layer_in = jnp.where(section_idx == 0, own_rows, received)
        which = jnp.clip(step_num - section_idx, 0, micro_count - 1)
        counts = lax.dynamic_index_in_dim(span_counts, which, 0, keepdims=False)
        tail_sizes = lax.dynamic_index_in_dim(tail_lens, which, 0, keepdims=False)
        tables = block_tables(counts, tail_sizes, MB_BLK, SPAN)
        layer_out, stash = layer_forward(layer_in, tables, params)
        out_low = layer_out.astype(jnp.bfloat16)
        layer_outs.append(out_low)
        kept.append((stash, tables, which))
        if step_num < micro_count:
            received = shifted(out_low, "section", 1)
    attn_sums = tuple((jnp.zeros(weight.shape, jnp.float32) for weight in params[:3]))
    mlp_sums = tuple((jnp.zeros(weight.shape, jnp.float32) for weight in params[3:]))
    back_in = jnp.zeros_like(received)
    grad_ins = []
    for step_num in range(micro_count + 1):
        stash, tables, which = kept[micro_count - step_num]
        live_rows = tables[0].reshape(-1, 1).astype(jnp.float32)
        seed_rows = (
            lax.dynamic_index_in_dim(grad_blocks, which, 0, keepdims=False).astype(jnp.float32)
            * live_rows
        )
        grad_out = jnp.where(section_idx == 1, seed_rows, back_in.astype(jnp.float32))
        active = jnp.logical_or(
            jnp.logical_and(section_idx == 1, step_num < micro_count),
            jnp.logical_and(section_idx == 0, step_num >= 1),
        )
        grad_hidden, mlp_terms = mlp_back(stash, grad_out, params)
        mlp_sums = tuple(
            (running + jnp.where(active, fresh, 0.0) for running, fresh in zip(mlp_sums, mlp_terms))
        )
        grad_in, attn_terms = attn_back(stash, tables, grad_hidden, params)
        attn_sums = tuple(
            (
                running + jnp.where(active, fresh, 0.0)
                for running, fresh in zip(attn_sums, attn_terms)
            )
        )
        in_low = grad_in.astype(jnp.bfloat16)
        grad_ins.append(in_low)
        if step_num < micro_count:
            back_in = shifted(in_low, "section", -1)
    summed = lax.psum(
        (attn_sums[0], attn_sums[1], attn_sums[2], mlp_sums[0], mlp_sums[1], mlp_sums[2]), "dp"
    )
    activations = jnp.concatenate(
        [
            jnp.where(section_idx == 0, layer_outs[index_m], layer_outs[index_m + 1])
            for index_m in range(micro_count)
        ],
        axis=0,
    )
    input_grads = jnp.concatenate(
        [
            jnp.where(
                section_idx == 0,
                grad_ins[micro_count - index_m],
                grad_ins[micro_count - 1 - index_m],
            )
            for index_m in range(micro_count)
        ],
        axis=0,
    )
    return (
        activations[None],
        input_grads[None],
        summed[0][None],
        summed[1][None],
        summed[2][None],
        summed[3][None],
        summed[4][None],
        summed[5][None],
    )


def solution(mesh):
    return jax.shard_map(
        per_device,
        mesh=mesh,
        in_specs=(
            P("dp", None),
            P("dp", None),
            P("dp", None),
            P("dp", None),
            P("section", None),
            P("section", None, None),
            P("section", None, None),
            P("section", None),
            P("section", None, None),
            P("section", None, None),
        ),
        out_specs=(
            P("section", "dp", None),
            P("section", "dp", None),
            P("section", None),
            P("section", None, None),
            P("section", None, None),
            P("section", None),
            P("section", None, None),
            P("section", None, None),
        ),
        check_vma=False,
    )
```

profile of v0, /device:TPU:0, one launch (start us, length us, event | category | flops | bytes accessed | tf_op | source)
XLA Modules:
  0.0 915.5 jit_solution(3185204247861383125)
XLA Ops:
  23.3 6.6 copy.401
  29.9 9.4 %reshape.808 = bf16[12,128,3,8,64]{1,0,4,3,2:T(8,128)(2,1)} reshape(bf16[1536,1536]{0,1:T(8,128)(2,1)} %copy.401) | data formatting | bytes 9437184 | tf_op jit(solution)/shard_map/reshape | solution.py:47
  39.4 7.5 fusion.416
  72.0 33.0 %multiply_convert_fusion.2 = (bf16[1536,2048]{1,0:T(8,128)(2,1)S(1)}, f32[1536,2048]{1,0:T(8,128)}, f32[1536,2048]{1,0:T(8,128)}) fusion(bf16[1,512,2048]{2,1,0:T(8,128)(2,1)S(1)} %copy-done, f32[1536,512]{0,1:T(8,128)S(1)} %get-tuple-element.151, f32[512]{0:T(512)S(1)} %bitcast.641, f32[1536]{0:T(1024)S(1)} %fusion.379, f32[1536]{0:T(1024)S(1)} %broadcast_multiply_fusion.4), kind=kOutput, calls=%fused_computation.35 | convolution fusion | flops 3428843520 | bytes 36714496 | tf_op jit(solution)/shard_map/dot_general | solution.py:110
  115.7 30.4 %collective-permute-done = bf16[1536,512]{0,1:T(8,128)(2,1)} collective-permute-done((bf16[1536,512]{0,1:T(8,128)(2,1)}, bf16[1536,512]{0,1:T(8,128)(2,1)}, u32[]{:S(2)}, u32[]{:S(2)}) %collective-permute-start) | collective-permute-done | bytes 1572896 | tf_op jit(solution)/shard_map/ppermute | solution.py:19
  154.4 6.7 copy.415
  161.1 9.8 %reshape.811 = bf16[12,128,3,8,64]{1,0,4,3,2:T(8,128)(2,1)} reshape(bf16[1536,1536]{0,1:T(8,128)(2,1)} %copy.415) | data formatting | bytes 9437184 | tf_op jit(solution)/shard_map/reshape | solution.py:47
  192.6 32.7 %multiply_convert_fusion.1 = (bf16[1536,2048]{1,0:T(8,128)(2,1)S(1)}, f32[1536,2048]{1,0:T(8,128)}, f32[1536,2048]{1,0:T(8,128)}) fusion(bf16[1,512,2048]{2,1,0:T(8,128)(2,1)S(1)} %copy-done, f32[1536,512]{0,1:T(8,128)S(1)} %get-tuple-element.158, f32[1536]{0:T(1024)S(1)} %fusion.381, f32[1536]{0:T(1024)S(1)} %broadcast_multiply_fusion.2, f32[512]{0:T(512)S(1)} %bitcast.642), kind=kOutput, calls=%fused_computation.22 | convolution fusion | flops 3428843520 | bytes 36714496 | tf_op jit(solution)/shard_map/dot_general | solution.py:110
  225.3 7.0 broadcast_select_fusion.2
  250.1 18.4 %collective-permute-done.1 = bf16[1536,512]{0,1:T(8,128)(2,1)} collective-permute-done((bf16[1536,512]{0,1:T(8,128)(2,1)}, bf16[1536,512]{0,1:T(8,128)(2,1)}, u32[]{:S(2)}, u32[]{:S(2)}) %collective-permute-start.1) | collective-permute-done | bytes 1572896 | tf_op jit(solution)/shard_map/ppermute | solution.py:19
  276.7 6.6 copy.428
  283.3 9.8 %reshape.814 = bf16[12,128,3,8,64]{1,0,4,3,2:T(8,128)(2,1)} reshape(bf16[1536,1536]{0,1:T(8,128)(2,1)} %copy.428) | data formatting | bytes 9437184 | tf_op jit(solution)/shard_map/reshape | solution.py:47
  314.9 32.9 %multiply_convert_fusion = (bf16[1536,2048]{1,0:T(8,128)(2,1)}, f32[1536,2048]{1,0:T(8,128)}, f32[1536,2048]{1,0:T(8,128)}) fusion(bf16[1,512,2048]{2,1,0:T(8,128)(2,1)S(1)} %copy-done, f32[1536,512]{0,1:T(8,128)S(1)} %get-tuple-element.165, f32[1536]{0:T(1024)S(1)} %fusion.383, f32[1536]{0:T(1024)S(1)} %broadcast_multiply_fusion, f32[512]{0:T(512)S(1)} %bitcast.643), kind=kOutput, calls=%fused_computation.9 | convolution fusion | flops 3428843520 | bytes 36714496 | tf_op jit(solution)/shard_map/dot_general | solution.py:110
  347.8 15.0 %add_convert_fusion.2 = bf16[1536,2048]{1,0:T(8,128)(2,1)} fusion(f32[1536,2048]{1,0:T(8,128)} %get-tuple-element.87, f32[1536,2048]{1,0:T(8,128)} %get-tuple-element.166, bf16[1,2048,512]{2,1,0:T(8,128)(2,1)} %param.19, bf16[1,1536,512]{1,2,0:T(8,128)(2,1)S(1)} %copy-done.34, f32[1536]{0:T(1024)S(1)} %copy-done.134, pred[]{:T(512)S(6)} %eq.163), kind=kOutput, calls=%fused_computation.8 | convolution fusion | flops 3268411392 | bytes 35133440 | tf_op jit(solution)/shard_map/td,fd->tf/dot_general | solution.py:136
  362.8 6.8 multiply_reduce_fusion.5
  384.9 5.6 multiply_reduce_fusion.2
  420.0 8.5 fusion.165
  433.6 21.7 %collective-permute-done.2 = bf16[1536,512]{0,1:T(8,128)(2,1)S(1)} collective-permute-done((bf16[1536,512]{0,1:T(8,128)(2,1)S(1)}, bf16[1536,512]{0,1:T(8,128)(2,1)S(1)}, u32[]{:S(2)}, u32[]{:S(2)}) %collective-permute-start.2) | collective-permute-done | bytes 1572896 | tf_op jit(solution)/shard_map/ppermute | solution.py:19
  456.5 16.3 %add_convert_fusion.1 = bf16[1536,2048]{1,0:T(8,128)(2,1)} fusion(f32[1536,2048]{1,0:T(8,128)} %get-tuple-element.93, f32[1536,2048]{1,0:T(8,128)} %get-tuple-element.159, bf16[1,2048,512]{2,1,0:T(8,128)(2,1)} %param.19, bf16[1536,512]{0,1:T(8,128)(2,1)} %copy-done.72, bf16[1,1536,512]{1,2,0:T(8,128)(2,1)S(1)} %copy-done.39, f32[1536]{0:T(1024)S(1)} %copy-done.126, ...), kind=kOutput, calls=%fused_computation.7 | convolution fusion | flops 3269197824 | bytes 36706304 | tf_op jit(solution)/shard_map/td,fd->tf/dot_general | solution.py:136
  472.8 6.6 multiply_reduce_fusion.4
  529.7 5.7 fusion.321
  544.9 19.3 %collective-permute-done.3 = bf16[1536,512]{0,1:T(8,128)(2,1)S(1)} collective-permute-done((bf16[1536,512]{0,1:T(8,128)(2,1)S(1)}, bf16[1536,512]{0,1:T(8,128)(2,1)S(1)}, u32[]{:S(2)}, u32[]{:S(2)}) %collective-permute-start.3) | collective-permute-done | bytes 1572896 | tf_op jit(solution)/shard_map/ppermute | solution.py:19
  565.3 16.3 %add_convert_fusion = bf16[1536,2048]{1,0:T(8,128)(2,1)} fusion(f32[1536,2048]{1,0:T(8,128)} %get-tuple-element.99, f32[1536,2048]{1,0:T(8,128)} %get-tuple-element.152, bf16[1,2048,512]{2,1,0:T(8,128)(2,1)} %param.19, bf16[1536,512]{0,1:T(8,128)(2,1)} %copy-done.68, bf16[1,1536,512]{1,2,0:T(8,128)(2,1)S(1)} %copy-done.36, f32[1536]{0:T(1024)S(1)} %copy-done.149, ...), kind=kOutput, calls=%fused_computation.6 | convolution fusion | flops 3269197824 | bytes 36706304 | tf_op jit(solution)/shard_map/td,fd->tf/dot_general | solution.py:136
  581.6 6.3 multiply_reduce_fusion.3
  603.4 5.6 multiply_reduce_fusion
  636.6 6.6 fusion.75
  645.3 9.4 %add_bitcast_fusion.1 = f32[1,512,2048]{2,1,0:T(8,128)} fusion(f32[512,2048]{1,0:T(8,128)} %fusion.403, f32[512,2048]{1,0:T(8,128)S(1)} %copy-done.186, bf16[1536,2048]{1,0:T(8,128)(2,1)} %add_convert_fusion, pred[]{:T(512)S(6)} %eq.141, pred[]{:T(512)S(6)} %or.3, pred[]{:T(512)S(6)} %eq.163, f32[1536,512]{0,1:T(8,128)S(1)} %copy-done.43, ...), kind=kOutput, calls=%fused_computation.121 | convolution fusion | flops 3229614080 | bytes 22034436 | tf_op jit(solution)/shard_map/td,tf->df/dot_general | solution.py:139
  655.1 6.2 add_bitcast_fusion
  661.4 8.4 fusion.136
  676.6 6.8 fusion.91
  694.8 33.6 %all-reduce = (f32[1,512]{1,0:T(1,128)}, f32[1,512]{1,0:T(1,128)}) all-reduce(f32[1,512]{1,0:T(1,128)S(1)} %bitcast.653, f32[1,512]{1,0:T(1,128)S(1)} %bitcast.654), channel_id=1, replica_groups=mesh['section'=2,'dp'=16] {'dp'}, use_global_device_ids=true, to_apply=%region_57.58 | all-reduce | flops 1024 | bytes 8192 | tf_op jit(solution)/shard_map/psum | solution.py:270
  728.4 169.4 %all-reduce.4.cloned.1.call-done = (f32[1,512,1536]{2,1,0:T(8,128)}, f32[1,512,512]{2,1,0:T(8,128)}, f32[1,512,2048]{2,1,0:T(8,128)}, f32[1,2048,512]{2,1,0:T(8,128)}) async-done(((f32[1,512,1536]{2,1,0:T(8,128)}, f32[1,512,512]{2,1,0:T(8,128)}, f32[1,512,2048]{2,1,0:T(8,128)}, f32[1,2048,512]{2,1,0:T(8,128)}), (f32[1,512,1536]{2,1,0:T(8,128)}, f32[1,512,512]{2,1,0:T(8,128)}, f32[1,512,2048]{2,1,0:T(8,128)}, ...) | async-done | bytes 12582928 | tf_op jit(solution)/shard_map/psum | solution.py:270
  (634 shorter events, 313.6 us)
Async XLA Ops:
  7.2 64.6 %copy-start = (bf16[1,512,2048]{2,1,0:T(8,128)(2,1)S(1)}, bf16[1,512,2048]{2,1,0:T(8,128)(2,1)}, u32[]{:S(2)}) copy-start(bf16[1,512,2048]{2,1,0:T(8,128)(2,1)} %param.18) | copy-start | bytes 6291460
  7.2 890.7 %all-reduce.4.cloned.1.call-start = ((), (), s32[]{:S(2)}) async-start(), calls=%async_computation | async-start | bytes 25165824 | tf_op jit(solution)/shard_map/psum | solution.py:270
  51.5 131.1 %copy-start.164 = (f32[12]{0:T(128)}, f32[12]{0:T(128)S(1)}, u32[]{:S(2)}) copy-start(f32[12]{0:T(128)S(1)} %get-tuple-element.94) | copy-start | bytes 148
  71.3 33.7 %copy-start.41 = (f32[1536,512]{0,1:T(8,128)}, f32[1536,512]{0,1:T(8,128)S(1)}, u32[]{:S(2)}) copy-start(f32[1536,512]{0,1:T(8,128)S(1)} %get-tuple-element.151) | copy-start | bytes 9437188
  71.3 33.7 %copy-start.145 = (f32[1536]{0:T(1024)}, f32[1536]{0:T(1024)S(1)}, u32[]{:S(2)}) copy-start(f32[1536]{0:T(1024)S(1)} %broadcast_multiply_fusion.4) | copy-start | bytes 18436
  71.7 33.3 %copy-start.137 = (f32[1536]{0:T(1024)}, f32[1536]{0:T(1024)S(1)}, u32[]{:S(2)}) copy-start(f32[1536]{0:T(1024)S(1)} %multiply_reduce_fusion.11) | copy-start | bytes 18436
  71.8 33.2 %copy-start.150 = (f32[1536]{0:T(1024)}, f32[1536]{0:T(1024)S(1)}, u32[]{:S(2)}) copy-start(f32[1536]{0:T(1024)S(1)} %fusion.379) | copy-start | bytes 18436
  72.0 33.0 %copy-start.174 = (bf16[1,2048,512]{2,1,0:T(8,128)(2,1)S(1)}, bf16[1,2048,512]{2,1,0:T(8,128)(2,1)}, u32[]{:S(2)}) copy-start(bf16[1,2048,512]{2,1,0:T(8,128)(2,1)} %param.19) | copy-start | bytes 6291460
  110.0 36.1 %collective-permute-start = (bf16[1536,512]{0,1:T(8,128)(2,1)}, bf16[1536,512]{0,1:T(8,128)(2,1)}, u32[]{:S(2)}, u32[]{:S(2)}) collective-permute-start(bf16[1536,512]{0,1:T(8,128)(2,1)} %fusion.131), channel_id=1, source_target_pairs={{0,16},{1,17},{2,18},{3,19},{4,20},{5,21},{6,22},{7,23},{8,24},{9,... | collective-permute-start | bytes 4718600 | tf_op jit(solution)/shard_map/ppermute | solution.py:19
  115.7 34.1 %copy-start.177 = (bf16[1,512,1536]{2,1,0:T(8,128)(2,1)S(1)}, bf16[1,512,1536]{2,1,0:T(8,128)(2,1)}, u32[]{:S(2)}) copy-start(bf16[1,512,1536]{2,1,0:T(8,128)(2,1)} %param.15) | copy-start | bytes 4718596
  187.2 62.2 %copy-start.107 = (f32[12,8,128]{2,1,0:T(8,128)}, f32[12,8,128]{2,1,0:T(8,128)S(1)}, u32[]{:S(2)}) copy-start(f32[12,8,128]{2,1,0:T(8,128)S(1)} %get-tuple-element.84) | copy-start | bytes 147460
  192.1 33.2 %copy-start.14 = (f32[1536,512]{0,1:T(8,128)}, f32[1536,512]{0,1:T(8,128)S(1)}, u32[]{:S(2)}) copy-start(f32[1536,512]{0,1:T(8,128)S(1)} %get-tuple-element.158) | copy-start | bytes 9437188
  192.1 33.2 %copy-start.147 = (f32[1536]{0:T(1024)}, f32[1536]{0:T(1024)S(1)}, u32[]{:S(2)}) copy-start(f32[1536]{0:T(1024)S(1)} %broadcast_multiply_fusion.2) | copy-start | bytes 18436
  192.5 32.8 %copy-start.141 = (f32[1536]{0:T(1024)}, f32[1536]{0:T(1024)S(1)}, u32[]{:S(2)}) copy-start(f32[1536]{0:T(1024)S(1)} %multiply_reduce_fusion.10) | copy-start | bytes 18436
  192.5 32.8 %copy-start.152 = (f32[1536]{0:T(1024)}, f32[1536]{0:T(1024)S(1)}, u32[]{:S(2)}) copy-start(f32[1536]{0:T(1024)S(1)} %fusion.381) | copy-start | bytes 18436
  192.6 32.8 %copy-start.175 = (bf16[1,2048,512]{2,1,0:T(8,128)(2,1)S(1)}, bf16[1,2048,512]{2,1,0:T(8,128)(2,1)}, u32[]{:S(2)}) copy-start(bf16[1,2048,512]{2,1,0:T(8,128)(2,1)} %param.19) | copy-start | bytes 6291460
  232.4 36.1 %collective-permute-start.1 = (bf16[1536,512]{0,1:T(8,128)(2,1)}, bf16[1536,512]{0,1:T(8,128)(2,1)}, u32[]{:S(2)}, u32[]{:S(2)}) collective-permute-start(bf16[1536,512]{0,1:T(8,128)(2,1)} %get-tuple-element.168), channel_id=1, source_target_pairs={{0,16},{1,17},{2,18},{3,19},{4,20},{5,21},{6,22},{7,23},{8,24},{9,... | collective-permute-start | bytes 4718600 | tf_op jit(solution)/shard_map/ppermute | solution.py:19
  250.0 22.1 %copy-start.178 = (bf16[1,512,1536]{2,1,0:T(8,128)(2,1)S(1)}, bf16[1,512,1536]{2,1,0:T(8,128)(2,1)}, u32[]{:S(2)}) copy-start(bf16[1,512,1536]{2,1,0:T(8,128)(2,1)} %param.15) | copy-start | bytes 4718596
  314.5 55.2 %copy-start.12 = (f32[1536,512]{0,1:T(8,128)}, f32[1536,512]{0,1:T(8,128)S(1)}, u32[]{:S(2)}) copy-start(f32[1536,512]{0,1:T(8,128)S(1)} %get-tuple-element.165) | copy-start | bytes 9437188
  314.9 32.9 %copy-start.34 = (bf16[1,1536,512]{1,2,0:T(8,128)(2,1)S(1)}, bf16[1,1536,512]{1,2,0:T(8,128)(2,1)}, u32[]{:S(2)}) copy-start(bf16[1,1536,512]{1,2,0:T(8,128)(2,1)} %copy.558) | copy-start | bytes 4718596
  314.9 32.9 %copy-start.134 = (f32[1536]{0:T(1024)S(1)}, f32[1536]{0:T(1024)}, u32[]{:S(2)}) copy-start(f32[1536]{0:T(1024)} %get-tuple-element.144) | copy-start | bytes 18436
  418.6 36.7 %collective-permute-start.2 = (bf16[1536,512]{0,1:T(8,128)(2,1)S(1)}, bf16[1536,512]{0,1:T(8,128)(2,1)S(1)}, u32[]{:S(2)}, u32[]{:S(2)}) collective-permute-start(bf16[1536,512]{0,1:T(8,128)(2,1)S(1)} %add_convert_fusion.5), channel_id=1, source_target_pairs={{16,0},{17,1},{18,2},{19,3},{20,4},{21,5},{22,6},{23,7},{24,8},{25... | collective-permute-start | bytes 4718600 | tf_op jit(solution)/shard_map/ppermute | solution.py:19
  428.5 28.0 %copy-start.39 = (bf16[1,1536,512]{1,2,0:T(8,128)(2,1)S(1)}, bf16[1,1536,512]{1,2,0:T(8,128)(2,1)}, u32[]{:S(2)}) copy-start(bf16[1,1536,512]{1,2,0:T(8,128)(2,1)} %copy.557) | copy-start | bytes 4718596
  428.5 27.9 %copy-start.126 = (f32[1536]{0:T(1024)S(1)}, f32[1536]{0:T(1024)}, u32[]{:S(2)}) copy-start(f32[1536]{0:T(1024)} %get-tuple-element.140) | copy-start | bytes 18436
  456.5 16.3 %copy-start.15 = (f32[1536,512]{0,1:T(8,128)S(1)}, f32[1536,512]{0,1:T(8,128)}, u32[]{:S(2)}) copy-start(f32[1536,512]{0,1:T(8,128)} %copy-done.14) | copy-start | bytes 9437188
  456.5 16.3 %copy-start.148 = (f32[1536]{0:T(1024)S(1)}, f32[1536]{0:T(1024)}, u32[]{:S(2)}) copy-start(f32[1536]{0:T(1024)} %copy-done.147) | copy-start | bytes 18436
  456.5 16.3 %copy-start.153 = (f32[1536]{0:T(1024)S(1)}, f32[1536]{0:T(1024)}, u32[]{:S(2)}) copy-start(f32[1536]{0:T(1024)} %copy-done.152) | copy-start | bytes 18436
  528.2 36.0 %collective-permute-start.3 = (bf16[1536,512]{0,1:T(8,128)(2,1)S(1)}, bf16[1536,512]{0,1:T(8,128)(2,1)S(1)}, u32[]{:S(2)}, u32[]{:S(2)}) collective-permute-start(bf16[1536,512]{0,1:T(8,128)(2,1)S(1)} %get-tuple-element.77), channel_id=1, source_target_pairs={{16,0},{17,1},{18,2},{19,3},{20,4},{21,5},{22,6},{23,7},{24,8},{25... | collective-permute-start | bytes 4718600 | tf_op jit(solution)/shard_map/ppermute | solution.py:19
  539.8 25.5 %copy-start.36 = (bf16[1,1536,512]{1,2,0:T(8,128)(2,1)S(1)}, bf16[1,1536,512]{1,2,0:T(8,128)(2,1)}, u32[]{:S(2)}) copy-start(bf16[1,1536,512]{1,2,0:T(8,128)(2,1)} %copy.556) | copy-start | bytes 4718596
  539.8 25.5 %copy-start.149 = (f32[1536]{0:T(1024)S(1)}, f32[1536]{0:T(1024)}, u32[]{:S(2)}) copy-start(f32[1536]{0:T(1024)} %get-tuple-element.136) | copy-start | bytes 18436
  565.3 16.3 %copy-start.146 = (f32[1536]{0:T(1024)S(1)}, f32[1536]{0:T(1024)}, u32[]{:S(2)}) copy-start(f32[1536]{0:T(1024)} %copy-done.145) | copy-start | bytes 18436
  565.3 16.3 %copy-start.151 = (f32[1536]{0:T(1024)S(1)}, f32[1536]{0:T(1024)}, u32[]{:S(2)}) copy-start(f32[1536]{0:T(1024)} %copy-done.150) | copy-start | bytes 18436
  (179 other events, 837.3 us)
Sparse Core Ops, SparseCore 0:
  661.5 236.3 all-reduce.3
where the time goes:
time: 924 us; the launch traced here: 915 us
  matrix products  362 us (39%)
  waiting for transfers between devices  259 us (28%)
  local copies, waits for them, and re-layouts  177 us (19%)
  other arithmetic  57.3 us (6%)
  blocking collectives  33.6 us (4%)
  between operations  17 us (2%)
  starting transfers between devices  9.76 us (1%)
    psum x1, waiting for transfers between devices, per_device(): lax.psum((attn_sums[0], attn_sums[1], attn_sums[2], mlp_sums[0], mlp_sums...  169 us
    dot_general x3, matrix products, layer_forward(): upward = jnp.dot(second, weight_up, preferred_element_type=jnp.float32)  98.6 us
    ppermute x4, waiting for transfers between devices, shifted(): return lax.ppermute(value, axis, pairs)  89.8 us
    unnamed x419, local copies, waits for them, and re-layouts  53 us
    dot_general x3, matrix products, mlp_back(): jnp.einsum('td,fd->tf', grad_low, weight_down, preferred_element_type=jnp...  47.6 us
    psum x1, blocking collectives, per_device(): lax.psum((attn_sums[0], attn_sums[1], attn_sums[2], mlp_sums[0], mlp_sums...  33.6 us
    reshape x3, local copies, waits for them, and re-layouts, split_heads(): parts = qkv_all.reshape(MB_BLK, SPAN, 3, HEADS, HEAD_DIM)  29 us
    dot_general x3, matrix products, layer_forward(): jnp.dot(activated, weight_down, preferred_element_type=jnp.float32)  20.4 us
  transfers between devices with their start and end apart: 5, of which 5 were waited for; matrix products, arithmetic and copies ran while one was open for 8% of the time, Pallas kernels for 0%

commit v1 on v0

v1 whole, which is shorter than its diff:
```python
import functools

import jax
import jax.numpy as jnp
from jax import lax
from jax.experimental import pallas as pl
from jax.experimental.pallas import tpu as pltpu
from jax.sharding import PartitionSpec as P

D = 512
HEADS = 8
HEAD_DIM = 64
FF = 2048
SPAN = 128
MB_BLK = 12
MB_TOK = MB_BLK * SPAN
PAD_BLK = 16
SUMS = HEADS * PAD_BLK
EPSILON = 1e-05
NEG_FILL = -1e30
BF = jnp.bfloat16
F32 = jnp.float32
VMEM_LIMIT = 58 * 2**20

TILE = 512
TILE_BLK = TILE // SPAN
N_TILE = MB_TOK // TILE
FF_STEP = 512


def dot(left, right, left_dim, right_dim):
    return lax.dot_general(
        left, right, (((left_dim,), (right_dim,)), ((), ())), preferred_element_type=F32
    )


def block_facts(meta_ref, block):
    end_one = meta_ref[0]
    end_two = end_one + meta_ref[1]
    in_one = block < end_one
    in_two = block < end_two
    first = jnp.where(in_one, 0, jnp.where(in_two, end_one, end_two))
    last = jnp.where(in_one, end_one, jnp.where(in_two, end_two, MB_BLK)) - 1
    tail = jnp.where(in_one, meta_ref[3], jnp.where(in_two, meta_ref[4], meta_ref[5]))
    filled = jnp.where(block == last, tail, SPAN)
    return filled, first


def filled_column(meta_ref, width):
    rows = lax.broadcasted_iota(jnp.int32, (PAD_BLK, width), 0)
    out = jnp.full((PAD_BLK, width), SPAN, jnp.int32)
    for block in range(MB_BLK):
        filled, _ = block_facts(meta_ref, block)
        out = jnp.where(rows == block, filled, out)
    return out.astype(F32)


def member_mask(meta_ref, tile_start):
    parts = []
    rows = lax.broadcasted_iota(jnp.int32, (PAD_BLK, SPAN), 0)
    cols = lax.broadcasted_iota(jnp.int32, (PAD_BLK, SPAN), 1)
    for j in range(TILE_BLK):
        block = tile_start + j
        filled, _ = block_facts(meta_ref, block)
        parts.append(jnp.where((rows == block) & (cols < filled), 1.0, 0.0).astype(BF))
    return jnp.concatenate(parts, axis=1)


def head_mask():
    rows = lax.broadcasted_iota(jnp.int32, (SUMS, D), 0) // PAD_BLK
    cols = lax.broadcasted_iota(jnp.int32, (SUMS, D), 1) // HEAD_DIM
    return rows == cols


def spread_heads(sums):
    return jnp.where(head_mask(), jnp.concatenate([sums] * HEADS, axis=0), jnp.zeros((), sums.dtype))


def pair_diag(rows_two):
    zero = jnp.zeros((HEAD_DIM, SPAN), rows_two.dtype)
    top = jnp.concatenate([rows_two[:HEAD_DIM], zero], axis=1)
    low = jnp.concatenate([zero, rows_two[HEAD_DIM:]], axis=1)
    return jnp.concatenate([top, low], axis=0)


def diag_rows(square):
    return jnp.concatenate([square[:HEAD_DIM, :SPAN], square[HEAD_DIM:, SPAN:]], axis=0)


def gain_column(gain_ref):
    return jnp.broadcast_to(gain_ref[...], (SPAN, D)).T


def times_gain(values, gain):
    return jnp.concatenate(
        [values[:, i * SPAN:(i + 1) * SPAN] * gain for i in range(values.shape[1] // SPAN)], axis=1
    )


def normalize(values):
    mean = jnp.sum(values, axis=0, keepdims=True) * (1.0 / D)
    center = values - mean
    spread = jnp.sum(center * center, axis=0, keepdims=True) * (1.0 / D)
    factor = lax.rsqrt(spread + EPSILON)
    return center * factor, factor


def local_mask(filled):
    keys = lax.broadcasted_iota(jnp.int32, (SPAN, 2 * SPAN), 0)
    rows = lax.broadcasted_iota(jnp.int32, (SPAN, 2 * SPAN), 1) % SPAN
    return (keys <= rows) & (keys < filled)


def summary_mask(block, first):
    cols = lax.broadcasted_iota(jnp.int32, (PAD_BLK, 2 * SPAN), 0)
    return (cols >= first) & (cols < block)


def pair_of(array, hp, cols):
    rows = slice(hp * 2 * PAD_BLK, hp * 2 * PAD_BLK + 2 * PAD_BLK)
    part = array[rows, cols]
    return jnp.concatenate([part[:PAD_BLK], part[PAD_BLK:]], axis=1)


def unpair(value):
    return jnp.concatenate([value[:, :SPAN], value[:, SPAN:]], axis=0)


def forward_kernel(
    meta_ref, x_ref, g1_ref, wqkv_ref, wout_ref, g2_ref, wup_ref, wdown_ref,
    out_ref, xh1_ref, r1_ref, qkv_ref, krow_ref, vrow_ref, lse_ref, att_ref, xh2_ref, r2_ref,
    act_ref, gp_ref, ks_ref, vs_ref,
    psum_ref, attf_ref,
):
    step = pl.program_id(0)
    tile_start = step * TILE_BLK
    x_t = x_ref[...].T.astype(F32)
    xhat, r1 = normalize(x_t)
    xh1_ref[...] = xhat.astype(BF)
    r1_ref[...] = r1
    normed = times_gain(xhat, gain_column(g1_ref)).astype(BF)
    q_t = (dot(wqkv_ref[:, :D], normed, 0, 0) * HEAD_DIM ** (-0.5)).astype(BF)
    k_t = dot(wqkv_ref[:, D:2 * D], normed, 0, 0).astype(BF)
    v_t = dot(wqkv_ref[:, 2 * D:], normed, 0, 0).astype(BF)
    qkv_ref[:D] = q_t
    qkv_ref[D:2 * D] = k_t
    qkv_ref[2 * D:] = v_t
    krow = k_t.T
    vrow = v_t.T
    krow_ref[...] = krow
    vrow_ref[...] = vrow
    members = member_mask(meta_ref, tile_start)
    fill = filled_column(meta_ref, D)
    block_rows = lax.broadcasted_iota(jnp.int32, (PAD_BLK, D), 0)
    fresh = (block_rows >= tile_start) & (block_rows < tile_start + TILE_BLK)

    @pl.when(step == 0)
    def _():
        ks_ref[...] = jnp.zeros_like(ks_ref)
        vs_ref[...] = jnp.zeros_like(vs_ref)

    key_sums = jnp.where(fresh, (dot(members, krow, 1, 0) / fill).astype(BF), ks_ref[...])
    value_sums = jnp.where(fresh, (dot(members, vrow, 1, 0) / fill).astype(BF), vs_ref[...])
    ks_ref[...] = key_sums
    vs_ref[...] = value_sums
    s_sum = dot(spread_heads(key_sums), q_t, 1, 0)
    for j in range(TILE_BLK):
        cols = slice(j * SPAN, (j + 1) * SPAN)
        block = tile_start + j
        filled, first = block_facts(meta_ref, block)
        ok = local_mask(filled)
        ok_sum = summary_mask(block, first)
        for hp in range(HEADS // 2):
            feats = slice(hp * SPAN, (hp + 1) * SPAN)
            scores = dot(krow[cols, feats], pair_diag(q_t[feats, cols]), 1, 0)
            scores = jnp.where(ok, scores, NEG_FILL)
            sums = jnp.where(ok_sum, pair_of(s_sum, hp, cols), NEG_FILL)
            top = jnp.maximum(
                jnp.max(scores, axis=0, keepdims=True), jnp.max(sums, axis=0, keepdims=True)
            )
            probs = jnp.exp(scores - top)
            probs_sum = jnp.exp(sums - top)
            total = jnp.sum(probs, axis=0, keepdims=True) + jnp.sum(probs_sum, axis=0, keepdims=True)
            inverse = 1.0 / total
            logs = top + jnp.log(total)
            lse_ref[2 * hp:2 * hp + 1, cols] = logs[:, :SPAN]
            lse_ref[2 * hp + 1:2 * hp + 2, cols] = logs[:, SPAN:]
            probs = (probs * inverse).astype(BF)
            psum_ref[hp * 2 * PAD_BLK:(hp + 1) * 2 * PAD_BLK, cols] = unpair(
                (probs_sum * inverse).astype(BF)
            )
            attf_ref[feats, cols] = diag_rows(dot(v_t[feats, cols], probs, 1, 0))
    att = (attf_ref[...] + dot(spread_heads(value_sums), psum_ref[...], 0, 0)).astype(BF)
    att_ref[...] = att
    hidden = x_t + dot(wout_ref[...], att, 0, 0)
    xhat2, r2 = normalize(hidden)
    xh2_ref[...] = xhat2.astype(BF)
    r2_ref[...] = r2
    second = times_gain(xhat2, gain_column(g2_ref)).astype(BF)
    total_out = hidden
    for f in range(FF // FF_STEP):
        part = slice(f * FF_STEP, (f + 1) * FF_STEP)
        up = dot(wup_ref[:, part], second, 0, 0)
        bell = jnp.exp(up * up * -0.5)
        phi = 0.5 + 0.5 * lax.erf(up * (0.5 ** 0.5))
        act = (up * phi).astype(BF)
        act_ref[part] = act
        gp_ref[part] = (phi + up * bell * 0.3989422804014327).astype(BF)
        total_out = total_out + dot(wdown_ref[part], act, 0, 0)
    out_ref[...] = total_out.astype(BF).T


def spec(shape, index):
    return pl.BlockSpec(shape, index)


def whole(shape):
    return pl.BlockSpec(shape, lambda t, *_: (0,) * len(shape), pipeline_mode=pl.Buffered(1))


def rows_spec(width):
    return pl.BlockSpec((TILE, width), lambda t, *_: (t, 0))


def cols_spec(height):
    return pl.BlockSpec((height, TILE), lambda t, *_: (0, t))


def layer_forward(meta, x, params, x_offset_tiles=False):
    g1, wqkv, wout, g2, wup, wdown = params
    sds = jax.ShapeDtypeStruct
    if x_offset_tiles:
        x_spec = pl.BlockSpec((TILE, D), lambda t, m: (m[6] * N_TILE + t, 0))
    else:
        x_spec = rows_spec(D)
    return pl.pallas_call(
        forward_kernel,
        out_shape=(
            sds((MB_TOK, D), BF), sds((D, MB_TOK), BF), sds((1, MB_TOK), F32),
            sds((3 * D, MB_TOK), BF), sds((MB_TOK, D), BF), sds((MB_TOK, D), BF),
            sds((HEADS, MB_TOK), F32), sds((D, MB_TOK), BF), sds((D, MB_TOK), BF),
            sds((1, MB_TOK), F32), sds((FF, MB_TOK), BF), sds((FF, MB_TOK), BF),
            sds((PAD_BLK, D), BF), sds((PAD_BLK, D), BF),
        ),
        grid_spec=pltpu.PrefetchScalarGridSpec(
            num_scalar_prefetch=1,
            grid=(N_TILE,),
            in_specs=[
                x_spec, whole((1, D)), whole((D, 3 * D)), whole((D, D)), whole((1, D)),
                whole((D, FF)), whole((FF, D)),
            ],
            out_specs=[
                rows_spec(D), cols_spec(D), cols_spec(1), cols_spec(3 * D), rows_spec(D),
                rows_spec(D), cols_spec(HEADS), cols_spec(D), cols_spec(D), cols_spec(1),
                cols_spec(FF), cols_spec(FF), whole((PAD_BLK, D)), whole((PAD_BLK, D)),
            ],
            scratch_shapes=[pltpu.VMEM((SUMS, TILE), BF), pltpu.VMEM((D, TILE), F32)],
        ),
        compiler_params=pltpu.CompilerParams(vmem_limit_bytes=VMEM_LIMIT),
    )(meta, x, g1, wqkv, wout, g2, wup, wdown)


def mlp_back_kernel(
    meta_ref, seed_ref, act_ref, gp_ref, xh2_ref, r2_ref, att_ref, g2_ref, wup_ref, wdown_ref,
    wout_ref,
    gcat_ref, gln_ref, gh_ref, gatt_ref,
    gdown_acc, gup_acc, gout_acc, gln_acc, *, masked,
):
    step = pl.program_id(0)
    tile = N_TILE - 1 - step

    @pl.when(step == 0)
    def _():
        gdown_acc[...] = jnp.zeros_like(gdown_acc)
        gup_acc[...] = jnp.zeros_like(gup_acc)
        gout_acc[...] = jnp.zeros_like(gout_acc)
        gln_acc[...] = jnp.zeros_like(gln_acc)

    low = seed_ref[...].T
    if masked:
        parts = []
        cols = lax.broadcasted_iota(jnp.int32, (D, SPAN), 1)
        for j in range(TILE_BLK):
            filled, _ = block_facts(meta_ref, tile * TILE_BLK + j)
            part = low[:, j * SPAN:(j + 1) * SPAN]
            parts.append(jnp.where(cols < filled, part, jnp.zeros((), BF)))
        low = jnp.concatenate(parts, axis=1)
    gain = gain_column(g2_ref)
    xhat = xh2_ref[...].astype(F32)
    second = times_gain(xhat, gain).astype(BF)
    e = None
    for f in range(FF // FF_STEP):
        part = slice(f * FF_STEP, (f + 1) * FF_STEP)
        gdown_acc[part] += dot(act_ref[part], low, 1, 1)
        ga = dot(wdown_ref[part], low, 1, 0)
        gui = (ga * gp_ref[part].astype(F32)).astype(BF)
        gup_acc[part] += dot(gui, second, 1, 1)
        term = dot(wup_ref[:, part], gui, 1, 0)
        e = term if e is None else e + term
    prod = e * xhat
    for j in range(TILE_BLK):
        gln_acc[...] += prod[:, j * SPAN:(j + 1) * SPAN]
    f_val = times_gain(e, gain)
    mean_f = jnp.sum(f_val, axis=0, keepdims=True) * (1.0 / D)
    mean_fx = jnp.sum(f_val * xhat, axis=0, keepdims=True) * (1.0 / D)
    gh = low.astype(F32) + r2_ref[...] * (f_val - mean_f - xhat * mean_fx)
    gh_ref[...] = gh
    ghb = gh.astype(BF)
    gout_acc[...] += dot(att_ref[...], ghb, 1, 1)
    gatt_ref[...] = dot(wout_ref[...], ghb, 1, 0).astype(BF)

    @pl.when(step == N_TILE - 1)
    def _():
        gcat_ref[:FF] = gdown_acc[...].astype(BF)
        gcat_ref[FF:2 * FF] = gup_acc[...].astype(BF)
        gcat_ref[2 * FF:] = gout_acc[...].astype(BF)
        gln_ref[...] = jnp.sum(gln_acc[...].T, axis=0, keepdims=True)


def rev_rows(width):
    return pl.BlockSpec((TILE, width), lambda t, *_: (N_TILE - 1 - t, 0))


def rev_cols(height):
    return pl.BlockSpec((height, TILE), lambda t, *_: (0, N_TILE - 1 - t))


def mlp_back(meta, seed, stash, params, masked):
    _, _, wout, g2, wup, wdown = params
    _, _, _, _, _, _, att, xh2, r2, act, gp, _, _ = stash
    sds = jax.ShapeDtypeStruct
    if masked:
        seed_spec = pl.BlockSpec((TILE, D), lambda t, m: (m[6] * N_TILE + N_TILE - 1 - t, 0))
    else:
        seed_spec = rev_rows(D)
    return pl.pallas_call(
        functools.partial(mlp_back_kernel, masked=masked),
        out_shape=(
            sds((2 * FF + D, D), BF), sds((1, D), F32), sds((D, MB_TOK), F32), sds((D, MB_TOK), BF),
        ),
        grid_spec=pltpu.PrefetchScalarGridSpec(
            num_scalar_prefetch=1,
            grid=(N_TILE,),
            in_specs=[
                seed_spec, rev_cols(FF), rev_cols(FF), rev_cols(D), rev_cols(1), rev_cols(D),
                whole((1, D)), whole((D, FF)), whole((FF, D)), whole((D, D)),
            ],
            out_specs=[whole((2 * FF + D, D)), whole((1, D)), rev_cols(D), rev_cols(D)],
            scratch_shapes=[
                pltpu.VMEM((FF, D), F32), pltpu.VMEM((FF, D), F32), pltpu.VMEM((D, D), F32),
                pltpu.VMEM((D, SPAN), F32),
            ],
        ),
        compiler_params=pltpu.CompilerParams(vmem_limit_bytes=VMEM_LIMIT),
    )(meta, seed, act, gp, xh2, r2, att, g2, wup, wdown, wout)


def attn_back_kernel(
    meta_ref, gh_ref, gatt_ref, xh1_ref, r1_ref, qkv_ref, krow_ref, vrow_ref, lse_ref, ks_ref,
    vs_ref, g1_ref, wqkv_ref,
    gin_ref, gqkv_ref, gln_ref,
    gqkv_acc, gln_acc, gks_acc, gvs_acc, rows_ref, psum_ref, dsum_ref,
):
    step = pl.program_id(0)
    tile_start = (N_TILE - 1 - step) * TILE_BLK

    @pl.when(step == 0)
    def _():
        gqkv_acc[...] = jnp.zeros_like(gqkv_acc)
        gln_acc[...] = jnp.zeros_like(gln_acc)
        gks_acc[...] = jnp.zeros_like(gks_acc)
        gvs_acc[...] = jnp.zeros_like(gvs_acc)

    q_t = qkv_ref[:D]
    gatt = gatt_ref[...]
    ks_heads = spread_heads(ks_ref[...])
    vs_heads = spread_heads(vs_ref[...])
    s_sum = dot(ks_heads, q_t, 1, 0)
    dp_sum = dot(vs_heads, gatt, 1, 0)
    for j in range(TILE_BLK):
        cols = slice(j * SPAN, (j + 1) * SPAN)
        block = tile_start + j
        filled, first = block_facts(meta_ref, block)
        ok = local_mask(filled)
        ok_sum = summary_mask(block, first)
        for hp in range(HEADS // 2):
            feats = slice(hp * SPAN, (hp + 1) * SPAN)
            keys = slice(D + hp * SPAN, D + (hp + 1) * SPAN)
            values = slice(2 * D + hp * SPAN, 2 * D + (hp + 1) * SPAN)
            logs = jnp.concatenate(
                [lse_ref[2 * hp:2 * hp + 1, cols], lse_ref[2 * hp + 1:2 * hp + 2, cols]], axis=1
            )
            q_diag = pair_diag(q_t[feats, cols])
            g_diag = pair_diag(gatt[feats, cols])
            scores = jnp.where(ok, dot(krow_ref[cols, feats], q_diag, 1, 0), NEG_FILL)
            probs = jnp.exp(scores - logs)
            dp = dot(vrow_ref[cols, feats], g_diag, 1, 0)
            sums = jnp.where(ok_sum, pair_of(s_sum, hp, cols), NEG_FILL)
            probs_sum = jnp.exp(sums - logs)
            dps = pair_of(dp_sum, hp, cols)
            weighted = probs * dp
            weighted_sum = probs_sum * dps
            delta = jnp.sum(weighted, axis=0, keepdims=True) + jnp.sum(
                weighted_sum, axis=0, keepdims=True
            )
            ds = (probs * (dp - delta)).astype(BF)
            dss = (probs_sum * (dps - delta)).astype(BF)
            sum_rows = slice(hp * 2 * PAD_BLK, (hp + 1) * 2 * PAD_BLK)
            psum_ref[sum_rows, cols] = unpair(probs_sum.astype(BF))
            dsum_ref[sum_rows, cols] = unpair(dss)
            rows_ref[feats, cols] = diag_rows(dot(qkv_ref[keys, cols], ds, 1, 0))
            rows_ref[keys, cols] = dot(q_diag, ds, 1, 1)
            rows_ref[values, cols] = dot(g_diag, probs.astype(BF), 1, 1)
    dsum = dsum_ref[...]
    gks_acc[...] += dot(dsum, q_t, 1, 1)
    gvs_acc[...] += dot(psum_ref[...], gatt, 1, 1)
    heads = head_mask()
    members = member_mask(meta_ref, tile_start)
    fill = filled_column(meta_ref, D)

    def spread_back(acc_ref):
        kept = jnp.where(heads, acc_ref[...], 0.0)
        merged = kept[:PAD_BLK]
        for h in range(1, HEADS):
            merged = merged + kept[h * PAD_BLK:(h + 1) * PAD_BLK]
        back = (merged.astype(BF).astype(F32) / fill).astype(BF)
        return dot(back, members, 0, 0)

    grad_q = (rows_ref[:D] + dot(ks_heads, dsum, 0, 0)) * HEAD_DIM ** (-0.5)
    grad_k = rows_ref[D:2 * D] + spread_back(gks_acc)
    grad_v = rows_ref[2 * D:] + spread_back(gvs_acc)
    gain = gain_column(g1_ref)
    xhat = xh1_ref[...].astype(F32)
    normed = times_gain(xhat, gain).astype(BF)
    e = None
    for i, rows in enumerate((grad_q, grad_k, grad_v)):
        rows = rows.astype(BF)
        part = slice(i * D, (i + 1) * D)
        gqkv_acc[part] += dot(rows, normed, 1, 1)
        term = dot(wqkv_ref[:, part], rows, 1, 0)
        e = term if e is None else e + term
    prod = e * xhat
    for j in range(TILE_BLK):
        gln_acc[...] += prod[:, j * SPAN:(j + 1) * SPAN]
    f_val = times_gain(e, gain)
    mean_f = jnp.sum(f_val, axis=0, keepdims=True) * (1.0 / D)
    mean_fx = jnp.sum(f_val * xhat, axis=0, keepdims=True) * (1.0 / D)
    gin = gh_ref[...] + r1_ref[...] * (f_val - mean_f - xhat * mean_fx)
    gin_ref[...] = gin.astype(BF).T

    @pl.when(step == N_TILE - 1)
    def _():
        gqkv_ref[...] = gqkv_acc[...].astype(BF)
        gln_ref[...] = jnp.sum(gln_acc[...].T, axis=0, keepdims=True)


def attn_back(meta, gh, gatt, stash, params):
    g1, wqkv = params[:2]
    xh1, r1, qkv, krow, vrow, lse, _, _, _, _, _, ks, vs = stash
    sds = jax.ShapeDtypeStruct
    return pl.pallas_call(
        attn_back_kernel,
        out_shape=(sds((MB_TOK, D), BF), sds((3 * D, D), BF), sds((1, D), F32)),
        grid_spec=pltpu.PrefetchScalarGridSpec(
            num_scalar_prefetch=1,
            grid=(N_TILE,),
            in_specs=[
                rev_cols(D), rev_cols(D), rev_cols(D), rev_cols(1), rev_cols(3 * D), rev_rows(D),
                rev_rows(D), rev_cols(HEADS), whole((PAD_BLK, D)), whole((PAD_BLK, D)),
                whole((1, D)), whole((D, 3 * D)),
            ],
            out_specs=[rev_rows(D), whole((3 * D, D)), whole((1, D))],
            scratch_shapes=[
                pltpu.VMEM((3 * D, D), F32), pltpu.VMEM((D, SPAN), F32),
                pltpu.VMEM((SUMS, D), F32), pltpu.VMEM((SUMS, D), F32),
                pltpu.VMEM((3 * D, TILE), F32), pltpu.VMEM((SUMS, TILE), BF),
                pltpu.VMEM((SUMS, TILE), BF),
            ],
        ),
        compiler_params=pltpu.CompilerParams(vmem_limit_bytes=VMEM_LIMIT),
    )(meta, gh, gatt, xh1, r1, qkv, krow, vrow, lse, ks, vs, g1, wqkv)


def axis_bits(axis):
    return lax.axis_size(axis).bit_length() - 1


def swap_bit(value, bit):
    size = lax.axis_size("dp")
    return lax.ppermute(value, "dp", [(i, i ^ (1 << bit)) for i in range(size)])


def reversed_index():
    index = lax.axis_index("dp")
    bits = axis_bits("dp")
    out = jnp.zeros((), jnp.int32)
    for bit in range(bits):
        out = out | (((index >> bit) & 1) << (bits - 1 - bit))
    return out


def scatter_sum(value):
    index = lax.axis_index("dp")
    for bit in range(axis_bits("dp")):
        half = value.shape[0] // 2
        mine = (index >> bit) & 1
        kept = lax.dynamic_slice_in_dim(value, mine * half, half, 0)
        sent = lax.dynamic_slice_in_dim(value, (1 - mine) * half, half, 0)
        value = (kept.astype(F32) + swap_bit(sent, bit).astype(F32)).astype(BF)
    return value


def gather_rows(value):
    index = lax.axis_index("dp")
    for bit in reversed(range(axis_bits("dp"))):
        mine = (index >> bit) & 1
        other = swap_bit(value, bit)
        value = jnp.where(
            mine == 0,
            jnp.concatenate([value, other], axis=0),
            jnp.concatenate([other, value], axis=0),
        )
    return value


def sum_all(value):
    for bit in range(axis_bits("dp")):
        value = value + swap_bit(value, bit)
    return value


def swap_section(value):
    return lax.ppermute(value, "section", [(0, 1), (1, 0)])


def to_section(value, target):
    return lax.ppermute(value, "section", [(1 - target, target)])


def per_device(
    tokens, cotangent, span_counts, tail_lens, ln1_gain, w_qkv, w_out, ln2_gain, w_up, w_down
):
    section = lax.axis_index("section")
    first = section == 0
    size = lax.axis_size("dp")
    meta = jnp.concatenate([
        lax.dynamic_index_in_dim(span_counts, section, 0, keepdims=False),
        lax.dynamic_index_in_dim(tail_lens, section, 0, keepdims=False),
        section.astype(jnp.int32)[None], jnp.zeros((1,), jnp.int32),
    ])
    own = (ln1_gain, w_qkv[0], w_out[0], ln2_gain, w_up[0], w_down[0])
    place = reversed_index()

    def shard_of(weight):
        rows = weight.shape[0] // size
        return lax.dynamic_slice_in_dim(weight, place * rows, rows, 0)

    attn_cat = jnp.concatenate([own[1], own[2]], axis=1)
    other_gains = swap_section(jnp.concatenate([ln1_gain, ln2_gain], axis=0))
    other_attn = gather_rows(swap_section(shard_of(attn_cat)))
    other_up = gather_rows(swap_section(shard_of(own[4])))
    other_down = gather_rows(swap_section(shard_of(own[5])))
    other = (
        other_gains[:1], other_attn[:, :3 * D], other_attn[:, 3 * D:], other_gains[1:],
        other_up, other_down,
    )
    layers = [
        tuple(jnp.where(first, a, b) for a, b in zip(own, other)),
        tuple(jnp.where(first, b, a) for a, b in zip(own, other)),
    ]
    out0 = layer_forward(meta, tokens, layers[0], True)
    act0, stash0 = out0[0], out0[1:]
    act0_in = to_section(act0, 0)
    out1 = layer_forward(meta, act0, layers[1], False)
    act1, stash1 = out1[0], out1[1:]
    act1_in = to_section(act1, 1)
    cat1, ln2_1, gh1, gatt1 = mlp_back(meta, cotangent, stash1, layers[1], True)
    cat1 = scatter_sum(cat1)
    ig1, qkv1, ln1_1 = attn_back(meta, gh1, gatt1, stash1, layers[1])
    ig1_in = to_section(ig1, 1)
    qkv1 = scatter_sum(qkv1)
    cat0, ln2_0, gh0, gatt0 = mlp_back(meta, ig1, stash0, layers[0], False)
    cat0 = scatter_sum(cat0)
    ig0, qkv0, ln1_0 = attn_back(meta, gh0, gatt0, stash0, layers[0])
    ig0_in = to_section(ig0, 0)
    qkv0 = scatter_sum(qkv0)
    lns = sum_all(jnp.concatenate([ln1_0, ln2_0, ln1_1, ln2_1], axis=0))
    lns_in = swap_section(jnp.where(first, lns[2:], lns[:2]))
    lns = jnp.where(first, lns[:2], lns[2:]) + lns_in

    def own_sum(grad0, grad1):
        other_in = swap_section(jnp.where(first, grad1, grad0))
        mine = jnp.where(first, grad0, grad1)
        return gather_rows((mine.astype(F32) + other_in.astype(F32)).astype(BF))

    cat = own_sum(cat0, cat1)
    qkv = own_sum(qkv0, qkv1)
    activations = jnp.concatenate(
        [jnp.where(first, act0, act1_in), jnp.where(first, act0_in, act1)], axis=0
    )
    input_grads = jnp.concatenate(
        [jnp.where(first, ig0, ig1_in), jnp.where(first, ig0_in, ig1)], axis=0
    )
    return (
        activations[None],
        input_grads[None],
        lns[:1],
        qkv.T.astype(F32)[None],
        cat[2 * FF:].astype(F32)[None],
        lns[1:],
        cat[FF:2 * FF].T.astype(F32)[None],
        cat[:FF].astype(F32)[None],
    )


def solution(mesh):
    return jax.shard_map(
        per_device,
        mesh=mesh,
        in_specs=(
            P("dp", None),
            P("dp", None),
            P("dp", None),
            P("dp", None),
            P("section", None),
            P("section", None, None),
            P("section", None, None),
            P("section", None),
            P("section", None, None),
            P("section", None, None),
        ),
        out_specs=(
            P("section", "dp", None),
            P("section", "dp", None),
            P("section", None),
            P("section", None, None),
            P("section", None, None),
            P("section", None),
            P("section", None, None),
            P("section", None, None),
        ),
        check_vma=False,
    )
```

time: 924 us -> 528 us (0.57)
  matrix products: 362 us -> 0 us
  Pallas kernels: 0 us -> 162 us
  local copies, waits for them, and re-layouts: 177 us -> 20.4 us
  starting transfers between devices: 9.76 us -> 62.7 us
  blocking collectives: 33.6 us -> 0 us
  waiting for transfers between devices: 259 us -> 228 us
  between operations: 17 us -> 1.58 us
    dot_general x75 -> x0, matrix products: 362 us -> none  [the longest x3 98.6 us: layer_forward(): upward = jnp.dot(second, weight_up, preferred_element_type=jnp.float32)]
    psum x1 -> x0, waiting for transfers between devices: 169 us -> none  [per_device(): lax.psum((attn_sums[0], attn_sums[1], attn_sums[2], mlp_sums[0], mlp_sums...]
    pallas_call x0 -> x6, Pallas kernels: none -> 162 us  [the longest x2 55.8 us: attn_back(): pl.pallas_call(attn_back_kernel, out_shape=(sds((MB_TOK, D), BF), sds((3...]
    ppermute x4 -> x51, waiting for transfers between devices: 89.8 us -> 228 us  [the longest x40 184 us: swap_bit(): return lax.ppermute(value, 'dp', [(i, i ^ 1 << bit) for i in range(size)])]
    ppermute x4 -> x51, starting transfers between devices: 9.72 us -> 62.7 us  [the longest x40 43.1 us: swap_bit(): return lax.ppermute(value, 'dp', [(i, i ^ 1 << bit) for i in range(size)])]
    unnamed x419 -> x42, local copies, waits for them, and re-layouts: 53 us -> 8.81 us
    convert_element_type x12 -> x0, local copies, waits for them, and re-layouts: 44.1 us -> none  [the longest x3 19.9 us: layer_forward(): jnp.dot(normed, weight_qkv, preferred_element_type=jnp.float32)]
    reshape x6 -> x0, local copies, waits for them, and re-layouts: 41.1 us -> none  [the longest x3 29 us: split_heads(): parts = qkv_all.reshape(MB_BLK, SPAN, 3, HEADS, HEAD_DIM)]
  transfers between devices with their start and end apart: 5 -> 51, of which waited for: 5 -> 26; matrix products, arithmetic and copies ran while one was open for 8% -> 9% of each run, Pallas kernels for 0% -> 16%
where the time goes in v1:
time: 528 us; the launch traced here: 524 us
  waiting for transfers between devices  228 us (43%)
  Pallas kernels  162 us (31%)
  starting transfers between devices  62.7 us (12%)
  other arithmetic  50.1 us (9%)
  local copies, waits for them, and re-layouts  20.4 us (4%)
    ppermute x40, waiting for transfers between devices, swap_bit(): return lax.ppermute(value, 'dp', [(i, i ^ 1 << bit) for i in range(size)])  184 us
    pallas_call x2, Pallas kernels, attn_back(): pl.pallas_call(attn_back_kernel, out_shape=(sds((MB_TOK, D), BF), sds((3...  55.8 us
    pallas_call x2, Pallas kernels, mlp_back(): pl.pallas_call(functools.partial(mlp_back_kernel, masked=masked), out_sha...  53 us
    pallas_call x2, Pallas kernels, layer_forward(): pl.pallas_call(forward_kernel, out_shape=(sds((MB_TOK, D), BF), sds((D, M...  52.7 us
    ppermute x7, waiting for transfers between devices, swap_section(): return lax.ppermute(value, 'section', [(0, 1), (1, 0)])  43.7 us
    ppermute x40, starting transfers between devices, swap_bit(): return lax.ppermute(value, 'dp', [(i, i ^ 1 << bit) for i in range(size)])  43.1 us
    select_n x17, other arithmetic, gather_rows(): jnp.where(mine == 0, jnp.concatenate([value, other], axis=0), jnp.concate...  17.4 us
    select_n x5, other arithmetic, per_device(): jnp.where(first, b, a)  10.8 us
  transfers between devices with their start and end apart: 51, of which 26 were waited for; matrix products, arithmetic and copies ran while one was open for 9% of the time, Pallas kernels for 16%

profile of v1, /device:TPU:0, one launch (start us, length us, event | category | flops | bytes accessed | tf_op | source)
XLA Modules:
  0.0 524.2 jit_solution(15875232140300263300)
XLA Ops:
  14.8 4.0 collective-permute-done.12
  23.3 3.4 collective-permute-start.7
  26.8 4.1 collective-permute-done.13
  39.5 5.1 collective-permute-done.14
  54.4 9.0 %collective-permute-done.9 = bf16[128,2048]{1,0:T(8,128)(2,1)} collective-permute-done((bf16[128,2048]{1,0:T(8,128)(2,1)}, bf16[128,2048]{1,0:T(8,128)(2,1)}, u32[]{:S(2)}, u32[]{:S(2)}) %collective-permute-start.9) | collective-permute-done | bytes 524320 | tf_op jit(solution)/shard_map/ppermute | solution.py:490
  65.4 4.3 bitcast_select_fusion
  77.3 26.2 %shard_map.161 = (bf16[1536,512]{1,0:T(8,128)(2,1)}, bf16[512,1536]{1,0:T(8,128)(2,1)}, f32[1,1536]{1,0:T(1,128)}, bf16[1536,1536]{1,0:T(8,128)(2,1)}, bf16[1536...) custom-call(s32[8]{0:T(128)} %pad_add_fusion.meta_ref, ...), custom_call_target="tpu_custom_call" | custom-call | tf_op jit(solution)/shard_map/pallas_call | solution.py:236
  103.5 26.5 %shard_map.162 = (bf16[1536,512]{1,0:T(8,128)(2,1)}, bf16[512,1536]{1,0:T(8,128)(2,1)}, f32[1,1536]{1,0:T(1,128)}, bf16[1536,1536]{1,0:T(8,128)(2,1)}, bf16[1536...) custom-call(s32[8]{0:T(128)} %pad_add_fusion.meta_ref, ...), custom_call_target="tpu_custom_call" | custom-call | tf_op jit(solution)/shard_map/pallas_call | solution.py:236
  130.1 26.4 %shard_map.163 = (bf16[4608,512]{1,0:T(8,128)(2,1)}, f32[1,512]{1,0:T(1,128)}, f32[512,1536]{1,0:T(8,128)}, bf16[512,1536]{1,0:T(8,128)(2,1)}) custom-call(s32[8]{0:T(128)} %pad_add_fusion.meta_ref, bf16[3072,512]{1,0:T(8,128)(2,1)} %seed_ref.1, bf16[2048,1536]{1,0:T(8,128)(2,1)} %get-tuple-element.52.act_ref, bf16[2048,1536]{1,0:T(8,128)(2,1)} %get-tuple-element.53.gp_ref, ...), custom_call_target="tpu_custom_call" | custom-call | tf_op jit(solution)/shard_map/pallas_call | solution.py:336
  160.1 28.0 %shard_map.164 = (bf16[1536,512]{1,0:T(8,128)(2,1)}, bf16[1536,512]{1,0:T(8,128)(2,1)}, f32[1,512]{1,0:T(1,128)}) custom-call(s32[8]{0:T(128)} %pad_add_fusion.meta_ref, f32[512,1536]{1,0:T(8,128)} %get-tuple-element.57.gh_ref, bf16[512,1536]{1,0:T(8,128)(2,1)} %get-tuple-element.58.gatt_ref, bf16[512,1536]{1,0:T(8,128)(2,1)} %get-tuple-element.59.xh1_ref, ...), custom_call_target="tpu_custom_call" | custom-call | tf_op jit(solution)/shard_map/pallas_call | solution.py:461
  188.1 26.6 %shard_map.165 = (bf16[4608,512]{1,0:T(8,128)(2,1)}, f32[1,512]{1,0:T(1,128)}, f32[512,1536]{1,0:T(8,128)}, bf16[512,1536]{1,0:T(8,128)(2,1)}) custom-call(s32[8]{0:T(128)} %pad_add_fusion.meta_ref, bf16[1536,512]{1,0:T(8,128)(2,1)} %get-tuple-element.67.seed_ref, bf16[2048,1536]{1,0:T(8,128)(2,1)} %get-tuple-element.68.act_ref, ...), custom_call_target="tpu_custom_call" | custom-call | tf_op jit(solution)/shard_map/pallas_call | solution.py:336
  214.8 27.8 %shard_map.166 = (bf16[1536,512]{1,0:T(8,128)(2,1)}, bf16[1536,512]{1,0:T(8,128)(2,1)}, f32[1,512]{1,0:T(1,128)}) custom-call(s32[8]{0:T(128)} %pad_add_fusion.meta_ref, f32[512,1536]{1,0:T(8,128)} %get-tuple-element.73.gh_ref, bf16[512,1536]{1,0:T(8,128)(2,1)} %get-tuple-element.74.gatt_ref, bf16[512,1536]{1,0:T(8,128)(2,1)} %get-tuple-element.75.xh1_ref, ...), custom_call_target="tpu_custom_call" | custom-call | tf_op jit(solution)/shard_map/pallas_call | solution.py:461
  243.4 3.4 constant_dynamic-slice_fusion.7
  254.8 4.7 collective-permute-start.23
  264.1 30.6 %collective-permute-done.24 = f32[2,512]{1,0:T(2,128)S(1)} collective-permute-done((f32[2,512]{1,0:T(2,128)S(1)}, f32[2,512]{1,0:T(2,128)S(1)}, u32[]{:S(2)}, u32[]{:S(2)}) %collective-permute-start.24) | collective-permute-done | bytes 4128 | tf_op jit(solution)/shard_map/ppermute | solution.py:533
  307.5 22.1 %collective-permute-done.43 = bf16[1152,512]{1,0:T(8,128)(2,1)S(1)} collective-permute-done((bf16[1152,512]{1,0:T(8,128)(2,1)S(1)}, bf16[1152,512]{1,0:T(8,128)(2,1)S(1)}, u32[]{:S(2)}, u32[]{:S(2)}) %collective-permute-start.43) | collective-permute-done | bytes 1179680 | tf_op jit(solution)/shard_map/ppermute | solution.py:490
  331.1 23.8 %collective-permute-done.39 = bf16[1152,512]{1,0:T(8,128)(2,1)S(1)} collective-permute-done((bf16[1152,512]{1,0:T(8,128)(2,1)S(1)}, bf16[1152,512]{1,0:T(8,128)(2,1)S(1)}, u32[]{:S(2)}, u32[]{:S(2)}) %collective-permute-start.39) | collective-permute-done | bytes 1179680 | tf_op jit(solution)/shard_map/ppermute | solution.py:490
  357.1 5.9 %collective-permute-done.30 = bf16[384,512]{1,0:T(8,128)(2,1)S(1)} collective-permute-done((bf16[384,512]{1,0:T(8,128)(2,1)S(1)}, bf16[384,512]{1,0:T(8,128)(2,1)S(1)}, u32[]{:S(2)}, u32[]{:S(2)}) %collective-permute-start.30) | collective-permute-done | bytes 393248 | tf_op jit(solution)/shard_map/ppermute | solution.py:490
  364.8 6.4 %collective-permute-done.44 = bf16[576,512]{1,0:T(8,128)(2,1)S(1)} collective-permute-done((bf16[576,512]{1,0:T(8,128)(2,1)S(1)}, bf16[576,512]{1,0:T(8,128)(2,1)S(1)}, u32[]{:S(2)}, u32[]{:S(2)}) %collective-permute-start.44) | collective-permute-done | bytes 589856 | tf_op jit(solution)/shard_map/ppermute | solution.py:490
  372.5 9.6 %collective-permute-done.40 = bf16[576,512]{1,0:T(8,128)(2,1)S(1)} collective-permute-done((bf16[576,512]{1,0:T(8,128)(2,1)S(1)}, bf16[576,512]{1,0:T(8,128)(2,1)S(1)}, u32[]{:S(2)}, u32[]{:S(2)}) %collective-permute-start.40) | collective-permute-done | bytes 589856 | tf_op jit(solution)/shard_map/ppermute | solution.py:490
  385.5 18.7 %collective-permute-done.45 = bf16[288,512]{1,0:T(8,128)(2,1)S(1)} collective-permute-done((bf16[288,512]{1,0:T(8,128)(2,1)S(1)}, bf16[288,512]{1,0:T(8,128)(2,1)S(1)}, u32[]{:S(2)}, u32[]{:S(2)}) %collective-permute-start.45) | collective-permute-done | bytes 294944 | tf_op jit(solution)/shard_map/ppermute | solution.py:490
  404.2 5.1 collective-permute-done.41
  409.5 4.0 collective-permute-done.31
  416.3 7.0 %collective-permute-done.46 = bf16[288,512]{1,0:T(8,128)(2,1)S(1)} collective-permute-done((bf16[288,512]{1,0:T(8,128)(2,1)S(1)}, bf16[288,512]{1,0:T(8,128)(2,1)S(1)}, u32[]{:S(2)}, u32[]{:S(2)}) %collective-permute-start.46) | collective-permute-done | bytes 294944 | tf_op jit(solution)/shard_map/ppermute | solution.py:533
  426.6 15.4 %collective-permute-done.47 = bf16[288,512]{1,0:T(8,128)(2,1)S(1)} collective-permute-done((bf16[288,512]{1,0:T(8,128)(2,1)S(1)}, bf16[288,512]{1,0:T(8,128)(2,1)S(1)}, u32[]{:S(2)}, u32[]{:S(2)}) %collective-permute-start.47) | collective-permute-done | bytes 294944 | tf_op jit(solution)/shard_map/ppermute | solution.py:490
  445.1 4.2 collective-permute-done.28
  462.4 3.5 collective-permute-done.34
  466.1 21.7 %collective-permute-done.49 = bf16[1152,512]{1,0:T(8,128)(2,1)S(1)} collective-permute-done((bf16[1152,512]{1,0:T(8,128)(2,1)S(1)}, bf16[1152,512]{1,0:T(8,128)(2,1)S(1)}, u32[]{:S(2)}, u32[]{:S(2)}) %collective-permute-start.49) | collective-permute-done | bytes 1179680 | tf_op jit(solution)/shard_map/ppermute | solution.py:490
  491.2 10.2 %collective-permute-done.36 = bf16[384,512]{1,0:T(8,128)(2,1)S(1)} collective-permute-done((bf16[384,512]{1,0:T(8,128)(2,1)S(1)}, bf16[384,512]{1,0:T(8,128)(2,1)S(1)}, u32[]{:S(2)}, u32[]{:S(2)}) %collective-permute-start.36) | collective-permute-done | bytes 393248 | tf_op jit(solution)/shard_map/ppermute | solution.py:490
  508.4 4.6 maximum_select_fusion
  512.9 4.6 fusion
  518.6 5.3 %copy.19 = f32[1,512,2048]{2,1,0:T(8,128)} copy(f32[1,512,2048]{1,2,0:T(8,128)} %get-tuple-element.101) | data formatting | bytes 8388608
  (196 shorter events, 120.4 us)
Async XLA Ops:
  13.8 12.9 %collective-permute-start.2 = (bf16[32,2048]{1,0:T(8,128)(2,1)S(1)}, bf16[32,2048]{1,0:T(8,128)(2,1)S(1)}, u32[]{:S(2)}, u32[]{:S(2)}) collective-permute-start(bf16[32,2048]{1,0:T(8,128)(2,1)S(1)} %collective-permute-done.1), channel_id=1, source_target_pairs={{0,8},{1,9},{2,10},{3,11},{4,12},{5,13},{6,14},{7,15},{8,0},{9,1},... | collective-permute-start | bytes 393224 | tf_op jit(solution)/shard_map/ppermute | solution.py:490
  18.9 12.0 %collective-permute-start.13 = (bf16[256,512]{1,0:T(8,128)(2,1)S(1)}, bf16[256,512]{1,0:T(8,128)(2,1)S(1)}, u32[]{:S(2)}, u32[]{:S(2)}) collective-permute-start(bf16[256,512]{1,0:T(8,128)(2,1)S(1)} %maximum_select_fusion.18), channel_id=1, source_target_pairs={{0,4},{1,5},{2,6},{3,7},{4,0},{5,1},{6,2},{7,3},{8,12},{9,13},{10,... | collective-permute-start | bytes 786440 | tf_op jit(solution)/shard_map/ppermute | solution.py:490
  21.6 32.2 %collective-permute-start = (f32[2,512]{1,0:T(2,128)S(1)}, f32[2,512]{1,0:T(2,128)S(1)}, u32[]{:S(2)}, u32[]{:S(2)}) collective-permute-start(f32[2,512]{1,0:T(2,128)S(1)} %pad_maximum_fusion.1), channel_id=1, source_target_pairs={{0,16},{16,0},{1,17},{17,1},{2,18},{18,2},{3,19},{19,3},{4,20},{20... | collective-permute-start | bytes 12296 | tf_op jit(solution)/shard_map/ppermute | solution.py:533
  31.1 13.4 %collective-permute-start.14 = (bf16[512,512]{1,0:T(8,128)(2,1)S(1)}, bf16[512,512]{1,0:T(8,128)(2,1)}, u32[]{:S(2)}, u32[]{:S(2)}) collective-permute-start(bf16[512,512]{1,0:T(8,128)(2,1)S(1)} %maximum_select_fusion.14), channel_id=1, source_target_pairs={{0,2},{1,3},{2,0},{3,1},{4,6},{5,7},{6,4},{7,5},{8,10},{9,11},{10,... | collective-permute-start | bytes 1572872 | tf_op jit(solution)/shard_map/ppermute | solution.py:490
  32.7 13.8 %collective-permute-start.8 = (bf16[64,2048]{1,0:T(8,128)(2,1)S(1)}, bf16[64,2048]{1,0:T(8,128)(2,1)}, u32[]{:S(2)}, u32[]{:S(2)}) collective-permute-start(bf16[64,2048]{1,0:T(8,128)(2,1)S(1)} %maximum_select_fusion.17), channel_id=1, source_target_pairs={{0,4},{1,5},{2,6},{3,7},{4,0},{5,1},{6,2},{7,3},{8,12},{9,13},{10,... | collective-permute-start | bytes 786440 | tf_op jit(solution)/shard_map/ppermute | solution.py:490
  37.4 14.3 %collective-permute-start.4 = (bf16[128,2048]{1,0:T(8,128)(2,1)}, bf16[128,2048]{1,0:T(8,128)(2,1)}, u32[]{:S(2)}, u32[]{:S(2)}) collective-permute-start(bf16[128,2048]{1,0:T(8,128)(2,1)} %maximum_select_fusion.12), channel_id=1, source_target_pairs={{0,2},{1,3},{2,0},{3,1},{4,6},{5,7},{6,4},{7,5},{8,10},{9,11},{10,... | collective-permute-start | bytes 1572872 | tf_op jit(solution)/shard_map/ppermute | solution.py:490
  46.4 18.9 %collective-permute-start.15 = (bf16[1024,512]{1,0:T(8,128)(2,1)S(1)}, bf16[1024,512]{1,0:T(8,128)(2,1)}, u32[]{:S(2)}, u32[]{:S(2)}) collective-permute-start(bf16[1024,512]{1,0:T(8,128)(2,1)S(1)} %maximum_select_fusion.9), channel_id=1, source_target_pairs={{0,1},{1,0},{2,3},{3,2},{4,5},{5,4},{6,7},{7,6},{8,9},{9,8},{10,11... | collective-permute-start | bytes 3145736 | tf_op jit(solution)/shard_map/ppermute | solution.py:490
  48.4 14.9 %collective-permute-start.9 = (bf16[128,2048]{1,0:T(8,128)(2,1)}, bf16[128,2048]{1,0:T(8,128)(2,1)}, u32[]{:S(2)}, u32[]{:S(2)}) collective-permute-start(bf16[128,2048]{1,0:T(8,128)(2,1)} %maximum_select_fusion.13), channel_id=1, source_target_pairs={{0,2},{1,3},{2,0},{3,1},{4,6},{5,7},{6,4},{7,5},{8,10},{9,11},{10,... | collective-permute-start | bytes 1572872 | tf_op jit(solution)/shard_map/ppermute | solution.py:490
  53.7 16.0 %collective-permute-start.5 = (bf16[256,2048]{1,0:T(8,128)(2,1)S(1)}, bf16[256,2048]{1,0:T(8,128)(2,1)S(1)}, u32[]{:S(2)}, u32[]{:S(2)}) collective-permute-start(bf16[256,2048]{1,0:T(8,128)(2,1)S(1)} %maximum_select_fusion.7), channel_id=1, source_target_pairs={{0,1},{1,0},{2,3},{3,2},{4,5},{5,4},{6,7},{7,6},{8,9},{9,8},{10,11... | collective-permute-start | bytes 3145736 | tf_op jit(solution)/shard_map/ppermute | solution.py:490
  159.7 137.9 %collective-permute-start.42 = (bf16[2304,512]{1,0:T(8,128)(2,1)}, bf16[2304,512]{1,0:T(8,128)(2,1)}, u32[]{:S(2)}, u32[]{:S(2)}) collective-permute-start(bf16[2304,512]{1,0:T(8,128)(2,1)} %constant_dynamic-slice_fusion.3), channel_id=1, source_target_pairs={{0,1},{1,0},{2,3},{3,2},{4,5},{5,4},{6,7},{7,6},{8,9},{9,8},{10,11... | collective-permute-start | bytes 7077896 | tf_op jit(solution)/shard_map/ppermute | solution.py:490
  246.8 55.2 %collective-permute-start.38 = (bf16[2304,512]{1,0:T(8,128)(2,1)}, bf16[2304,512]{1,0:T(8,128)(2,1)}, u32[]{:S(2)}, u32[]{:S(2)}) collective-permute-start(bf16[2304,512]{1,0:T(8,128)(2,1)} %constant_dynamic-slice_fusion.7), channel_id=1, source_target_pairs={{0,1},{1,0},{2,3},{3,2},{4,5},{5,4},{6,7},{7,6},{8,9},{9,8},{10,11... | collective-permute-start | bytes 7077896 | tf_op jit(solution)/shard_map/ppermute | solution.py:490
  250.1 45.9 %collective-permute-start.29 = (bf16[768,512]{1,0:T(8,128)(2,1)}, bf16[768,512]{1,0:T(8,128)(2,1)}, u32[]{:S(2)}, u32[]{:S(2)}) collective-permute-start(bf16[768,512]{1,0:T(8,128)(2,1)} %constant_dynamic-slice_fusion.11), channel_id=1, source_target_pairs={{0,1},{1,0},{2,3},{3,2},{4,5},{5,4},{6,7},{7,6},{8,9},{9,8},{10,11... | collective-permute-start | bytes 2359304 | tf_op jit(solution)/shard_map/ppermute | solution.py:490
  259.4 201.4 %collective-permute-start.18 = (bf16[1536,512]{1,0:T(8,128)(2,1)S(1)}, bf16[1536,512]{1,0:T(8,128)(2,1)S(1)}, u32[]{:S(2)}, u32[]{:S(2)}) collective-permute-start(bf16[1536,512]{1,0:T(8,128)(2,1)S(1)} %copy-done.1), channel_id=1, source_target_pairs={{0,16},{1,17},{2,18},{3,19},{4,20},{5,21},{6,22},{7,23},{8,24},{9,... | collective-permute-start | bytes 4718600 | tf_op jit(solution)/shard_map/ppermute | solution.py:537
  262.8 31.9 %collective-permute-start.24 = (f32[2,512]{1,0:T(2,128)S(1)}, f32[2,512]{1,0:T(2,128)S(1)}, u32[]{:S(2)}, u32[]{:S(2)}) collective-permute-start(f32[2,512]{1,0:T(2,128)S(1)} %broadcast_select_fusion.10), channel_id=1, source_target_pairs={{0,16},{16,0},{1,17},{17,1},{2,18},{18,2},{3,19},{19,3},{4,20},{20... | collective-permute-start | bytes 12296 | tf_op jit(solution)/shard_map/ppermute | solution.py:533
  294.7 196.3 %collective-permute-start.17 = (bf16[1536,512]{1,0:T(8,128)(2,1)S(1)}, bf16[1536,512]{1,0:T(8,128)(2,1)S(1)}, u32[]{:S(2)}, u32[]{:S(2)}) collective-permute-start(bf16[1536,512]{1,0:T(8,128)(2,1)S(1)} %copy-done), channel_id=1, source_target_pairs={{16,0},{17,1},{18,2},{19,3},{20,4},{21,5},{22,6},{23,7},{24,8},{25... | collective-permute-start | bytes 4718600 | tf_op jit(solution)/shard_map/ppermute | solution.py:537
  300.8 28.8 %collective-permute-start.43 = (bf16[1152,512]{1,0:T(8,128)(2,1)S(1)}, bf16[1152,512]{1,0:T(8,128)(2,1)S(1)}, u32[]{:S(2)}, u32[]{:S(2)}) collective-permute-start(bf16[1152,512]{1,0:T(8,128)(2,1)S(1)} %constant_dynamic-slice_fusion.2), channel_id=1, source_target_pairs={{0,2},{1,3},{2,0},{3,1},{4,6},{5,7},{6,4},{7,5},{8,10},{9,11},{10,... | collective-permute-start | bytes 3538952 | tf_op jit(solution)/shard_map/ppermute | solution.py:490
  304.5 50.5 %collective-permute-start.39 = (bf16[1152,512]{1,0:T(8,128)(2,1)S(1)}, bf16[1152,512]{1,0:T(8,128)(2,1)S(1)}, u32[]{:S(2)}, u32[]{:S(2)}) collective-permute-start(bf16[1152,512]{1,0:T(8,128)(2,1)S(1)} %constant_dynamic-slice_fusion.6), channel_id=1, source_target_pairs={{0,2},{1,3},{2,0},{3,1},{4,6},{5,7},{6,4},{7,5},{8,10},{9,11},{10,... | collective-permute-start | bytes 3538952 | tf_op jit(solution)/shard_map/ppermute | solution.py:490
  305.8 156.5 %collective-permute-start.19 = (bf16[1536,512]{1,0:T(8,128)(2,1)S(1)}, bf16[1536,512]{1,0:T(8,128)(2,1)S(1)}, u32[]{:S(2)}, u32[]{:S(2)}) collective-permute-start(bf16[1536,512]{1,0:T(8,128)(2,1)S(1)} %copy-done.8), channel_id=1, source_target_pairs={{16,0},{17,1},{18,2},{19,3},{20,4},{21,5},{22,6},{23,7},{24,8},{25... | collective-permute-start | bytes 4718600 | tf_op jit(solution)/shard_map/ppermute | solution.py:537
  329.7 33.3 %collective-permute-start.30 = (bf16[384,512]{1,0:T(8,128)(2,1)S(1)}, bf16[384,512]{1,0:T(8,128)(2,1)S(1)}, u32[]{:S(2)}, u32[]{:S(2)}) collective-permute-start(bf16[384,512]{1,0:T(8,128)(2,1)S(1)} %constant_dynamic-slice_fusion.10), channel_id=1, source_target_pairs={{0,2},{1,3},{2,0},{3,1},{4,6},{5,7},{6,4},{7,5},{8,10},{9,11},{10,... | collective-permute-start | bytes 1179656 | tf_op jit(solution)/shard_map/ppermute | solution.py:490
  354.9 16.3 %collective-permute-start.44 = (bf16[576,512]{1,0:T(8,128)(2,1)S(1)}, bf16[576,512]{1,0:T(8,128)(2,1)S(1)}, u32[]{:S(2)}, u32[]{:S(2)}) collective-permute-start(bf16[576,512]{1,0:T(8,128)(2,1)S(1)} %constant_dynamic-slice_fusion.1), channel_id=1, source_target_pairs={{0,4},{1,5},{2,6},{3,7},{4,0},{5,1},{6,2},{7,3},{8,12},{9,13},{10,... | collective-permute-start | bytes 1769480 | tf_op jit(solution)/shard_map/ppermute | solution.py:490
  362.9 19.1 %collective-permute-start.40 = (bf16[576,512]{1,0:T(8,128)(2,1)S(1)}, bf16[576,512]{1,0:T(8,128)(2,1)S(1)}, u32[]{:S(2)}, u32[]{:S(2)}) collective-permute-start(bf16[576,512]{1,0:T(8,128)(2,1)S(1)} %constant_dynamic-slice_fusion.5), channel_id=1, source_target_pairs={{0,4},{1,5},{2,6},{3,7},{4,0},{5,1},{6,2},{7,3},{8,12},{9,13},{10,... | collective-permute-start | bytes 1769480 | tf_op jit(solution)/shard_map/ppermute | solution.py:490
  382.1 22.1 %collective-permute-start.45 = (bf16[288,512]{1,0:T(8,128)(2,1)S(1)}, bf16[288,512]{1,0:T(8,128)(2,1)S(1)}, u32[]{:S(2)}, u32[]{:S(2)}) collective-permute-start(bf16[288,512]{1,0:T(8,128)(2,1)S(1)} %constant_dynamic-slice_fusion), channel_id=1, source_target_pairs={{0,8},{1,9},{2,10},{3,11},{4,12},{5,13},{6,14},{7,15},{8,0},{9,1},... | collective-permute-start | bytes 884744 | tf_op jit(solution)/shard_map/ppermute | solution.py:490
  382.6 26.7 %collective-permute-start.41 = (bf16[288,512]{1,0:T(8,128)(2,1)S(1)}, bf16[288,512]{1,0:T(8,128)(2,1)S(1)}, u32[]{:S(2)}, u32[]{:S(2)}) collective-permute-start(bf16[288,512]{1,0:T(8,128)(2,1)S(1)} %constant_dynamic-slice_fusion.4), channel_id=1, source_target_pairs={{0,8},{1,9},{2,10},{3,11},{4,12},{5,13},{6,14},{7,15},{8,0},{9,1},... | collective-permute-start | bytes 884744 | tf_op jit(solution)/shard_map/ppermute | solution.py:490
  409.3 14.3 %collective-permute-start.27 = (bf16[192,512]{1,0:T(8,128)(2,1)S(1)}, bf16[192,512]{1,0:T(8,128)(2,1)S(1)}, u32[]{:S(2)}, u32[]{:S(2)}) collective-permute-start(bf16[192,512]{1,0:T(8,128)(2,1)S(1)} %constant_dynamic-slice_fusion.13), channel_id=1, source_target_pairs={{0,4},{1,5},{2,6},{3,7},{4,0},{5,1},{6,2},{7,3},{8,12},{9,13},{10,... | collective-permute-start | bytes 589832 | tf_op jit(solution)/shard_map/ppermute | solution.py:490
  423.3 19.0 %collective-permute-start.32 = (bf16[96,512]{1,0:T(8,128)(2,1)S(1)}, bf16[96,512]{1,0:T(8,128)(2,1)S(1)}, u32[]{:S(2)}, u32[]{:S(2)}) collective-permute-start(bf16[96,512]{1,0:T(8,128)(2,1)S(1)} %constant_dynamic-slice_fusion.8), channel_id=1, source_target_pairs={{0,8},{1,9},{2,10},{3,11},{4,12},{5,13},{6,14},{7,15},{8,0},{9,1},... | collective-permute-start | bytes 294920 | tf_op jit(solution)/shard_map/ppermute | solution.py:490
  423.6 18.5 %collective-permute-start.47 = (bf16[288,512]{1,0:T(8,128)(2,1)S(1)}, bf16[288,512]{1,0:T(8,128)(2,1)S(1)}, u32[]{:S(2)}, u32[]{:S(2)}) collective-permute-start(bf16[288,512]{1,0:T(8,128)(2,1)S(1)} %add_convert_fusion.10), channel_id=1, source_target_pairs={{0,8},{1,9},{2,10},{3,11},{4,12},{5,13},{6,14},{7,15},{8,0},{9,1},... | collective-permute-start | bytes 884744 | tf_op jit(solution)/shard_map/ppermute | solution.py:490
  442.3 17.9 %collective-permute-start.48 = (bf16[576,512]{1,0:T(8,128)(2,1)S(1)}, bf16[576,512]{1,0:T(8,128)(2,1)S(1)}, u32[]{:S(2)}, u32[]{:S(2)}) collective-permute-start(bf16[576,512]{1,0:T(8,128)(2,1)S(1)} %maximum_select_fusion.11), channel_id=1, source_target_pairs={{0,4},{1,5},{2,6},{3,7},{4,0},{5,1},{6,2},{7,3},{8,12},{9,13},{10,... | collective-permute-start | bytes 1769480 | tf_op jit(solution)/shard_map/ppermute | solution.py:490
  454.1 35.4 %collective-permute-start.16 = (bf16[1536,512]{1,0:T(8,128)(2,1)S(1)}, bf16[1536,512]{1,0:T(8,128)(2,1)S(1)}, u32[]{:S(2)}, u32[]{:S(2)}) collective-permute-start(bf16[1536,512]{1,0:T(8,128)(2,1)S(1)} %copy-done.7), channel_id=1, source_target_pairs={{0,16},{1,17},{2,18},{3,19},{4,20},{5,21},{6,22},{7,23},{8,24},{9,... | collective-permute-start | bytes 4718600 | tf_op jit(solution)/shard_map/ppermute | solution.py:537
  460.9 26.9 %collective-permute-start.49 = (bf16[1152,512]{1,0:T(8,128)(2,1)S(1)}, bf16[1152,512]{1,0:T(8,128)(2,1)S(1)}, u32[]{:S(2)}, u32[]{:S(2)}) collective-permute-start(bf16[1152,512]{1,0:T(8,128)(2,1)S(1)} %maximum_select_fusion.6), channel_id=1, source_target_pairs={{0,2},{1,3},{2,0},{3,1},{4,6},{5,7},{6,4},{7,5},{8,10},{9,11},{10,... | collective-permute-start | bytes 3538952 | tf_op jit(solution)/shard_map/ppermute | solution.py:490
  466.0 23.7 %collective-permute-start.35 = (bf16[192,512]{1,0:T(8,128)(2,1)S(1)}, bf16[192,512]{1,0:T(8,128)(2,1)S(1)}, u32[]{:S(2)}, u32[]{:S(2)}) collective-permute-start(bf16[192,512]{1,0:T(8,128)(2,1)S(1)} %maximum_select_fusion.19), channel_id=1, source_target_pairs={{0,4},{1,5},{2,6},{3,7},{4,0},{5,1},{6,2},{7,3},{8,12},{9,13},{10,... | collective-permute-start | bytes 589832 | tf_op jit(solution)/shard_map/ppermute | solution.py:490
  489.5 18.9 %collective-permute-start.50 = (bf16[2304,512]{1,0:T(8,128)(2,1)}, bf16[2304,512]{1,0:T(8,128)(2,1)}, u32[]{:S(2)}, u32[]{:S(2)}) collective-permute-start(bf16[2304,512]{1,0:T(8,128)(2,1)} %maximum_select_fusion.1), channel_id=1, source_target_pairs={{0,1},{1,0},{2,3},{3,2},{4,5},{5,4},{6,7},{7,6},{8,9},{9,8},{10,11... | collective-permute-start | bytes 7077896 | tf_op jit(solution)/shard_map/ppermute | solution.py:490
  489.8 11.6 %collective-permute-start.36 = (bf16[384,512]{1,0:T(8,128)(2,1)S(1)}, bf16[384,512]{1,0:T(8,128)(2,1)S(1)}, u32[]{:S(2)}, u32[]{:S(2)}) collective-permute-start(bf16[384,512]{1,0:T(8,128)(2,1)S(1)} %maximum_select_fusion.15), channel_id=1, source_target_pairs={{0,2},{1,3},{2,0},{3,1},{4,6},{5,7},{6,4},{7,5},{8,10},{9,11},{10,... | collective-permute-start | bytes 1179656 | tf_op jit(solution)/shard_map/ppermute | solution.py:490
  (39 other events, 470.1 us)

commit v2 on v1

v2 whole, which is shorter than its diff:
```python
import functools

import jax
import jax.numpy as jnp
from jax import lax
from jax.experimental import pallas as pl
from jax.experimental.pallas import tpu as pltpu
from jax.sharding import PartitionSpec as P

D = 512
HEADS = 8
HEAD_DIM = 64
FF = 2048
SPAN = 128
MB_BLK = 12
MB_TOK = MB_BLK * SPAN
PAD_BLK = 16
EPSILON = 1e-05
NEG_FILL = -1e30
BF = jnp.bfloat16
F32 = jnp.float32
VMEM_LIMIT = 58 * 2**20

TILE = 512
TILE_BLK = TILE // SPAN
N_TILE = MB_TOK // TILE
FF_STEP = 512
FWD_STEP = 512
FWD_GROUP = 2
BACK_GROUP = 2


def dot(left, right, left_dim, right_dim):
    return lax.dot_general(
        left, right, (((left_dim,), (right_dim,)), ((), ())), preferred_element_type=F32
    )


def block_facts(meta_ref, block):
    end_one = meta_ref[0]
    end_two = end_one + meta_ref[1]
    in_one = block < end_one
    in_two = block < end_two
    first = jnp.where(in_one, 0, jnp.where(in_two, end_one, end_two))
    last = jnp.where(in_one, end_one, jnp.where(in_two, end_two, MB_BLK)) - 1
    tail = jnp.where(in_one, meta_ref[3], jnp.where(in_two, meta_ref[4], meta_ref[5]))
    filled = jnp.where(block == last, tail, SPAN)
    return filled, first


def filled_column(meta_ref, width):
    rows = lax.broadcasted_iota(jnp.int32, (PAD_BLK, width), 0)
    out = jnp.full((PAD_BLK, width), SPAN, jnp.int32)
    for block in range(MB_BLK):
        filled, _ = block_facts(meta_ref, block)
        out = jnp.where(rows == block, filled, out)
    return out.astype(F32)


def filled_row(meta_ref):
    cols = lax.broadcasted_iota(jnp.int32, (1, PAD_BLK), 1)
    out = jnp.full((1, PAD_BLK), SPAN, jnp.int32)
    for block in range(MB_BLK):
        filled, _ = block_facts(meta_ref, block)
        out = jnp.where(cols == block, filled, out)
    return out.astype(F32)


def member_mask(meta_ref, tile_start):
    parts = []
    rows = lax.broadcasted_iota(jnp.int32, (PAD_BLK, SPAN), 0)
    cols = lax.broadcasted_iota(jnp.int32, (PAD_BLK, SPAN), 1)
    for j in range(TILE_BLK):
        block = tile_start + j
        filled, _ = block_facts(meta_ref, block)
        parts.append(jnp.where((rows == block) & (cols < filled), 1.0, 0.0).astype(BF))
    return jnp.concatenate(parts, axis=1)


def pair_diag(rows_two):
    zero = jnp.zeros((HEAD_DIM, SPAN), rows_two.dtype)
    top = jnp.concatenate([rows_two[:HEAD_DIM], zero], axis=1)
    low = jnp.concatenate([zero, rows_two[HEAD_DIM:]], axis=1)
    return jnp.concatenate([top, low], axis=0)


def diag_rows(square):
    return jnp.concatenate([square[:HEAD_DIM, :SPAN], square[HEAD_DIM:, SPAN:]], axis=0)


def gain_column(gains_ref, index):
    return jnp.broadcast_to(gains_ref[index:index + 1], (SPAN, D)).T


def times_gain(values, gain):
    return jnp.concatenate(
        [values[:, i * SPAN:(i + 1) * SPAN] * gain for i in range(values.shape[1] // SPAN)], axis=1
    )


def normalize(values):
    mean = jnp.sum(values, axis=0, keepdims=True) * (1.0 / D)
    center = values - mean
    spread = jnp.sum(center * center, axis=0, keepdims=True) * (1.0 / D)
    factor = lax.rsqrt(spread + EPSILON)
    return center * factor, factor


def score_mask(block, filled, first):
    rows = lax.broadcasted_iota(jnp.int32, (SPAN + PAD_BLK, 2 * SPAN), 0)
    cols = lax.broadcasted_iota(jnp.int32, (SPAN + PAD_BLK, 2 * SPAN), 1) % SPAN
    local = (rows <= cols) & (rows < filled)
    earlier = (rows >= SPAN + first) & (rows < SPAN + block)
    return local | earlier


def attention_items(meta_ref, tile_start, blocks):
    items = []
    for j in blocks:
        filled, first = block_facts(meta_ref, tile_start + j)
        mask = score_mask(tile_start + j, filled, first)
        for hp in range(HEADS // 2):
            items.append((slice(j * SPAN, (j + 1) * SPAN), hp, slice(hp * SPAN, (hp + 1) * SPAN), mask))
    return items


def weight_rows(place, index, rows):
    return pl.ds(pl.multiple_of((place ^ index) * rows, rows), rows)


def start_weight(meta_ref, layer, refs, target, sem):
    own, pieces = refs[0], refs[1:]

    @pl.when(meta_ref[6] == layer)
    def _():
        pltpu.make_async_copy(own, target, sem).start()

    @pl.when(meta_ref[6] != layer)
    def _():
        rows = target.shape[0] // 4
        for index, piece in enumerate(pieces):
            pltpu.make_async_copy(
                piece, target.at[weight_rows(meta_ref[7], index, rows)], sem
            ).start()


def wait_weight(refs, target, sem):
    pltpu.make_async_copy(refs[0], target, sem).wait()


def forward_attn_part(meta_ref, x_ref, gains_ref, outs, scratch, wqkv_ref, wout_ref, wait):
    (xh1_ref, r1_ref, qkv_ref, krow_ref, vrow_ref, lse_ref, att_ref, xh2_ref, r2_ref, ks_ref,
     vs_ref) = outs
    (attf_ref,) = scratch
    step = pl.program_id(0)
    tile_start = step * TILE_BLK

    @pl.when(step == 0)
    def _():
        ks_ref[...] = jnp.zeros_like(ks_ref)
        vs_ref[...] = jnp.zeros_like(vs_ref)

    x_t = x_ref[...].T.astype(F32)
    xhat, r1 = normalize(x_t)
    xh1_ref[...] = xhat.astype(BF)
    r1_ref[...] = r1
    normed = times_gain(xhat, gain_column(gains_ref, 0)).astype(BF)
    wait(0)
    q_t = (dot(wqkv_ref[:, :D], normed, 0, 0) * HEAD_DIM ** (-0.5)).astype(BF)
    k_t = dot(wqkv_ref[:, D:2 * D], normed, 0, 0).astype(BF)
    v_t = dot(wqkv_ref[:, 2 * D:], normed, 0, 0).astype(BF)
    qkv_ref[:D] = q_t
    qkv_ref[D:2 * D] = k_t
    qkv_ref[2 * D:] = v_t
    krow = k_t.T
    vrow = v_t.T
    krow_ref[...] = krow
    vrow_ref[...] = vrow
    members = member_mask(meta_ref, tile_start)
    fill = filled_column(meta_ref, D)
    block_rows = lax.broadcasted_iota(jnp.int32, (PAD_BLK, D), 0)
    fresh = (block_rows >= tile_start) & (block_rows < tile_start + TILE_BLK)
    key_sums = jnp.where(fresh, (dot(members, krow, 1, 0) / fill).astype(BF), ks_ref[...])
    value_sums = jnp.where(fresh, (dot(members, vrow, 1, 0) / fill).astype(BF), vs_ref[...])
    ks_ref[...] = key_sums
    vs_ref[...] = value_sums
    vs_t = value_sums.T
    for j in range(0, TILE_BLK, FWD_GROUP):
        items = attention_items(meta_ref, tile_start, range(j, j + FWD_GROUP))
        scores = [
            dot(
                jnp.concatenate([krow[cols, feats], key_sums[:, feats]], axis=0),
                pair_diag(q_t[feats, cols]), 1, 0,
            )
            for cols, _, feats, _ in items
        ]
        probs = []
        for (cols, hp, feats, mask), score in zip(items, scores):
            score = jnp.where(mask, score, NEG_FILL)
            top = jnp.max(score, axis=0, keepdims=True)
            prob = jnp.exp(score - top)
            total = jnp.sum(prob, axis=0, keepdims=True)
            logs = top + jnp.log(total)
            lse_ref[2 * hp:2 * hp + 1, cols] = logs[:, :SPAN]
            lse_ref[2 * hp + 1:2 * hp + 2, cols] = logs[:, SPAN:]
            probs.append((prob * (1.0 / total)).astype(BF))
        for (cols, _, feats, _), prob in zip(items, probs):
            values = jnp.concatenate([v_t[feats, cols], vs_t[feats]], axis=1)
            attf_ref[feats, cols] = diag_rows(dot(values, prob, 1, 0)).astype(BF)
    att = attf_ref[...]
    att_ref[...] = att
    wait(1)
    hidden = x_t + dot(wout_ref[...], att, 0, 0)
    xhat2, r2 = normalize(hidden)
    xh2_ref[...] = xhat2.astype(BF)
    r2_ref[...] = r2
    return hidden, times_gain(xhat2, gain_column(gains_ref, 1)).astype(BF)


def forward_mlp_part(hidden, second, outs, wup_ref, wdown_ref):
    out_ref, act_ref, gp_ref = outs
    total_out = hidden
    up = dot(wup_ref[:, :FWD_STEP], second, 0, 0)
    for f in range(FF // FWD_STEP):
        part = slice(f * FWD_STEP, (f + 1) * FWD_STEP)
        later = slice((f + 1) * FWD_STEP, (f + 2) * FWD_STEP)
        ahead = dot(wup_ref[:, later], second, 0, 0) if later.stop <= FF else None
        bell = jnp.exp(up * up * -0.5)
        phi = 0.5 + 0.5 * lax.erf(up * (0.5 ** 0.5))
        act = (up * phi).astype(BF)
        act_ref[part] = act
        gp_ref[part] = (phi + up * bell * 0.3989422804014327).astype(BF)
        total_out = total_out + dot(wdown_ref[part], act, 0, 0)
        up = ahead
    out_ref[...] = total_out.astype(BF).T


def weight_waits(meta_ref, layer, weights, targets, sems):
    begin = pl.program_id(0) == 0

    @pl.when(begin)
    def _():
        for i, (sources, target) in enumerate(zip(weights, targets)):
            start_weight(meta_ref, layer, sources, target, sems.at[i])

    def wait(i):
        @pl.when(begin)
        def _():
            wait_weight(weights[i], targets[i], sems.at[i])

    return wait


def fives(refs, count):
    return [refs[5 * i:5 * i + 5] for i in range(count)], refs[5 * count:]


def forward_kernel(meta_ref, x_ref, gains_ref, *refs, layer):
    weights, refs = fives(refs, 4)
    attn_outs, mlp_outs, scratch, targets, sems = (
        refs[:11], refs[11:14], refs[14:15], refs[15:19], refs[19]
    )
    wait = weight_waits(meta_ref, layer, weights, targets, sems)
    hidden, second = forward_attn_part(
        meta_ref, x_ref, gains_ref, attn_outs, scratch, targets[0], targets[1], wait
    )
    wait(2)
    wait(3)
    forward_mlp_part(hidden, second, mlp_outs, targets[2], targets[3])


def forward_attn_kernel(meta_ref, x_ref, gains_ref, *refs, layer):
    weights, refs = fives(refs, 2)
    attn_outs, (hid_ref, sec_ref), scratch, targets, sems = (
        refs[:11], refs[11:13], refs[13:14], refs[14:16], refs[16]
    )
    wait = weight_waits(meta_ref, layer, weights, targets, sems)
    hidden, second = forward_attn_part(
        meta_ref, x_ref, gains_ref, attn_outs, scratch, targets[0], targets[1], wait
    )
    hid_ref[...] = hidden
    sec_ref[...] = second


def forward_mlp_kernel(meta_ref, hid_ref, sec_ref, *refs, layer):
    weights, refs = fives(refs, 2)
    outs, targets, sems = refs[:3], refs[3:5], refs[5]
    wait = weight_waits(meta_ref, layer, weights, targets, sems)
    wait(0)
    wait(1)
    forward_mlp_part(hid_ref[...], sec_ref[...], outs, *targets)


def write_halves(meta_ref, accs, shards, send_ref, keep_ref, last=None):
    core = meta_ref[7] & 1
    total = send_ref.shape[0] // 8
    for target, side in ((send_ref, 1 - core), (keep_ref, core)):
        for s in range(8):
            start = s * total
            for acc, shard in zip(accs, shards):
                rows = pl.ds(pl.multiple_of(side * (8 * shard), 8 * shard) + s * shard, shard)
                target[pl.ds(start, shard)] = acc[rows].astype(BF)
                start += shard
            if last is not None:
                target[pl.ds(start, last.shape[0])] = last


MLP_SHARDS = (FF // 16, FF // 16, D // 16)
QKV_SHARDS = (3 * D // 16,)
GAIN_ROWS = 16


def norm_back(grad, gain, xhat, factor, gln_acc):
    prod = grad * xhat
    for j in range(TILE_BLK):
        gln_acc[...] += prod[:, j * SPAN:(j + 1) * SPAN]
    scaled = times_gain(grad, gain)
    mean = jnp.sum(scaled, axis=0, keepdims=True) * (1.0 / D)
    mean_x = jnp.sum(scaled * xhat, axis=0, keepdims=True) * (1.0 / D)
    return factor * (scaled - mean - xhat * mean_x)


def mlp_back_kernel(
    meta_ref, seed_ref, act_ref, gp_ref, xh2_ref, r2_ref, att_ref, gains_ref, *refs, layer, masked,
):
    weights, refs = fives(refs, 3)
    (send_ref, keep_ref, gln_ref, gh_ref, gatt_ref, gdown_acc, gup_acc, gout_acc, gln_acc,
     wdown_ref, wup_ref, wout_ref, sems) = refs
    step = pl.program_id(0)
    tile = N_TILE - 1 - step
    wait = weight_waits(meta_ref, layer, weights, (wdown_ref, wup_ref, wout_ref), sems)

    @pl.when(step == 0)
    def _():
        gdown_acc[...] = jnp.zeros_like(gdown_acc)
        gup_acc[...] = jnp.zeros_like(gup_acc)
        gout_acc[...] = jnp.zeros_like(gout_acc)
        gln_acc[...] = jnp.zeros_like(gln_acc)

    low = seed_ref[...].T
    if masked:
        parts = []
        cols = lax.broadcasted_iota(jnp.int32, (D, SPAN), 1)
        for j in range(TILE_BLK):
            filled, _ = block_facts(meta_ref, tile * TILE_BLK + j)
            part = low[:, j * SPAN:(j + 1) * SPAN]
            parts.append(jnp.where(cols < filled, part, jnp.zeros((), BF)))
        low = jnp.concatenate(parts, axis=1)
    gain = gain_column(gains_ref, 1)
    xhat = xh2_ref[...].astype(F32)
    second = times_gain(xhat, gain).astype(BF)
    wait(0)
    wait(1)
    e = None
    for f in range(FF // FF_STEP):
        part = slice(f * FF_STEP, (f + 1) * FF_STEP)
        gdown_acc[part] += dot(act_ref[part], low, 1, 1)
        ga = dot(wdown_ref[part], low, 1, 0)
        gui = (ga * gp_ref[part].astype(F32)).astype(BF)
        gup_acc[part] += dot(gui, second, 1, 1)
        term = dot(wup_ref[:, part], gui, 1, 0)
        e = term if e is None else e + term
    gh = low.astype(F32) + norm_back(e, gain, xhat, r2_ref[...], gln_acc)
    gh_ref[...] = gh
    ghb = gh.astype(BF)
    gout_acc[...] += dot(att_ref[...], ghb, 1, 1)
    wait(2)
    gatt_ref[...] = dot(wout_ref[...], ghb, 1, 0).astype(BF)

    @pl.when(step == N_TILE - 1)
    def _():
        write_halves(meta_ref, (gdown_acc, gup_acc, gout_acc), MLP_SHARDS, send_ref, keep_ref)
        gln_ref[...] = jnp.sum(gln_acc[...].T, axis=0, keepdims=True)


def attn_back_kernel(
    meta_ref, gh_ref, gatt_ref, xh1_ref, r1_ref, qkv_ref, krow_ref, vrow_ref, lse_ref, ks_ref,
    vs_ref, gains_ref, gln2_ref, *refs, layer,
):
    weights, refs = fives(refs, 1)
    (gin_ref, send_ref, keep_ref, gqkv_acc, gln_acc, gks_acc, gvs_acc, rows_ref, wqkv_ref,
     sems) = refs
    step = pl.program_id(0)
    tile_start = (N_TILE - 1 - step) * TILE_BLK
    wait = weight_waits(meta_ref, layer, weights, (wqkv_ref,), sems)

    @pl.when(step == 0)
    def _():
        gqkv_acc[...] = jnp.zeros_like(gqkv_acc)
        gln_acc[...] = jnp.zeros_like(gln_acc)
        gks_acc[...] = jnp.zeros_like(gks_acc)
        gvs_acc[...] = jnp.zeros_like(gvs_acc)

    q_t = qkv_ref[:D]
    gatt = gatt_ref[...]
    key_sums, value_sums = ks_ref[...], vs_ref[...]
    ks_t = key_sums.T
    for j in range(0, TILE_BLK, BACK_GROUP):
        items = attention_items(meta_ref, tile_start, range(j, j + BACK_GROUP))
        q_diags = [pair_diag(q_t[feats, cols]) for cols, _, feats, _ in items]
        g_diags = [pair_diag(gatt[feats, cols]) for cols, _, feats, _ in items]
        scores = [
            dot(jnp.concatenate([krow_ref[cols, feats], key_sums[:, feats]], axis=0), q, 1, 0)
            for (cols, _, feats, _), q in zip(items, q_diags)
        ]
        dps = [
            dot(jnp.concatenate([vrow_ref[cols, feats], value_sums[:, feats]], axis=0), g, 1, 0)
            for (cols, _, feats, _), g in zip(items, g_diags)
        ]
        grads, probs = [], []
        for (cols, hp, feats, mask), score, dp in zip(items, scores, dps):
            logs = jnp.concatenate(
                [lse_ref[2 * hp:2 * hp + 1, cols], lse_ref[2 * hp + 1:2 * hp + 2, cols]], axis=1
            )
            prob = jnp.exp(jnp.where(mask, score, NEG_FILL) - logs)
            weighted = prob * dp
            delta = jnp.sum(weighted, axis=0, keepdims=True)
            grads.append((weighted - prob * delta).astype(BF))
            probs.append(prob.astype(BF))
        for (cols, hp, feats, _), grad, prob, q, g in zip(items, grads, probs, q_diags, g_diags):
            key_feats = slice(D + hp * SPAN, D + (hp + 1) * SPAN)
            value_feats = slice(2 * D + hp * SPAN, 2 * D + (hp + 1) * SPAN)
            keys = jnp.concatenate([qkv_ref[key_feats, cols], ks_t[feats]], axis=1)
            rows_ref[feats, cols] = diag_rows(dot(keys, grad, 1, 0))
            key_grad = dot(q, grad, 1, 1)
            value_grad = dot(g, prob, 1, 1)
            rows_ref[key_feats, cols] = key_grad[:, :SPAN]
            rows_ref[value_feats, cols] = value_grad[:, :SPAN]
            gks_acc[feats] += key_grad[:, SPAN:]
            gvs_acc[feats] += value_grad[:, SPAN:]
    members = member_mask(meta_ref, tile_start)
    fill = filled_row(meta_ref)

    def spread_back(acc_ref):
        back = (acc_ref[...].astype(BF).astype(F32) / fill).astype(BF)
        return dot(back, members, 1, 0)

    grad_q = rows_ref[:D] * HEAD_DIM ** (-0.5)
    grad_k = rows_ref[D:2 * D] + spread_back(gks_acc)
    grad_v = rows_ref[2 * D:] + spread_back(gvs_acc)
    gain = gain_column(gains_ref, 0)
    xhat = xh1_ref[...].astype(F32)
    normed = times_gain(xhat, gain).astype(BF)
    wait(0)
    e = None
    for i, rows in enumerate((grad_q, grad_k, grad_v)):
        rows = rows.astype(BF)
        part = slice(i * D, (i + 1) * D)
        gqkv_acc[part] += dot(rows, normed, 1, 1)
        term = dot(wqkv_ref[:, part], rows, 1, 0)
        e = term if e is None else e + term
    gin = gh_ref[...] + norm_back(e, gain, xhat, r1_ref[...], gln_acc)
    gin_ref[...] = gin.astype(BF).T

    @pl.when(step == N_TILE - 1)
    def _():
        gln = jnp.sum(gln_acc[...].T, axis=0, keepdims=True)
        rest = jnp.zeros((GAIN_ROWS - 2, D), F32)
        last = jnp.concatenate([gln, gln2_ref[...], rest], axis=0).astype(BF)
        write_halves(meta_ref, (gqkv_acc,), QKV_SHARDS, send_ref, keep_ref, last)


ANY = pl.BlockSpec(memory_space=pl.ANY)
sds = jax.ShapeDtypeStruct


def whole(shape):
    return pl.BlockSpec(shape, lambda t, *_: (0,) * len(shape), pipeline_mode=pl.Buffered(1))


def rows_spec(width):
    return pl.BlockSpec((TILE, width), lambda t, *_: (t, 0))


def cols_spec(height):
    return pl.BlockSpec((height, TILE), lambda t, *_: (0, t))


def rev_rows(width):
    return pl.BlockSpec((TILE, width), lambda t, *_: (N_TILE - 1 - t, 0))


def rev_cols(height):
    return pl.BlockSpec((height, TILE), lambda t, *_: (0, N_TILE - 1 - t))


def call(kernel, grid, outs, in_specs, out_specs, scratch, flops, args):
    moved = sum(a.size * a.dtype.itemsize for a in args) + sum(
        o.size * o.dtype.itemsize for o in outs
    )
    return pl.pallas_call(
        kernel,
        out_shape=tuple(outs),
        grid_spec=pltpu.PrefetchScalarGridSpec(
            num_scalar_prefetch=1, grid=grid, in_specs=in_specs, out_specs=out_specs,
            scratch_shapes=scratch,
        ),
        cost_estimate=pl.CostEstimate(
            flops=int(flops), bytes_accessed=int(moved), transcendentals=0
        ),
        compiler_params=pltpu.CompilerParams(vmem_limit_bytes=VMEM_LIMIT),
    )(*args)


LINEAR = 2.0 * MB_TOK * D


def col(height, kind=BF):
    return sds((height, MB_TOK), kind)


def attn_outputs():
    shapes = [
        col(D), col(1, F32), col(3 * D), sds((MB_TOK, D), BF), sds((MB_TOK, D), BF),
        col(HEADS, F32), col(D), col(D), col(1, F32), sds((PAD_BLK, D), BF), sds((PAD_BLK, D), BF),
    ]
    specs = [
        cols_spec(D), cols_spec(1), cols_spec(3 * D), rows_spec(D), rows_spec(D), cols_spec(HEADS),
        cols_spec(D), cols_spec(D), cols_spec(1), whole((PAD_BLK, D)), whole((PAD_BLK, D)),
    ]
    return shapes, specs


MLP_OUTS = ([sds((MB_TOK, D), BF), col(FF), col(FF)], [(D, 0), (FF, 1), (FF, 1)])


def input_spec(layer):
    if layer == 0:
        return pl.BlockSpec((TILE, D), lambda t, m: (m[6] * N_TILE + t, 0))
    return rows_spec(D)


def weight_scratch(*weights):
    return [pltpu.VMEM(w[0].shape, BF) for w in weights] + [
        pltpu.SemaphoreType.DMA((len(weights),))
    ]


def flat(weights):
    return [ref for weight in weights for ref in weight]


def attn_scratch():
    return [pltpu.VMEM((D, TILE), BF)]


def forward(meta, x, gains, wqkv, wout, wup, wdown, layer):
    shapes, specs = attn_outputs()
    weights = (wqkv, wout, wup, wdown)
    out = call(
        functools.partial(forward_kernel, layer=layer), (N_TILE,),
        shapes + MLP_OUTS[0],
        [input_spec(layer), whole((2, D))] + [ANY] * 20,
        specs + [rows_spec(D), cols_spec(FF), cols_spec(FF)],
        attn_scratch() + weight_scratch(*weights),
        LINEAR * (4 * D + 2 * FF) * 1.5,
        (meta, x, gains, *flat(weights)),
    )
    return out[:11], out[11:]


def forward_attn(meta, x, gains, wqkv, wout, layer):
    shapes, specs = attn_outputs()
    weights = (wqkv, wout)
    out = call(
        functools.partial(forward_attn_kernel, layer=layer), (N_TILE,),
        shapes + [col(D, F32), col(D)],
        [input_spec(layer), whole((2, D))] + [ANY] * 10,
        specs + [cols_spec(D), cols_spec(D)],
        attn_scratch() + weight_scratch(*weights),
        LINEAR * 4 * D * 2,
        (meta, x, gains, *flat(weights)),
    )
    return out[:11], out[11], out[12]


def forward_mlp(meta, hidden, second, wup, wdown, layer):
    weights = (wup, wdown)
    return call(
        functools.partial(forward_mlp_kernel, layer=layer), (N_TILE,),
        MLP_OUTS[0],
        [cols_spec(D), cols_spec(D)] + [ANY] * 10,
        [rows_spec(D), cols_spec(FF), cols_spec(FF)],
        weight_scratch(*weights),
        LINEAR * 2 * FF * 1.5,
        (meta, hidden, second, *flat(weights)),
    )


def mlp_back(meta, seed, act, gp, xh2, r2, att, gains, wdown, wup, wout, layer):
    masked = layer == 1
    if masked:
        seed_spec = pl.BlockSpec((TILE, D), lambda t, m: (m[6] * N_TILE + N_TILE - 1 - t, 0))
    else:
        seed_spec = rev_rows(D)
    weights = (wdown, wup, wout)
    half = 8 * sum(MLP_SHARDS)
    return call(
        functools.partial(mlp_back_kernel, layer=layer, masked=masked), (N_TILE,),
        [sds((half, D), BF), sds((half, D), BF), sds((1, D), F32), col(D, F32), col(D)],
        [
            seed_spec, rev_cols(FF), rev_cols(FF), rev_cols(D), rev_cols(1), rev_cols(D),
            whole((2, D)),
        ] + [ANY] * 15,
        [whole((half, D)), whole((half, D)), whole((1, D)), rev_cols(D), rev_cols(D)],
        [
            pltpu.VMEM((FF, D), F32), pltpu.VMEM((FF, D), F32), pltpu.VMEM((D, D), F32),
            pltpu.VMEM((D, SPAN), F32),
        ] + weight_scratch(*weights),
        LINEAR * (4 * FF + 2 * D) * 1.5,
        (meta, seed, act, gp, xh2, r2, att, gains, *flat(weights)),
    )


def attn_back(meta, gh, gatt, xh1, r1, qkv, krow, vrow, lse, ks, vs, gains, gln2, wqkv, layer):
    half = 8 * (sum(QKV_SHARDS) + GAIN_ROWS)
    return call(
        functools.partial(attn_back_kernel, layer=layer), (N_TILE,),
        [sds((MB_TOK, D), BF), sds((half, D), BF), sds((half, D), BF)],
        [
            rev_cols(D), rev_cols(D), rev_cols(D), rev_cols(1), rev_cols(3 * D), rev_rows(D),
            rev_rows(D), rev_cols(HEADS), whole((PAD_BLK, D)), whole((PAD_BLK, D)), whole((2, D)),
            whole((1, D)),
        ] + [ANY] * 5,
        [rev_rows(D), whole((half, D)), whole((half, D))],
        [
            pltpu.VMEM((3 * D, D), F32), pltpu.VMEM((D, SPAN), F32), pltpu.VMEM((D, PAD_BLK), F32),
            pltpu.VMEM((D, PAD_BLK), F32), pltpu.VMEM((3 * D, TILE), F32),
        ] + weight_scratch(wqkv),
        LINEAR * 12 * D * 1.5,
        (meta, gh, gatt, xh1, r1, qkv, krow, vrow, lse, ks, vs, gains, gln2, *wqkv),
    )


def finish_kernel(meta_ref, *refs, widths, flips):
    pieces, refs = refs[:4], refs[4:]
    outs, held, sem = refs[:len(widths)], refs[-2], refs[-1]
    rows = held.shape[0] // 4
    for index, piece in enumerate(pieces):
        place = meta_ref[7] ^ index
        spot = (place & 1) * 2 + (place >> 1)
        pltpu.make_async_copy(
            piece, held.at[pl.ds(pl.multiple_of(spot * rows, rows), rows)], sem
        ).start()
    for index, piece in enumerate(pieces):
        pltpu.make_async_copy(piece, held.at[pl.ds(index * rows, rows)], sem).wait()
    total = sum(widths)
    for i, (width, flip) in enumerate(zip(widths, flips)):
        for s in range(16):
            start = s * total + sum(widths[:i])
            part = held[pl.ds(start, width)].astype(F32)
            if flip:
                outs[i][:, pl.ds(s * width, width)] = part.T
            else:
                outs[i][pl.ds(s * width, width)] = part


def finish(meta, pieces, widths, flips):
    rows = pieces[0].shape[0]
    outs = [
        sds((D, 16 * w), F32) if flip else sds((16 * w, D), F32) for w, flip in zip(widths, flips)
    ]
    return call(
        functools.partial(finish_kernel, widths=widths, flips=flips), (1,),
        outs, [ANY] * 4, [whole(o.shape) for o in outs],
        [pltpu.VMEM((4 * rows, D), BF), pltpu.SemaphoreType.DMA],
        0.0, (meta, *pieces),
    )


def swap_xor(value, mask):
    size = lax.axis_size("dp")
    return lax.ppermute(value, "dp", [(i, i ^ mask) for i in range(size)])


def swap_section(value):
    return lax.ppermute(value, "section", [(0, 1), (1, 0)])


def to_section(value, target):
    return lax.ppermute(value, "section", [(1 - target, target)])


def added(*values):
    total = values[0].astype(F32)
    for value in values[1:]:
        total = total + value.astype(F32)
    return total.astype(BF)


def halves(value, bit):
    half = value.shape[0] // 2
    mine = (lax.axis_index("dp") >> bit) & 1
    return (
        lax.dynamic_slice_in_dim(value, mine * half, half, 0),
        lax.dynamic_slice_in_dim(value, (1 - mine) * half, half, 0),
    )


def half_sum(pair, bit):
    return added(pair[0], swap_xor(pair[1], 1 << bit))


def quarters(value, bit):
    rows = value.shape[0] // 4
    mine = (lax.axis_index("dp") >> bit) & 3
    return tuple(lax.dynamic_slice_in_dim(value, (mine ^ k) * rows, rows, 0) for k in range(4))


def swap_quarters(parts, bit):
    return [swap_xor(parts[k], k << bit) for k in (1, 2, 3)]


def quarter_sum(parts, bit):
    return added(parts[0], *swap_quarters(parts, bit))


def tie(*values):
    return lax.optimization_barrier(values)


def rest_bits():
    return range(4, lax.axis_size("dp").bit_length() - 1)


def reduce_core(halves):
    return added(halves[1], swap_xor(halves[0], 1))


def reduce_rest(value):
    for bit in rest_bits():
        value = half_sum(halves(value, bit), bit)
    return value


def gather_bit(value, bit):
    mine = (lax.axis_index("dp") >> bit) & 1
    other = swap_xor(value, 1 << bit)
    return jnp.where(
        mine == 0,
        jnp.concatenate([value, other], axis=0),
        jnp.concatenate([other, value], axis=0),
    )


def gather_quad(value, bit):
    mine = (lax.axis_index("dp") >> bit) & 3
    got = [value] + [swap_xor(value, k << bit) for k in (1, 2, 3)]
    parts = []
    for p in range(4):
        which = mine ^ p
        part = got[3]
        for k in (2, 1, 0):
            part = jnp.where(which == k, got[k], part)
        parts.append(part)
    return jnp.concatenate(parts, axis=0)


def gather_pieces(value):
    for bit in reversed(rest_bits()):
        value = gather_bit(value, bit)
    value = gather_quad(value, 2)
    across = swap_xor(value, 2)
    return value, swap_xor(value, 1), across, swap_xor(across, 1)


def fetch_pieces(value):
    piece = swap_section(value)
    across = swap_xor(piece, 2)
    return piece, swap_xor(piece, 1), across, swap_xor(across, 1)


def sum_rest(value):
    for bit in rest_bits():
        value = added(value, swap_xor(value, 1 << bit))
    return value


def per_device(
    tokens, cotangent, span_counts, tail_lens, ln1_gain, w_qkv, w_out, ln2_gain, w_up, w_down
):
    section = lax.axis_index("section")
    first = section == 0
    place = lax.axis_index("dp") & 3
    meta = jnp.concatenate([
        lax.dynamic_index_in_dim(span_counts, section, 0, keepdims=False),
        lax.dynamic_index_in_dim(tail_lens, section, 0, keepdims=False),
        section.astype(jnp.int32)[None], place.astype(jnp.int32)[None],
    ])
    own = (w_qkv[0], w_out[0], w_up[0], w_down[0])

    def quarter(weight):
        rows = weight.shape[0] // 4
        return lax.dynamic_slice_in_dim(weight, place * rows, rows, 0)

    own_gains = jnp.concatenate([ln1_gain, ln2_gain], axis=0)
    other_gains = swap_section(own_gains)
    wqkv = (own[0],) + fetch_pieces(quarter(own[0]))
    wout = (own[1],) + fetch_pieces(quarter(own[1]))
    up = swap_section(quarter(own[2]))
    down = swap_section(quarter(own[3]))
    up_x, up_c = swap_xor(up, 2), swap_xor(up, 1)
    gains = [jnp.where(first, own_gains, other_gains), jnp.where(first, other_gains, own_gains)]

    keep0, hidden, second = forward_attn(meta, tokens, gains[0], wqkv, wout, 0)
    keep0, hidden, second, up_x, up_c, down = tie(keep0, hidden, second, up_x, up_c, down)
    down_x = swap_xor(down, 2)
    wup = (own[2], up, up_c, up_x, swap_xor(up_x, 1))
    wdown = (own[3], down, swap_xor(down, 1), down_x, swap_xor(down_x, 1))
    act_out0, act0, gp0 = forward_mlp(meta, hidden, second, wup, wdown, 0)
    half = MB_TOK // 2
    out0_a = to_section(act_out0[:half], 0)
    forward1 = forward(meta, act_out0, gains[1], wqkv, wout, wup, wdown, 1)
    (keep1, (act_out1, act1, gp1)), out0_a, act_out0 = tie(forward1, out0_a, act_out0)
    out0_b = to_section(act_out0[half:], 0)
    out1_a = to_section(act_out1[:half], 1)

    def back_mlp(layer, seed, keep, act, gp):
        att, xh2, r2 = keep[6:9]
        return mlp_back(meta, seed, act, gp, xh2, r2, att, gains[layer], wdown, wup, wout, layer)

    def back_attn(layer, gh, gatt, keep, gln2):
        xh1, r1, qkv, krow, vrow, lse = keep[:6]
        return attn_back(
            meta, gh, gatt, xh1, r1, qkv, krow, vrow, lse, keep[9], keep[10], gains[layer], gln2,
            wqkv, layer,
        )

    back = back_mlp(1, cotangent, keep1, act1, gp1)
    (send, kept, gln2, gh, gatt), out0_b, out1_a, act_out1 = tie(back, out0_b, out1_a, act_out1)
    mlp1 = halves(reduce_core((send, kept)), 1)
    gh, mlp1 = tie(gh, mlp1)
    mlp1_x = swap_xor(mlp1[1], 2)
    out1_b = to_section(act_out1[half:], 1)
    back = back_attn(1, gh, gatt, keep1, gln2)
    (ig1, send, kept), mlp1_x, out1_b = tie(back, mlp1_x, out1_b)
    qkv1 = halves(reduce_core((send, kept)), 1)
    mlp1 = quarters(added(mlp1[0], mlp1_x), 2)
    ig1, mlp1, qkv1 = tie(ig1, mlp1, qkv1)
    mlp1_z = swap_quarters(mlp1, 2)
    qkv1_x = swap_xor(qkv1[1], 2)
    ig1_a = to_section(ig1[:half], 1)
    back = back_mlp(0, ig1, keep0, act0, gp0)
    (send, kept, gln2, gh, gatt), mlp1_z, qkv1_x, ig1_a, ig1 = tie(
        back, mlp1_z, qkv1_x, ig1_a, ig1
    )
    mlp0 = halves(reduce_core((send, kept)), 1)
    mlp1 = added(mlp1[0], *mlp1_z)
    qkv1 = quarters(added(qkv1[0], qkv1_x), 2)
    gh, mlp0, mlp1, qkv1 = tie(gh, mlp0, mlp1, qkv1)
    mlp0_x = swap_xor(mlp0[1], 2)
    qkv1_z = swap_quarters(qkv1, 2)
    ig1_b = to_section(ig1[half:], 1)
    back = back_attn(0, gh, gatt, keep0, gln2)
    (ig0, send, kept), mlp0_x, qkv1_z, ig1_b = tie(back, mlp0_x, qkv1_z, ig1_b)
    ig0_in = to_section(ig0, 0)
    qkv0 = halves(reduce_core((send, kept)), 1)
    mlp0 = quarter_sum(quarters(added(mlp0[0], mlp0_x), 2), 2)
    qkv1 = added(qkv1[0], *qkv1_z)
    qkv0 = quarter_sum(quarters(half_sum(qkv0, 1), 2), 2)

    def own_sum(grad0, grad1):
        got = swap_section(jnp.where(first, grad1, grad0))
        return added(jnp.where(first, grad0, grad1), got)

    mlp = gather_pieces(own_sum(reduce_rest(mlp0), reduce_rest(mlp1)))
    cut = sum(QKV_SHARDS)
    qkv = jnp.concatenate([reduce_rest(qkv0[:cut]), sum_rest(qkv0[cut:])], axis=0)
    qkv = own_sum(qkv, jnp.concatenate([reduce_rest(qkv1[:cut]), sum_rest(qkv1[cut:])], axis=0))
    lns = qkv[-GAIN_ROWS:][:2].astype(F32)
    qkv = gather_pieces(qkv[:-GAIN_ROWS])
    grad_down, grad_up, grad_out = finish(meta, mlp, MLP_SHARDS, (False, True, False))
    (grad_qkv,) = finish(meta, qkv, QKV_SHARDS, (True,))
    out0_in = jnp.concatenate([out0_a, out0_b], axis=0)
    out1_in = jnp.concatenate([out1_a, out1_b], axis=0)
    ig1_in = jnp.concatenate([ig1_a, ig1_b], axis=0)
    activations = jnp.concatenate(
        [jnp.where(first, act_out0, out1_in), jnp.where(first, out0_in, act_out1)], axis=0
    )
    input_grads = jnp.concatenate(
        [jnp.where(first, ig0, ig1_in), jnp.where(first, ig0_in, ig1)], axis=0
    )
    return (
        activations[None],
        input_grads[None],
        lns[:1],
        grad_qkv[None],
        grad_out[None],
        lns[1:],
        grad_up[None],
        grad_down[None],
    )


def solution(mesh):
    return jax.shard_map(
        per_device,
        mesh=mesh,
        in_specs=(
            P("dp", None),
            P("dp", None),
            P("dp", None),
            P("dp", None),
            P("section", None),
            P("section", None, None),
            P("section", None, None),
            P("section", None),
            P("section", None, None),
            P("section", None, None),
        ),
        out_specs=(
            P("section", "dp", None),
            P("section", "dp", None),
            P("section", None),
            P("section", None, None),
            P("section", None, None),
            P("section", None),
            P("section", None, None),
            P("section", None, None),
        ),
        check_vma=False,
    )
```

time: 528 us -> 393 us (0.74)
  waiting for transfers between devices: 228 us -> 111 us
  other arithmetic: 50.1 us -> 22.4 us
    ppermute x40 -> x44, waiting for transfers between devices: 184 us -> 91.7 us  [swap_xor(): return lax.ppermute(value, 'dp', [(i, i ^ mask) for i in range(size)])]
    ppermute x7, waiting for transfers between devices: 43.7 us -> 19.1 us  [swap_section(): return lax.ppermute(value, 'section', [(0, 1), (1, 0)])]
    select_n x27 -> x7, other arithmetic: 28.8 us -> 4.2 us  [the longest x1 1.64 us: per_device(): jnp.where(first, act_out0, out1_in)]
    ppermute x4 -> x7, starting transfers between devices: 8.88 us -> 17 us  [to_section(): return lax.ppermute(value, 'section', [(1 - target, target)])]
    broadcast_in_dim x3 -> x0, other arithmetic: 6.15 us -> none  [the longest x1 4.6 us: per_device(): cat[:FF].astype(F32)[None]]
    pallas_call x6 -> x9, Pallas kernels: 162 us -> 165 us  [call(): pl.pallas_call(kernel, out_shape=tuple(outs), grid_spec=pltpu.PrefetchSca...]
    convert_element_type x14 -> x12, other arithmetic: 8.78 us -> 11 us  [the longest x11 11 us: added(): return total.astype(BF)]
    ppermute x40 -> x44, starting transfers between devices: 43.1 us -> 43 us  [swap_xor(): return lax.ppermute(value, 'dp', [(i, i ^ mask) for i in range(size)])]
  transfers between devices with their start and end apart: 51 -> 58, of which waited for: 26 -> 21; matrix products, arithmetic and copies ran while one was open for 9% -> 7% of each run, Pallas kernels for 16% -> 37%
where the time goes in v2:
time: 393 us; the launch traced here: 386 us
  Pallas kernels  165 us (42%)
  waiting for transfers between devices  111 us (28%)
  starting transfers between devices  67.3 us (17%)
  other arithmetic  22.4 us (6%)
  local copies, waits for them, and re-layouts  18.5 us (5%)
    pallas_call x9, Pallas kernels, call(): pl.pallas_call(kernel, out_shape=tuple(outs), grid_spec=pltpu.PrefetchSca...  165 us
    ppermute x44, waiting for transfers between devices, swap_xor(): return lax.ppermute(value, 'dp', [(i, i ^ mask) for i in range(size)])  91.7 us
    ppermute x44, starting transfers between devices, swap_xor(): return lax.ppermute(value, 'dp', [(i, i ^ mask) for i in range(size)])  43 us
    ppermute x7, waiting for transfers between devices, swap_section(): return lax.ppermute(value, 'section', [(0, 1), (1, 0)])  19.1 us
    ppermute x7, starting transfers between devices, to_section(): return lax.ppermute(value, 'section', [(1 - target, target)])  17 us
    convert_element_type x11, other arithmetic, added(): return total.astype(BF)  11 us
  transfers between devices with their start and end apart: 58, of which 21 were waited for; matrix products, arithmetic and copies ran while one was open for 7% of the time, Pallas kernels for 37%

profile of v2, /device:TPU:0, one launch (start us, length us, event | category | flops | bytes accessed | tf_op | source)
XLA Modules:
  0.0 385.9 jit_solution(9427565502954726795)
XLA Ops:
  1.7 3.0 collective-permute-start.1
  5.8 8.9 %collective-permute-done.1.refs_1_ = bf16[128,1536]{1,0:T(8,128)(2,1)S(1)} collective-permute-done((bf16[128,1536]{1,0:T(8,128)(2,1)S(1)}, bf16[128,1536]{1,0:T(8,128)(2,1)S(1)}, u32[]{:S(2)}, u32[]{:S(2)}) %collective-permute-start.1) | collective-permute-done | bytes 393248 | tf_op jit(solution)/shard_map/ppermute | solution.py:677
  21.9 3.7 collective-permute-done.3.refs_3_
  32.8 16.4 %shard_map.161 = (bf16[512,1536]{1,0:T(8,128)(2,1)}, f32[1,1536]{1,0:T(1,128)}, bf16[1536,1536]{1,0:T(8,128)(2,1)}, bf16[1536,512]{1,0:T(8,128)(2,1)}, bf16[1536...) custom-call(s32[8]{0:T(128)} %pad_add_fusion.meta_ref, ...), custom_call_target="tpu_custom_call" | custom-call | flops 6442450944 | bytes 24739872 | tf_op jit(solution)/shard_map/pallas_call | solution.py:491
  51.7 12.1 %collective-permute-done.15.refs_8_.refs_18_.refs_3_ = bf16[512,512]{1,0:T(8,128)(2,1)S(1)} collective-permute-done((bf16[512,512]{1,0:T(8,128)(2,1)S(1)}, bf16[512,512]{1,0:T(8,128)(2,1)S(1)}, u32[]{:S(2)}, u32[]{:S(2)}) %collective-permute-start.15) | collective-permute-done | bytes 524320 | tf_op jit(solution)/shard_map/ppermute | solution.py:673
  66.5 16.2 %shard_map.162 = (bf16[1536,512]{1,0:T(8,128)(2,1)}, bf16[2048,1536]{1,0:T(8,128)(2,1)}, bf16[2048,1536]{1,0:T(8,128)(2,1)}) custom-call(s32[8]{0:T(128)} %pad_add_fusion.meta_ref, f32[512,1536]{1,0:T(8,128)} %get-tuple-element.152.hid_ref, bf16[512,1536]{1,0:T(8,128)(2,1)} %get-tuple-element.153.sec_ref, bf16[512,2048]{1,0:T(8,128)(2,1)} %bitcast.27, ...), custom_call_target="tpu_custom_call" | custom-call | flops 9663676416 | bytes 27263008 | tf_op jit(solution)/shard_map/pallas_call | solution.py:491
  85.4 25.4 %shard_map.163 = (bf16[512,1536]{1,0:T(8,128)(2,1)}, f32[1,1536]{1,0:T(1,128)}, bf16[1536,1536]{1,0:T(8,128)(2,1)}, bf16[1536,512]{1,0:T(8,128)(2,1)}, bf16[1536...) custom-call(s32[8]{0:T(128)} %pad_add_fusion.meta_ref, ...), custom_call_target="tpu_custom_call" | custom-call | flops 14495514624 | bytes 40992800 | tf_op jit(solution)/shard_map/pallas_call | solution.py:491
  113.4 5.8 %collective-permute-start.19 = (bf16[768,512]{1,0:T(8,128)(2,1)}, bf16[768,512]{1,0:T(8,128)(2,1)}, u32[]{:S(2)}, u32[]{:S(2)}) collective-permute-start(bf16[768,512]{1,0:T(8,128)(2,1)} %slice.40), channel_id=1, source_target_pairs={{0,16},{1,17},{2,18},{3,19},{4,20},{5,21},{6,22},{7,23},{8,24},{9,... | collective-permute-start | bytes 2359304 | tf_op jit(solution)/shard_map/ppermute | solution.py:681
  119.2 28.0 %shard_map.164 = (bf16[2304,512]{1,0:T(8,128)(2,1)}, bf16[2304,512]{1,0:T(8,128)(2,1)}, f32[1,512]{1,0:T(1,128)}, f32[512,1536]{1,0:T(8,128)}, bf16[512,1536]{1,0:T(8,128)(2,1)}) custom-call(s32[8]{0:T(128)} %pad_add_fusion.meta_ref, bf16[3072,512]{1,0:T(8,128)(2,1)} %seed_ref.1, bf16[2048,1536]{1,0:T(8,128)(2,1)} %get-tuple-element.173.act_ref, ...), custom_call_target="tpu_custom_call" | custom-call | flops 21743271936 | bytes 37761056 | tf_op jit(solution)/shard_map/pallas_call | solution.py:491
  153.1 3.0 add_convert_fusion.1
  158.1 19.2 %shard_map.165 = (bf16[1536,512]{1,0:T(8,128)(2,1)}, bf16[896,512]{1,0:T(8,128)(2,1)}, bf16[896,512]{1,0:T(8,128)(2,1)}) custom-call(s32[8]{0:T(128)} %pad_add_fusion.meta_ref, f32[512,1536]{1,0:T(8,128)} %get-tuple-element.188.gh_ref, bf16[512,1536]{1,0:T(8,128)(2,1)} %get-tuple-element.189.gatt_ref, bf16[512,1536]{1,0:T(8,128)(2,1)} %get-tuple-element.190.xh1_ref, ...), custom_call_target="tpu_custom_call" | custom-call | flops 14495514624 | bytes 20803616 | tf_op jit(solution)/shard_map/pallas_call | solution.py:491
  177.3 7.1 %collective-permute-done.21 = bf16[1152,512]{1,0:T(8,128)(2,1)} collective-permute-done((bf16[1152,512]{1,0:T(8,128)(2,1)S(1)}, bf16[1152,512]{1,0:T(8,128)(2,1)}, u32[]{:S(2)}, u32[]{:S(2)}) %collective-permute-start.21) | collective-permute-done | bytes 1179680 | tf_op jit(solution)/shard_map/ppermute | solution.py:673
  189.9 2.7 collective-permute-start.28
  196.1 2.6 collective-permute-start.25
  198.8 28.2 %shard_map.166 = (bf16[2304,512]{1,0:T(8,128)(2,1)}, bf16[2304,512]{1,0:T(8,128)(2,1)}, f32[1,512]{1,0:T(1,128)}, f32[512,1536]{1,0:T(8,128)}, bf16[512,1536]{1,0:T(8,128)(2,1)}) custom-call(s32[8]{0:T(128)} %pad_add_fusion.meta_ref, bf16[1536,512]{1,0:T(8,128)(2,1)} %get-tuple-element.254.seed_ref, bf16[2048,1536]{1,0:T(8,128)(2,1)} %get-tuple-element.213.act_ref, ...), custom_call_target="tpu_custom_call" | custom-call | flops 21743271936 | bytes 36188192 | tf_op jit(solution)/shard_map/pallas_call | solution.py:491
  236.7 3.5 collective-permute-start.32
  240.3 19.2 %shard_map.167 = (bf16[1536,512]{1,0:T(8,128)(2,1)}, bf16[896,512]{1,0:T(8,128)(2,1)}, bf16[896,512]{1,0:T(8,128)(2,1)}) custom-call(s32[8]{0:T(128)} %pad_add_fusion.meta_ref, f32[512,1536]{1,0:T(8,128)} %get-tuple-element.236.gh_ref, bf16[512,1536]{1,0:T(8,128)(2,1)} %get-tuple-element.237.gatt_ref, bf16[512,1536]{1,0:T(8,128)(2,1)} %get-tuple-element.238.xh1_ref, ...), custom_call_target="tpu_custom_call" | custom-call | flops 14495514624 | bytes 20803616 | tf_op jit(solution)/shard_map/pallas_call | solution.py:491
  259.6 4.2 %collective-permute-done.30 = bf16[1152,512]{1,0:T(8,128)(2,1)} collective-permute-done((bf16[1152,512]{1,0:T(8,128)(2,1)S(1)}, bf16[1152,512]{1,0:T(8,128)(2,1)}, u32[]{:S(2)}, u32[]{:S(2)}) %collective-permute-start.30) | collective-permute-done | bytes 1179680 | tf_op jit(solution)/shard_map/ppermute | solution.py:673
  266.5 3.5 collective-permute-start.49
  271.2 8.3 %collective-permute-done.48 = bf16[288,512]{1,0:T(8,128)(2,1)S(1)} collective-permute-done((bf16[288,512]{1,0:T(8,128)(2,1)S(1)}, bf16[288,512]{1,0:T(8,128)(2,1)S(1)}, u32[]{:S(2)}, u32[]{:S(2)}) %collective-permute-start.48) | collective-permute-done | bytes 294944 | tf_op jit(solution)/shard_map/ppermute | solution.py:673
  279.4 11.1 %collective-permute-done.49 = bf16[288,512]{1,0:T(8,128)(2,1)S(1)} collective-permute-done((bf16[288,512]{1,0:T(8,128)(2,1)S(1)}, bf16[288,512]{1,0:T(8,128)(2,1)S(1)}, u32[]{:S(2)}, u32[]{:S(2)}) %collective-permute-start.49) | collective-permute-done | bytes 294944 | tf_op jit(solution)/shard_map/ppermute | solution.py:673
  292.5 5.1 %collective-permute-done.51 = bf16[288,512]{1,0:T(8,128)(2,1)S(1)} collective-permute-done((bf16[288,512]{1,0:T(8,128)(2,1)S(1)}, bf16[288,512]{1,0:T(8,128)(2,1)S(1)}, u32[]{:S(2)}, u32[]{:S(2)}) %collective-permute-start.51) | collective-permute-done | bytes 294944 | tf_op jit(solution)/shard_map/ppermute | solution.py:677
  297.7 6.1 %collective-permute-start.52 = (bf16[288,512]{1,0:T(8,128)(2,1)S(1)}, bf16[288,512]{1,0:T(8,128)(2,1)S(1)}, u32[]{:S(2)}, u32[]{:S(2)}) collective-permute-start(bf16[288,512]{1,0:T(8,128)(2,1)S(1)} %add_convert_fusion.8), channel_id=1, source_target_pairs={{0,4},{1,5},{2,6},{3,7},{4,0},{5,1},{6,2},{7,3},{8,12},{9,13},{10,... | collective-permute-start | bytes 884744 | tf_op jit(solution)/shard_map/ppermute | solution.py:673
  310.3 2.5 collective-permute-done.52
  312.8 13.9 %collective-permute-done.53 = bf16[288,512]{1,0:T(8,128)(2,1)S(1)} collective-permute-done((bf16[288,512]{1,0:T(8,128)(2,1)S(1)}, bf16[288,512]{1,0:T(8,128)(2,1)S(1)}, u32[]{:S(2)}, u32[]{:S(2)}) %collective-permute-start.53) | collective-permute-done | bytes 294944 | tf_op jit(solution)/shard_map/ppermute | solution.py:673
  327.1 3.8 collective-permute-start.38
  333.8 6.2 %collective-permute-done.39 = bf16[112,512]{1,0:T(8,128)(2,1)S(1)} collective-permute-done((bf16[112,512]{1,0:T(8,128)(2,1)S(1)}, bf16[112,512]{1,0:T(8,128)(2,1)S(1)}, u32[]{:S(2)}, u32[]{:S(2)}) %collective-permute-start.39) | collective-permute-done | bytes 114720 | tf_op jit(solution)/shard_map/ppermute | solution.py:673
  343.5 2.6 collective-permute-done.41
  350.9 7.4 %collective-permute-done.56.refs_2_ = bf16[1152,512]{1,0:T(8,128)(2,1)S(1)} collective-permute-done((bf16[1152,512]{1,0:T(8,128)(2,1)S(1)}, bf16[1152,512]{1,0:T(8,128)(2,1)S(1)}, u32[]{:S(2)}, u32[]{:S(2)}) %collective-permute-start.56) | collective-permute-done | bytes 1179680 | tf_op jit(solution)/shard_map/ppermute | solution.py:673
  360.8 9.1 %collective-permute-done.46.refs_2_ = bf16[384,512]{1,0:T(8,128)(2,1)S(1)} collective-permute-done((bf16[384,512]{1,0:T(8,128)(2,1)S(1)}, bf16[384,512]{1,0:T(8,128)(2,1)S(1)}, u32[]{:S(2)}, u32[]{:S(2)}) %collective-permute-start.46) | collective-permute-done | bytes 393248 | tf_op jit(solution)/shard_map/ppermute | solution.py:673
  372.4 4.8 %shard_map.168 = f32[512,1536]{1,0:T(8,128)} custom-call(s32[8]{0:T(128)} %pad_add_fusion.meta_ref, bf16[384,512]{1,0:T(8,128)(2,1)} %copy-done.9, bf16[384,512]{1,0:T(8,128)(2,1)} %copy-done.23, bf16[384,512]{1,0:T(8,128)(2,1)} %copy-done.22, bf16[384,512]{1,0:T(8,128)(2,1)} %copy-done.24), custom_call_target="tpu_custom_call" | custom-call | bytes 4718624 | tf_op jit(solution)/shard_map/pallas_call | solution.py:491
  378.3 7.4 %shard_map.169 = (f32[2048,512]{1,0:T(8,128)}, f32[512,2048]{1,0:T(8,128)}, f32[512,512]{1,0:T(8,128)}) custom-call(s32[8]{0:T(128)} %pad_add_fusion.meta_ref, bf16[1152,512]{1,0:T(8,128)(2,1)} %copy-done.5, bf16[1152,512]{1,0:T(8,128)(2,1)} %collective-permute-done.55.refs_1_, bf16[1152,512]{1,0:T(8,128)(2,1)} %copy-done.10, bf16[1152,512]{1,0:T(8,128)(2,1)} %copy-done.11), custom_call_target="tpu_custom_call" | custom-call | bytes 14155808 | tf_op jit(solution)/shard_map/pallas_call | solution.py:491
  (251 shorter events, 83.0 us)
Async XLA Ops:
  5.7 16.1 %collective-permute-start.5 = (bf16[128,512]{1,0:T(8,128)(2,1)S(1)}, bf16[128,512]{1,0:T(8,128)(2,1)S(1)}, u32[]{:S(2)}, u32[]{:S(2)}) collective-permute-start(bf16[128,512]{1,0:T(8,128)(2,1)S(1)} %dynamic-slice_bitcast_fusion.3), channel_id=1, source_target_pairs={{0,16},{16,0},{1,17},{17,1},{2,18},{18,2},{3,19},{19,3},{4,20},{20... | collective-permute-start | bytes 393224 | tf_op jit(solution)/shard_map/ppermute | solution.py:677
  27.8 21.5 %collective-permute-start.12 = (bf16[512,512]{1,0:T(8,128)(2,1)S(1)}, bf16[512,512]{1,0:T(8,128)(2,1)S(1)}, u32[]{:S(2)}, u32[]{:S(2)}) collective-permute-start(bf16[512,512]{1,0:T(8,128)(2,1)S(1)} %dynamic-slice_bitcast_fusion), channel_id=1, source_target_pairs={{0,16},{16,0},{1,17},{17,1},{2,18},{18,2},{3,19},{19,3},{4,20},{20... | collective-permute-start | bytes 1572872 | tf_op jit(solution)/shard_map/ppermute | solution.py:677
  31.7 17.6 %collective-permute-start.10 = (bf16[128,2048]{1,0:T(8,128)(2,1)S(1)}, bf16[128,2048]{1,0:T(8,128)(2,1)S(1)}, u32[]{:S(2)}, u32[]{:S(2)}) collective-permute-start(bf16[128,2048]{1,0:T(8,128)(2,1)S(1)} %collective-permute-done.9.refs_1_.refs_11_.refs_6_), channel_id=1, source_target_pairs={{0,2},{1,3},{2,0},{3,1},{4,6},{5,7},{6,4},{7,5},{8,10},{9,11},{10,... | collective-permute-start | bytes 1572872 | tf_op jit(solution)/shard_map/ppermute | solution.py:673
  31.8 17.4 %collective-permute-start.11 = (bf16[128,2048]{1,0:T(8,128)(2,1)S(1)}, bf16[128,2048]{1,0:T(8,128)(2,1)S(1)}, u32[]{:S(2)}, u32[]{:S(2)}) collective-permute-start(bf16[128,2048]{1,0:T(8,128)(2,1)S(1)} %collective-permute-done.9.refs_1_.refs_11_.refs_6_), channel_id=1, source_target_pairs={{0,1},{1,0},{2,3},{3,2},{4,5},{5,4},{6,7},{7,6},{8,9},{9,8},{10,11... | collective-permute-start | bytes 1572872 | tf_op jit(solution)/shard_map/ppermute | solution.py:673
  49.3 14.5 %collective-permute-start.15 = (bf16[512,512]{1,0:T(8,128)(2,1)S(1)}, bf16[512,512]{1,0:T(8,128)(2,1)S(1)}, u32[]{:S(2)}, u32[]{:S(2)}) collective-permute-start(bf16[512,512]{1,0:T(8,128)(2,1)S(1)} %collective-permute-done.12.refs_6_.refs_16_.refs_1_), channel_id=1, source_target_pairs={{0,2},{1,3},{2,0},{3,1},{4,6},{5,7},{6,4},{7,5},{8,10},{9,11},{10,... | collective-permute-start | bytes 1572872 | tf_op jit(solution)/shard_map/ppermute | solution.py:673
  83.9 26.9 %collective-permute-start.17 = (bf16[768,512]{1,0:T(8,128)(2,1)S(1)}, bf16[768,512]{1,0:T(8,128)(2,1)S(1)}, u32[]{:S(2)}, u32[]{:S(2)}) collective-permute-start(bf16[768,512]{1,0:T(8,128)(2,1)S(1)} %slice.38), channel_id=1, source_target_pairs={{16,0},{17,1},{18,2},{19,3},{20,4},{21,5},{22,6},{23,7},{24,8},{25... | collective-permute-start | bytes 2359304 | tf_op jit(solution)/shard_map/ppermute | solution.py:681
  110.9 36.3 %collective-permute-start.18 = (bf16[768,512]{1,0:T(8,128)(2,1)S(1)}, bf16[768,512]{1,0:T(8,128)(2,1)S(1)}, u32[]{:S(2)}, u32[]{:S(2)}) collective-permute-start(bf16[768,512]{1,0:T(8,128)(2,1)S(1)} %slice.39), channel_id=1, source_target_pairs={{16,0},{17,1},{18,2},{19,3},{20,4},{21,5},{22,6},{23,7},{24,8},{25... | collective-permute-start | bytes 2359304 | tf_op jit(solution)/shard_map/ppermute | solution.py:681
  113.4 34.7 %collective-permute-start.19 = (bf16[768,512]{1,0:T(8,128)(2,1)}, bf16[768,512]{1,0:T(8,128)(2,1)}, u32[]{:S(2)}, u32[]{:S(2)}) collective-permute-start(bf16[768,512]{1,0:T(8,128)(2,1)} %slice.40), channel_id=1, source_target_pairs={{0,16},{1,17},{2,18},{3,19},{4,20},{5,21},{6,22},{7,23},{8,24},{9,... | collective-permute-start | bytes 2359304 | tf_op jit(solution)/shard_map/ppermute | solution.py:681
  149.1 28.2 %collective-permute-start.22 = (bf16[768,512]{1,0:T(8,128)(2,1)}, bf16[768,512]{1,0:T(8,128)(2,1)S(1)}, u32[]{:S(2)}, u32[]{:S(2)}) collective-permute-start(bf16[768,512]{1,0:T(8,128)(2,1)} %slice.41), channel_id=1, source_target_pairs={{0,16},{1,17},{2,18},{3,19},{4,20},{5,21},{6,22},{7,23},{8,24},{9,... | collective-permute-start | bytes 2359304 | tf_op jit(solution)/shard_map/ppermute | solution.py:681
  156.3 28.2 %collective-permute-start.21 = (bf16[1152,512]{1,0:T(8,128)(2,1)S(1)}, bf16[1152,512]{1,0:T(8,128)(2,1)}, u32[]{:S(2)}, u32[]{:S(2)}) collective-permute-start(bf16[1152,512]{1,0:T(8,128)(2,1)S(1)} %get-tuple-element.202), channel_id=1, source_target_pairs={{0,2},{1,3},{2,0},{3,1},{4,6},{5,7},{6,4},{7,5},{8,10},{9,11},{10,... | collective-permute-start | bytes 3538952 | tf_op jit(solution)/shard_map/ppermute | solution.py:673
  189.9 37.2 %collective-permute-start.28 = (bf16[768,512]{1,0:T(8,128)(2,1)S(1)}, bf16[768,512]{1,0:T(8,128)(2,1)}, u32[]{:S(2)}, u32[]{:S(2)}) collective-permute-start(bf16[768,512]{1,0:T(8,128)(2,1)S(1)} %slice.42), channel_id=1, source_target_pairs={{0,16},{1,17},{2,18},{3,19},{4,20},{5,21},{6,22},{7,23},{8,24},{9,... | collective-permute-start | bytes 2359304 | tf_op jit(solution)/shard_map/ppermute | solution.py:681
  192.6 34.5 %collective-permute-start.27 = (bf16[448,512]{1,0:T(8,128)(2,1)S(1)}, bf16[448,512]{1,0:T(8,128)(2,1)S(1)}, u32[]{:S(2)}, u32[]{:S(2)}) collective-permute-start(bf16[448,512]{1,0:T(8,128)(2,1)S(1)} %get-tuple-element.226), channel_id=1, source_target_pairs={{0,2},{1,3},{2,0},{3,1},{4,6},{5,7},{6,4},{7,5},{8,10},{9,11},{10,... | collective-permute-start | bytes 1376264 | tf_op jit(solution)/shard_map/ppermute | solution.py:673
  194.4 32.6 %collective-permute-start.24 = (bf16[288,512]{1,0:T(8,128)(2,1)}, bf16[288,512]{1,0:T(8,128)(2,1)S(1)}, u32[]{:S(2)}, u32[]{:S(2)}) collective-permute-start(bf16[288,512]{1,0:T(8,128)(2,1)} %get-tuple-element.223), channel_id=1, source_target_pairs={{0,4},{1,5},{2,6},{3,7},{4,0},{5,1},{6,2},{7,3},{8,12},{9,13},{10,... | collective-permute-start | bytes 884744 | tf_op jit(solution)/shard_map/ppermute | solution.py:673
  196.1 31.0 %collective-permute-start.25 = (bf16[288,512]{1,0:T(8,128)(2,1)}, bf16[288,512]{1,0:T(8,128)(2,1)S(1)}, u32[]{:S(2)}, u32[]{:S(2)}) collective-permute-start(bf16[288,512]{1,0:T(8,128)(2,1)} %get-tuple-element.224), channel_id=1, source_target_pairs={{0,8},{1,9},{2,10},{3,11},{4,12},{5,13},{6,14},{7,15},{8,0},{9,1},... | collective-permute-start | bytes 884744 | tf_op jit(solution)/shard_map/ppermute | solution.py:673
  198.7 28.4 %collective-permute-start.26 = (bf16[288,512]{1,0:T(8,128)(2,1)}, bf16[288,512]{1,0:T(8,128)(2,1)S(1)}, u32[]{:S(2)}, u32[]{:S(2)}) collective-permute-start(bf16[288,512]{1,0:T(8,128)(2,1)} %get-tuple-element.225), channel_id=1, source_target_pairs={{0,12},{1,13},{2,14},{3,15},{4,8},{5,9},{6,10},{7,11},{8,4},{9,5},... | collective-permute-start | bytes 884744 | tf_op jit(solution)/shard_map/ppermute | solution.py:673
  229.2 30.4 %collective-permute-start.34 = (bf16[768,512]{1,0:T(8,128)(2,1)}, bf16[768,512]{1,0:T(8,128)(2,1)}, u32[]{:S(2)}, u32[]{:S(2)}) collective-permute-start(bf16[768,512]{1,0:T(8,128)(2,1)} %slice.43), channel_id=1, source_target_pairs={{0,16},{1,17},{2,18},{3,19},{4,20},{5,21},{6,22},{7,23},{8,24},{9,... | collective-permute-start | bytes 2359304 | tf_op jit(solution)/shard_map/ppermute | solution.py:681
  235.5 28.3 %collective-permute-start.30 = (bf16[1152,512]{1,0:T(8,128)(2,1)S(1)}, bf16[1152,512]{1,0:T(8,128)(2,1)}, u32[]{:S(2)}, u32[]{:S(2)}) collective-permute-start(bf16[1152,512]{1,0:T(8,128)(2,1)S(1)} %get-tuple-element.250), channel_id=1, source_target_pairs={{0,2},{1,3},{2,0},{3,1},{4,6},{5,7},{6,4},{7,5},{8,10},{9,11},{10,... | collective-permute-start | bytes 3538952 | tf_op jit(solution)/shard_map/ppermute | solution.py:673
  235.9 23.6 %collective-permute-start.31 = (bf16[112,512]{1,0:T(8,128)(2,1)}, bf16[112,512]{1,0:T(8,128)(2,1)S(1)}, u32[]{:S(2)}, u32[]{:S(2)}) collective-permute-start(bf16[112,512]{1,0:T(8,128)(2,1)} %get-tuple-element.251), channel_id=1, source_target_pairs={{0,4},{1,5},{2,6},{3,7},{4,0},{5,1},{6,2},{7,3},{8,12},{9,13},{10,... | collective-permute-start | bytes 344072 | tf_op jit(solution)/shard_map/ppermute | solution.py:673
  236.7 22.9 %collective-permute-start.32 = (bf16[112,512]{1,0:T(8,128)(2,1)}, bf16[112,512]{1,0:T(8,128)(2,1)S(1)}, u32[]{:S(2)}, u32[]{:S(2)}) collective-permute-start(bf16[112,512]{1,0:T(8,128)(2,1)} %get-tuple-element.252), channel_id=1, source_target_pairs={{0,8},{1,9},{2,10},{3,11},{4,12},{5,13},{6,14},{7,15},{8,0},{9,1},... | collective-permute-start | bytes 344072 | tf_op jit(solution)/shard_map/ppermute | solution.py:673
  240.2 19.4 %collective-permute-start.33 = (bf16[112,512]{1,0:T(8,128)(2,1)}, bf16[112,512]{1,0:T(8,128)(2,1)}, u32[]{:S(2)}, u32[]{:S(2)}) collective-permute-start(bf16[112,512]{1,0:T(8,128)(2,1)} %get-tuple-element.253), channel_id=1, source_target_pairs={{0,12},{1,13},{2,14},{3,15},{4,8},{5,9},{6,10},{7,11},{8,4},{9,5},... | collective-permute-start | bytes 344072 | tf_op jit(solution)/shard_map/ppermute | solution.py:673
  265.7 13.8 %collective-permute-start.48 = (bf16[288,512]{1,0:T(8,128)(2,1)S(1)}, bf16[288,512]{1,0:T(8,128)(2,1)S(1)}, u32[]{:S(2)}, u32[]{:S(2)}) collective-permute-start(bf16[288,512]{1,0:T(8,128)(2,1)S(1)} %get-tuple-element.283), channel_id=1, source_target_pairs={{0,4},{1,5},{2,6},{3,7},{4,0},{5,1},{6,2},{7,3},{8,12},{9,13},{10,... | collective-permute-start | bytes 884744 | tf_op jit(solution)/shard_map/ppermute | solution.py:673
  266.5 24.0 %collective-permute-start.49 = (bf16[288,512]{1,0:T(8,128)(2,1)S(1)}, bf16[288,512]{1,0:T(8,128)(2,1)S(1)}, u32[]{:S(2)}, u32[]{:S(2)}) collective-permute-start(bf16[288,512]{1,0:T(8,128)(2,1)S(1)} %get-tuple-element.285), channel_id=1, source_target_pairs={{0,8},{1,9},{2,10},{3,11},{4,12},{5,13},{6,14},{7,15},{8,0},{9,1},... | collective-permute-start | bytes 884744 | tf_op jit(solution)/shard_map/ppermute | solution.py:673
  270.0 20.6 %collective-permute-start.50 = (bf16[288,512]{1,0:T(8,128)(2,1)S(1)}, bf16[288,512]{1,0:T(8,128)(2,1)S(1)}, u32[]{:S(2)}, u32[]{:S(2)}) collective-permute-start(bf16[288,512]{1,0:T(8,128)(2,1)S(1)} %get-tuple-element.284), channel_id=1, source_target_pairs={{0,12},{1,13},{2,14},{3,15},{4,8},{5,9},{6,10},{7,11},{8,4},{9,5},... | collective-permute-start | bytes 884744 | tf_op jit(solution)/shard_map/ppermute | solution.py:673
  271.2 35.0 %collective-permute-start.36 = (bf16[896,512]{1,0:T(8,128)(2,1)S(1)}, bf16[896,512]{1,0:T(8,128)(2,1)S(1)}, u32[]{:S(2)}, u32[]{:S(2)}) collective-permute-start(bf16[896,512]{1,0:T(8,128)(2,1)S(1)} %copy-done.39), channel_id=1, source_target_pairs={{0,1},{1,0},{2,3},{3,2},{4,5},{5,4},{6,7},{7,6},{8,9},{9,8},{10,11... | collective-permute-start | bytes 2752520 | tf_op jit(solution)/shard_map/ppermute | solution.py:673
  297.7 15.1 %collective-permute-start.52 = (bf16[288,512]{1,0:T(8,128)(2,1)S(1)}, bf16[288,512]{1,0:T(8,128)(2,1)S(1)}, u32[]{:S(2)}, u32[]{:S(2)}) collective-permute-start(bf16[288,512]{1,0:T(8,128)(2,1)S(1)} %add_convert_fusion.8), channel_id=1, source_target_pairs={{0,4},{1,5},{2,6},{3,7},{4,0},{5,1},{6,2},{7,3},{8,12},{9,13},{10,... | collective-permute-start | bytes 884744 | tf_op jit(solution)/shard_map/ppermute | solution.py:673
  303.7 23.0 %collective-permute-start.53 = (bf16[288,512]{1,0:T(8,128)(2,1)S(1)}, bf16[288,512]{1,0:T(8,128)(2,1)S(1)}, u32[]{:S(2)}, u32[]{:S(2)}) collective-permute-start(bf16[288,512]{1,0:T(8,128)(2,1)S(1)} %add_convert_fusion.8), channel_id=1, source_target_pairs={{0,8},{1,9},{2,10},{3,11},{4,12},{5,13},{6,14},{7,15},{8,0},{9,1},... | collective-permute-start | bytes 884744 | tf_op jit(solution)/shard_map/ppermute | solution.py:673
  304.8 21.9 %collective-permute-start.54 = (bf16[288,512]{1,0:T(8,128)(2,1)S(1)}, bf16[288,512]{1,0:T(8,128)(2,1)S(1)}, u32[]{:S(2)}, u32[]{:S(2)}) collective-permute-start(bf16[288,512]{1,0:T(8,128)(2,1)S(1)} %add_convert_fusion.8), channel_id=1, source_target_pairs={{0,12},{1,13},{2,14},{3,15},{4,8},{5,9},{6,10},{7,11},{8,4},{9,5},... | collective-permute-start | bytes 884744 | tf_op jit(solution)/shard_map/ppermute | solution.py:673
  306.5 20.3 %collective-permute-start.37 = (bf16[448,512]{1,0:T(8,128)(2,1)S(1)}, bf16[448,512]{1,0:T(8,128)(2,1)S(1)}, u32[]{:S(2)}, u32[]{:S(2)}) collective-permute-start(bf16[448,512]{1,0:T(8,128)(2,1)S(1)} %constant_dynamic-slice_fusion.6), channel_id=1, source_target_pairs={{0,2},{1,3},{2,0},{3,1},{4,6},{5,7},{6,4},{7,5},{8,10},{9,11},{10,... | collective-permute-start | bytes 1376264 | tf_op jit(solution)/shard_map/ppermute | solution.py:673
  308.8 40.5 %collective-permute-start.35 = (bf16[1536,512]{1,0:T(8,128)(2,1)S(1)}, bf16[1536,512]{1,0:T(8,128)(2,1)S(1)}, u32[]{:S(2)}, u32[]{:S(2)}) collective-permute-start(bf16[1536,512]{1,0:T(8,128)(2,1)S(1)} %copy-done.8), channel_id=1, source_target_pairs={{16,0},{17,1},{18,2},{19,3},{20,4},{21,5},{22,6},{23,7},{24,8},{25... | collective-permute-start | bytes 4718600 | tf_op jit(solution)/shard_map/ppermute | solution.py:681
  333.4 24.8 %collective-permute-start.56 = (bf16[1152,512]{1,0:T(8,128)(2,1)S(1)}, bf16[1152,512]{1,0:T(8,128)(2,1)S(1)}, u32[]{:S(2)}, u32[]{:S(2)}) collective-permute-start(bf16[1152,512]{1,0:T(8,128)(2,1)S(1)} %pad_maximum_fusion.refs_0_), channel_id=1, source_target_pairs={{0,2},{1,3},{2,0},{3,1},{4,6},{5,7},{6,4},{7,5},{8,10},{9,11},{10,... | collective-permute-start | bytes 3538952 | tf_op jit(solution)/shard_map/ppermute | solution.py:673
  343.5 33.8 %collective-permute-start.55 = (bf16[1152,512]{1,0:T(8,128)(2,1)S(1)}, bf16[1152,512]{1,0:T(8,128)(2,1)}, u32[]{:S(2)}, u32[]{:S(2)}) collective-permute-start(bf16[1152,512]{1,0:T(8,128)(2,1)S(1)} %pad_maximum_fusion.refs_0_), channel_id=1, source_target_pairs={{0,1},{1,0},{2,3},{3,2},{4,5},{5,4},{6,7},{7,6},{8,9},{9,8},{10,11... | collective-permute-start | bytes 3538952 | tf_op jit(solution)/shard_map/ppermute | solution.py:673
  358.2 19.0 %collective-permute-start.57 = (bf16[1152,512]{1,0:T(8,128)(2,1)S(1)}, bf16[1152,512]{1,0:T(8,128)(2,1)S(1)}, u32[]{:S(2)}, u32[]{:S(2)}) collective-permute-start(bf16[1152,512]{1,0:T(8,128)(2,1)S(1)} %collective-permute-done.56.refs_2_), channel_id=1, source_target_pairs={{0,1},{1,0},{2,3},{3,2},{4,5},{5,4},{6,7},{7,6},{8,9},{9,8},{10,11... | collective-permute-start | bytes 3538952 | tf_op jit(solution)/shard_map/ppermute | solution.py:673
  (81 other events, 666.3 us)

commit v3 on v2

--- a/solution.py
+++ b/solution.py
@@ -124,38 +124,51 @@
     return items
 
 
-def weight_rows(place, index, rows):
-    return pl.ds(pl.multiple_of((place ^ index) * rows, rows), rows)
-
-
-def start_weight(meta_ref, layer, refs, target, sem):
-    own, pieces = refs[0], refs[1:]
-
+class Weight:
+    def __init__(self, own, *groups):
+        self.own = own
+        self.groups = [(tuple(p), lane, at, width or own.shape[1]) for p, lane, at, width in groups]
+
+    def flat(self):
+        return (self.own,) + sum((group[0] for group in self.groups), ())
+
+    def bind(self, refs):
+        own, refs, groups = refs[0], refs[1:], []
+        for pieces, *rest in self.groups:
+            groups.append((refs[:len(pieces)], *rest))
+            refs = refs[len(pieces):]
+        return Weight(own, *groups), refs
+
+
+def start_weight(meta_ref, layer, weight, target, sem):
     @pl.when(meta_ref[6] == layer)
     def _():
-        pltpu.make_async_copy(own, target, sem).start()
+        pltpu.make_async_copy(weight.own, target, sem).start()
 
     @pl.when(meta_ref[6] != layer)
     def _():
-        rows = target.shape[0] // 4
-        for index, piece in enumerate(pieces):
-            pltpu.make_async_copy(
-                piece, target.at[weight_rows(meta_ref[7], index, rows)], sem
-            ).start()
-
-
-def wait_weight(refs, target, sem):
-    pltpu.make_async_copy(refs[0], target, sem).wait()
-
-
-def forward_attn_part(meta_ref, x_ref, gains_ref, outs, scratch, wqkv_ref, wout_ref, wait):
+        for pieces, lane, at, width in weight.groups:
+            count = len(pieces)
+            rows = target.shape[0] // count
+            for index, piece in enumerate(pieces):
+                spot = (meta_ref[7] & (count - 1)) ^ index
+                pltpu.make_async_copy(
+                    piece.at[:, pl.ds(lane, width)],
+                    target.at[pl.ds(pl.multiple_of(spot * rows, rows), rows), pl.ds(at, width)], sem,
+                ).start()
+
+
+def wait_weight(weight, target, sem):
+    pltpu.make_async_copy(weight.own, target, sem).wait()
+
+
+def forward_attn_part(meta_ref, tile, x_ref, gains_ref, outs, scratch, wqkv_ref, wout_ref, wait):
     (xh1_ref, r1_ref, qkv_ref, krow_ref, vrow_ref, lse_ref, att_ref, xh2_ref, r2_ref, ks_ref,
      vs_ref) = outs
     (attf_ref,) = scratch
-    step = pl.program_id(0)
-    tile_start = step * TILE_BLK
-
-    @pl.when(step == 0)
+    tile_start = tile * TILE_BLK
+
+    @pl.when(tile == 0)
     def _():
         ks_ref[...] = jnp.zeros_like(ks_ref)
         vs_ref[...] = jnp.zeros_like(vs_ref)
@@ -240,8 +253,8 @@
 
     @pl.when(begin)
     def _():
-        for i, (sources, target) in enumerate(zip(weights, targets)):
-            start_weight(meta_ref, layer, sources, target, sems.at[i])
+        for i, (weight, target) in enumerate(zip(weights, targets)):
+            start_weight(meta_ref, layer, weight, target, sems.at[i])
 
     def wait(i):
         @pl.when(begin)
@@ -251,39 +264,29 @@
     return wait
 
 
-def fives(refs, count):
-    return [refs[5 * i:5 * i + 5] for i in range(count)], refs[5 * count:]
-
-
-def forward_kernel(meta_ref, x_ref, gains_ref, *refs, layer):
-    weights, refs = fives(refs, 4)
-    attn_outs, mlp_outs, scratch, targets, sems = (
-        refs[:11], refs[11:14], refs[14:15], refs[15:19], refs[19]
+def bound(weights, refs):
+    out = []
+    for weight in weights:
+        weight, refs = weight.bind(refs)
+        out.append(weight)
+    return out, refs
+
+
+def forward_attn_kernel(meta_ref, x_ref, gains_ref, *refs, layer, weights):
+    weights, refs = bound(weights, refs)
+    attn_outs, (hid_ref, sec_ref), scratch, targets, sems = (
+        refs[:11], refs[11:13], refs[13:14], refs[14:16], refs[16]
     )
     wait = weight_waits(meta_ref, layer, weights, targets, sems)
     hidden, second = forward_attn_part(
-        meta_ref, x_ref, gains_ref, attn_outs, scratch, targets[0], targets[1], wait
-    )
-    wait(2)
-    wait(3)
-    forward_mlp_part(hidden, second, mlp_outs, targets[2], targets[3])
-
-
-def forward_attn_kernel(meta_ref, x_ref, gains_ref, *refs, layer):
-    weights, refs = fives(refs, 2)
-    attn_outs, (hid_ref, sec_ref), scratch, targets, sems = (
-        refs[:11], refs[11:13], refs[13:14], refs[14:16], refs[16]
-    )
-    wait = weight_waits(meta_ref, layer, weights, targets, sems)
-    hidden, second = forward_attn_part(
-        meta_ref, x_ref, gains_ref, attn_outs, scratch, targets[0], targets[1], wait
+        meta_ref, pl.program_id(0), x_ref, gains_ref, attn_outs, scratch, targets[0], targets[1], wait
     )
     hid_ref[...] = hidden
     sec_ref[...] = second
 
 
-def forward_mlp_kernel(meta_ref, hid_ref, sec_ref, *refs, layer):
-    weights, refs = fives(refs, 2)
+def forward_mlp_kernel(meta_ref, hid_ref, sec_ref, *refs, layer, weights):
+    weights, refs = bound(weights, refs)
     outs, targets, sems = refs[:3], refs[3:5], refs[5]
     wait = weight_waits(meta_ref, layer, weights, targets, sems)
     wait(0)
@@ -291,23 +294,37 @@
     forward_mlp_part(hid_ref[...], sec_ref[...], outs, *targets)
 
 
-def write_halves(meta_ref, accs, shards, send_ref, keep_ref, last=None):
+def write_halves(meta_ref, parts, send_ref, keep_ref, start=0, z_first=False):
     core = meta_ref[7] & 1
-    total = send_ref.shape[0] // 8
+    total = sum(rows for _, _, rows in parts)
     for target, side in ((send_ref, 1 - core), (keep_ref, core)):
         for s in range(8):
-            start = s * total
-            for acc, shard in zip(accs, shards):
-                rows = pl.ds(pl.multiple_of(side * (8 * shard), 8 * shard) + s * shard, shard)
-                target[pl.ds(start, shard)] = acc[rows].astype(BF)
-                start += shard
-            if last is not None:
-                target[pl.ds(start, last.shape[0])] = last
-
-
-MLP_SHARDS = (FF // 16, FF // 16, D // 16)
-QKV_SHARDS = (3 * D // 16,)
-GAIN_ROWS = 16
+            spot = start + ((s % 4) * 2 + s // 4 if z_first else s) * total
+            for acc, base, rows in parts:
+                if acc.shape[0] == rows:
+                    value = acc[...]
+                else:
+                    first = base + pl.multiple_of(side * (8 * rows), 8 * rows) + s * rows
+                    value = acc[pl.ds(first, rows)]
+                target[pl.ds(spot, rows)] = value.astype(BF)
+                spot += rows
+
+
+def write_shards(parts, target):
+    for place in range(16):
+        s = (place & 1) * 8 + ((place >> 1) & 1) * 4 + (place >> 2)
+        spot = 0
+        for acc, base, rows in parts:
+            value = acc[...] if acc.shape[0] == rows else acc[pl.ds(base + s * rows, rows)]
+            target[place, pl.ds(spot, rows)] = value.astype(BF)
+            spot += rows
+
+
+DOWN_ROWS, OUT_ROWS, QKV_ROWS, GAIN_ROWS = FF // 16, D // 16, 3 * D // 16, 16
+UP_A = FF // 4
+UP_B = FF - UP_A
+PART_A, PART_B = DOWN_ROWS + UP_A // 16 + OUT_ROWS, UP_B // 16
+PART_C = QKV_ROWS + GAIN_ROWS
 
 
 def norm_back(grad, gain, xhat, factor, gln_acc):
@@ -320,32 +337,25 @@
     return factor * (scaled - mean - xhat * mean_x)
 
 
-def mlp_back_kernel(
-    meta_ref, seed_ref, act_ref, gp_ref, xh2_ref, r2_ref, att_ref, gains_ref, *refs, layer, masked,
-):
-    weights, refs = fives(refs, 3)
-    (send_ref, keep_ref, gln_ref, gh_ref, gatt_ref, gdown_acc, gup_acc, gout_acc, gln_acc,
-     wdown_ref, wup_ref, wout_ref, sems) = refs
-    step = pl.program_id(0)
-    tile = N_TILE - 1 - step
-    wait = weight_waits(meta_ref, layer, weights, (wdown_ref, wup_ref, wout_ref), sems)
-
-    @pl.when(step == 0)
-    def _():
-        gdown_acc[...] = jnp.zeros_like(gdown_acc)
-        gup_acc[...] = jnp.zeros_like(gup_acc)
-        gout_acc[...] = jnp.zeros_like(gout_acc)
-        gln_acc[...] = jnp.zeros_like(gln_acc)
-
-    low = seed_ref[...].T
-    if masked:
-        parts = []
-        cols = lax.broadcasted_iota(jnp.int32, (D, SPAN), 1)
-        for j in range(TILE_BLK):
-            filled, _ = block_facts(meta_ref, tile * TILE_BLK + j)
-            part = low[:, j * SPAN:(j + 1) * SPAN]
-            parts.append(jnp.where(cols < filled, part, jnp.zeros((), BF)))
-        low = jnp.concatenate(parts, axis=1)
+def masked_low(meta_ref, tile, low):
+    parts = []
+    cols = lax.broadcasted_iota(jnp.int32, (D, SPAN), 1)
+    for j in range(TILE_BLK):
+        filled, _ = block_facts(meta_ref, tile * TILE_BLK + j)
+        part = low[:, j * SPAN:(j + 1) * SPAN]
+        parts.append(jnp.where(cols < filled, part, jnp.zeros((), BF)))
+    return jnp.concatenate(parts, axis=1)
+
+
+def zero_all(refs):
+    for ref in refs:
+        ref[...] = jnp.zeros_like(ref)
+
+
+def mlp_back_part(low, data, gains_ref, weights, accs, wait, gh_ref, gatt_ref):
+    act_ref, gp_ref, xh2_ref, r2_ref, att_ref = data
+    wdown_ref, wup_ref, wout_ref = weights
+    gdown_acc, gup_acc, gout_acc, gln_acc = accs
     gain = gain_column(gains_ref, 1)
     xhat = xh2_ref[...].astype(F32)
     second = times_gain(xhat, gain).astype(BF)
@@ -367,30 +377,44 @@
     wait(2)
     gatt_ref[...] = dot(wout_ref[...], ghb, 1, 0).astype(BF)
 
+
+def mlp_parts(gdown_acc, gup_acc, gout_acc):
+    part_a = ((gdown_acc, 0, DOWN_ROWS), (gup_acc, UP_B, UP_A // 16), (gout_acc, 0, OUT_ROWS))
+    return part_a, ((gup_acc, 0, UP_B // 16),)
+
+
+def mlp_back_kernel(
+    meta_ref, seed_ref, act_ref, gp_ref, xh2_ref, r2_ref, att_ref, gains_ref, *refs, layer, weights,
+):
+    weights, refs = bound(weights, refs)
+    (send_ref, keep_ref, gln_ref, gh_ref, gatt_ref, gdown_acc, gup_acc, gout_acc, gln_acc,
+     wdown_ref, wup_ref, wout_ref, sems) = refs
+    step = pl.program_id(0)
+    targets = (wdown_ref, wup_ref, wout_ref)
+    accs = (gdown_acc, gup_acc, gout_acc, gln_acc)
+    wait = weight_waits(meta_ref, layer, weights, targets, sems)
+
+    @pl.when(step == 0)
+    def _():
+        zero_all(accs)
+
+    mlp_back_part(
+        seed_ref[...].T, (act_ref, gp_ref, xh2_ref, r2_ref, att_ref), gains_ref, targets, accs, wait,
+        gh_ref, gatt_ref,
+    )
+
     @pl.when(step == N_TILE - 1)
     def _():
-        write_halves(meta_ref, (gdown_acc, gup_acc, gout_acc), MLP_SHARDS, send_ref, keep_ref)
+        part_a, part_b = mlp_parts(*accs[:3])
+        write_halves(meta_ref, part_a, send_ref, keep_ref)
+        write_halves(meta_ref, part_b, send_ref, keep_ref, 8 * PART_A, True)
         gln_ref[...] = jnp.sum(gln_acc[...].T, axis=0, keepdims=True)
 
 
-def attn_back_kernel(
-    meta_ref, gh_ref, gatt_ref, xh1_ref, r1_ref, qkv_ref, krow_ref, vrow_ref, lse_ref, ks_ref,
-    vs_ref, gains_ref, gln2_ref, *refs, layer,
-):
-    weights, refs = fives(refs, 1)
-    (gin_ref, send_ref, keep_ref, gqkv_acc, gln_acc, gks_acc, gvs_acc, rows_ref, wqkv_ref,
-     sems) = refs
-    step = pl.program_id(0)
-    tile_start = (N_TILE - 1 - step) * TILE_BLK
-    wait = weight_waits(meta_ref, layer, weights, (wqkv_ref,), sems)
-
-    @pl.when(step == 0)
-    def _():
-        gqkv_acc[...] = jnp.zeros_like(gqkv_acc)
-        gln_acc[...] = jnp.zeros_like(gln_acc)
-        gks_acc[...] = jnp.zeros_like(gks_acc)
-        gvs_acc[...] = jnp.zeros_like(gvs_acc)
-
+def attn_back_part(meta_ref, tile, gh_ref, gatt_ref, data, gains_ref, wqkv_ref, accs, rows_ref, wait):
+    xh1_ref, r1_ref, qkv_ref, krow_ref, vrow_ref, lse_ref, ks_ref, vs_ref = data
+    gqkv_acc, gln_acc, gks_acc, gvs_acc = accs
+    tile_start = tile * TILE_BLK
     q_t = qkv_ref[:D]
     gatt = gatt_ref[...]
     key_sums, value_sums = ks_ref[...], vs_ref[...]
@@ -449,15 +473,109 @@
         gqkv_acc[part] += dot(rows, normed, 1, 1)
         term = dot(wqkv_ref[:, part], rows, 1, 0)
         e = term if e is None else e + term
-    gin = gh_ref[...] + norm_back(e, gain, xhat, r1_ref[...], gln_acc)
-    gin_ref[...] = gin.astype(BF).T
+    return (gh_ref[...] + norm_back(e, gain, xhat, r1_ref[...], gln_acc)).astype(BF).T
+
+
+def gain_rows(gln_acc, gln2):
+    gln = jnp.sum(gln_acc[...].T, axis=0, keepdims=True)
+    rest = jnp.zeros((GAIN_ROWS - 2, D), F32)
+    return jnp.concatenate([gln, gln2, rest], axis=0).astype(BF)
+
+
+def attn_back_kernel(
+    meta_ref, gh_ref, gatt_ref, xh1_ref, r1_ref, qkv_ref, krow_ref, vrow_ref, lse_ref, ks_ref,
+    vs_ref, gains_ref, gln2_ref, *refs, layer, weights,
+):
+    weights, refs = bound(weights, refs)
+    (gin_ref, send_ref, keep_ref, gqkv_acc, gln_acc, gks_acc, gvs_acc, rows_ref, wqkv_ref,
+     sems) = refs
+    step = pl.program_id(0)
+    wait = weight_waits(meta_ref, layer, weights, (wqkv_ref,), sems)
+    accs = (gqkv_acc, gln_acc, gks_acc, gvs_acc)
+
+    @pl.when(step == 0)
+    def _():
+        zero_all(accs)
+
+    data = (xh1_ref, r1_ref, qkv_ref, krow_ref, vrow_ref, lse_ref, ks_ref, vs_ref)
+    gin_ref[...] = attn_back_part(
+        meta_ref, N_TILE - 1 - step, gh_ref, gatt_ref, data, gains_ref, wqkv_ref, accs, rows_ref, wait
+    )
 
     @pl.when(step == N_TILE - 1)
     def _():
-        gln = jnp.sum(gln_acc[...].T, axis=0, keepdims=True)
-        rest = jnp.zeros((GAIN_ROWS - 2, D), F32)
-        last = jnp.concatenate([gln, gln2_ref[...], rest], axis=0).astype(BF)
-        write_halves(meta_ref, (gqkv_acc,), QKV_SHARDS, send_ref, keep_ref, last)
+        parts = ((gqkv_acc, 0, QKV_ROWS), (gain_rows(gln_acc, gln2_ref[...]), 0, GAIN_ROWS))
+        write_halves(meta_ref, parts, send_ref, keep_ref)
+
+
+def layer_kernel(meta_ref, x_ref, cot_ref, gains_ref, *refs, layer, weights):
+    weights, refs = bound(weights, refs)
+    out_ref, gin_ref, sums_ref, *refs = refs
+    keep, refs = refs[:13], refs[13:]
+    (xh1, r1, qkv, krow, vrow, lse, att_ref, xh2_ref, r2_ref, ks_ref, vs_ref, gh, gatt) = keep
+    act_ref, gp_ref, attf_ref, rows_ref, *refs = refs
+    mlp_accs, attn_accs, refs = refs[:4], refs[4:8], refs[8:]
+    held_mlp, held_qkv, *refs = refs
+    targets, sems, copies = refs[:4], refs[4], refs[5]
+    wqkv_ref, wout_ref, wup_ref, wdown_ref = targets
+    step = pl.program_id(0)
+    wait = weight_waits(meta_ref, layer, weights, targets, sems)
+    mlp_rows = PART_A + PART_B
+    mlp_copy = pltpu.make_async_copy(held_mlp, sums_ref.at[:, pl.ds(0, mlp_rows)], copies.at[0])
+    qkv_copy = pltpu.make_async_copy(held_qkv, sums_ref.at[:, pl.ds(mlp_rows, PART_C)], copies.at[1])
+
+    @pl.when(step == 0)
+    def _():
+        zero_all(mlp_accs)
+        zero_all(attn_accs)
+
+    @pl.when(step < N_TILE)
+    def _():
+        tile = step
+        outs = (
+            xh1.at[tile], r1.at[tile], qkv.at[tile], krow.at[tile], vrow.at[tile], lse.at[tile],
+            att_ref, xh2_ref, r2_ref, ks_ref, vs_ref,
+        )
+        hidden, second = forward_attn_part(
+            meta_ref, tile, x_ref, gains_ref, outs, (attf_ref,), wqkv_ref, wout_ref, wait
+        )
+        wait(2)
+        wait(3)
+        forward_mlp_part(hidden, second, (out_ref, act_ref, gp_ref), wup_ref, wdown_ref)
+        mlp_back_part(
+            masked_low(meta_ref, tile, cot_ref[...].T), (act_ref, gp_ref, xh2_ref, r2_ref, att_ref),
+            gains_ref, (wdown_ref, wup_ref, wout_ref), mlp_accs, lambda i: None, gh.at[tile],
+            gatt.at[tile],
+        )
+
+    @pl.when(step == N_TILE)
+    def _():
+        part_a, part_b = mlp_parts(*mlp_accs[:3])
+        write_shards(part_a + part_b, held_mlp)
+        mlp_copy.start()
+
+    @pl.when(step >= N_TILE)
+    def _():
+        tile = 2 * N_TILE - 1 - step
+        data = (
+            xh1.at[tile], r1.at[tile], qkv.at[tile], krow.at[tile], vrow.at[tile], lse.at[tile],
+            ks_ref, vs_ref,
+        )
+        gin_ref[...] = attn_back_part(
+            meta_ref, tile, gh.at[tile], gatt.at[tile], data, gains_ref, wqkv_ref, attn_accs,
+            rows_ref, lambda i: None,
+        )
+
+    @pl.when(step == 2 * N_TILE - 1)
+    def _():
+        gln2 = jnp.sum(mlp_accs[3][...].T, axis=0, keepdims=True)
+        parts = (
+            (attn_accs[0], 0, QKV_ROWS), (gain_rows(attn_accs[1], gln2), 0, GAIN_ROWS)
+        )
+        write_shards(parts, held_qkv)
+        qkv_copy.start()
+        mlp_copy.wait()
+        qkv_copy.wait()
 
 
 ANY = pl.BlockSpec(memory_space=pl.ANY)
@@ -484,10 +602,7 @@
     return pl.BlockSpec((height, TILE), lambda t, *_: (0, N_TILE - 1 - t))
 
 
-def call(kernel, grid, outs, in_specs, out_specs, scratch, flops, args):
-    moved = sum(a.size * a.dtype.itemsize for a in args) + sum(
-        o.size * o.dtype.itemsize for o in outs
-    )
+def call(kernel, grid, outs, in_specs, out_specs, scratch, args):
     return pl.pallas_call(
         kernel,
         out_shape=tuple(outs),
@@ -495,14 +610,9 @@
             num_scalar_prefetch=1, grid=grid, in_specs=in_specs, out_specs=out_specs,
             scratch_shapes=scratch,
         ),
-        cost_estimate=pl.CostEstimate(
-            flops=int(flops), bytes_accessed=int(moved), transcendentals=0
-        ),
+        cost_estimate=pl.CostEstimate(flops=0, bytes_accessed=0, transcendentals=0),
         compiler_params=pltpu.CompilerParams(vmem_limit_bytes=VMEM_LIMIT),
     )(*args)
-
-
-LINEAR = 2.0 * MB_TOK * D
 
 
 def col(height, kind=BF):
@@ -524,51 +634,31 @@
 MLP_OUTS = ([sds((MB_TOK, D), BF), col(FF), col(FF)], [(D, 0), (FF, 1), (FF, 1)])
 
 
-def input_spec(layer):
-    if layer == 0:
-        return pl.BlockSpec((TILE, D), lambda t, m: (m[6] * N_TILE + t, 0))
-    return rows_spec(D)
-
-
 def weight_scratch(*weights):
-    return [pltpu.VMEM(w[0].shape, BF) for w in weights] + [
+    return [pltpu.VMEM(w.own.shape, BF) for w in weights] + [
         pltpu.SemaphoreType.DMA((len(weights),))
     ]
 
 
 def flat(weights):
-    return [ref for weight in weights for ref in weight]
+    return [ref for weight in weights for ref in weight.flat()]
 
 
 def attn_scratch():
     return [pltpu.VMEM((D, TILE), BF)]
-
-
-def forward(meta, x, gains, wqkv, wout, wup, wdown, layer):
-    shapes, specs = attn_outputs()
-    weights = (wqkv, wout, wup, wdown)
-    out = call(
-        functools.partial(forward_kernel, layer=layer), (N_TILE,),
-        shapes + MLP_OUTS[0],
-        [input_spec(layer), whole((2, D))] + [ANY] * 20,
-        specs + [rows_spec(D), cols_spec(FF), cols_spec(FF)],
-        attn_scratch() + weight_scratch(*weights),
-        LINEAR * (4 * D + 2 * FF) * 1.5,
-        (meta, x, gains, *flat(weights)),
-    )
-    return out[:11], out[11:]
 
 
 def forward_attn(meta, x, gains, wqkv, wout, layer):
     shapes, specs = attn_outputs()
     weights = (wqkv, wout)
     out = call(
-        functools.partial(forward_attn_kernel, layer=layer), (N_TILE,),
+        functools.partial(forward_attn_kernel, layer=layer, weights=weights), (N_TILE,),
         shapes + [col(D, F32), col(D)],
-        [input_spec(layer), whole((2, D))] + [ANY] * 10,
+        [
+            pl.BlockSpec((TILE, D), lambda t, m: (m[6] * N_TILE + t, 0)), whole((2, D)),
+        ] + [ANY] * len(flat(weights)),
         specs + [cols_spec(D), cols_spec(D)],
         attn_scratch() + weight_scratch(*weights),
-        LINEAR * 4 * D * 2,
         (meta, x, gains, *flat(weights)),
     )
     return out[:11], out[11], out[12]
@@ -577,63 +667,115 @@
 def forward_mlp(meta, hidden, second, wup, wdown, layer):
     weights = (wup, wdown)
     return call(
-        functools.partial(forward_mlp_kernel, layer=layer), (N_TILE,),
+        functools.partial(forward_mlp_kernel, layer=layer, weights=weights), (N_TILE,),
         MLP_OUTS[0],
-        [cols_spec(D), cols_spec(D)] + [ANY] * 10,
+        [cols_spec(D), cols_spec(D)] + [ANY] * len(flat(weights)),
         [rows_spec(D), cols_spec(FF), cols_spec(FF)],
         weight_scratch(*weights),
-        LINEAR * 2 * FF * 1.5,
         (meta, hidden, second, *flat(weights)),
     )
 
 
+def mlp_scratch():
+    return [
+        pltpu.VMEM((FF, D), F32), pltpu.VMEM((FF, D), F32), pltpu.VMEM((D, D), F32),
+        pltpu.VMEM((D, SPAN), F32),
+    ]
+
+
+def attn_back_scratch():
+    return [
+        pltpu.VMEM((3 * D, D), F32), pltpu.VMEM((D, SPAN), F32), pltpu.VMEM((D, PAD_BLK), F32),
+        pltpu.VMEM((D, PAD_BLK), F32),
+    ]
+
+
 def mlp_back(meta, seed, act, gp, xh2, r2, att, gains, wdown, wup, wout, layer):
-    masked = layer == 1
-    if masked:
-        seed_spec = pl.BlockSpec((TILE, D), lambda t, m: (m[6] * N_TILE + N_TILE - 1 - t, 0))
-    else:
-        seed_spec = rev_rows(D)
     weights = (wdown, wup, wout)
-    half = 8 * sum(MLP_SHARDS)
+    half = 8 * (PART_A + PART_B)
     return call(
-        functools.partial(mlp_back_kernel, layer=layer, masked=masked), (N_TILE,),
+        functools.partial(mlp_back_kernel, layer=layer, weights=weights), (N_TILE,),
         [sds((half, D), BF), sds((half, D), BF), sds((1, D), F32), col(D, F32), col(D)],
         [
-            seed_spec, rev_cols(FF), rev_cols(FF), rev_cols(D), rev_cols(1), rev_cols(D),
+            rev_rows(D), rev_cols(FF), rev_cols(FF), rev_cols(D), rev_cols(1), rev_cols(D),
             whole((2, D)),
-        ] + [ANY] * 15,
+        ] + [ANY] * len(flat(weights)),
         [whole((half, D)), whole((half, D)), whole((1, D)), rev_cols(D), rev_cols(D)],
-        [
-            pltpu.VMEM((FF, D), F32), pltpu.VMEM((FF, D), F32), pltpu.VMEM((D, D), F32),
-            pltpu.VMEM((D, SPAN), F32),
-        ] + weight_scratch(*weights),
-        LINEAR * (4 * FF + 2 * D) * 1.5,
+        mlp_scratch() + weight_scratch(*weights),
         (meta, seed, act, gp, xh2, r2, att, gains, *flat(weights)),
     )
 
 
 def attn_back(meta, gh, gatt, xh1, r1, qkv, krow, vrow, lse, ks, vs, gains, gln2, wqkv, layer):
-    half = 8 * (sum(QKV_SHARDS) + GAIN_ROWS)
+    half = 8 * PART_C
     return call(
-        functools.partial(attn_back_kernel, layer=layer), (N_TILE,),
+        functools.partial(attn_back_kernel, layer=layer, weights=(wqkv,)), (N_TILE,),
         [sds((MB_TOK, D), BF), sds((half, D), BF), sds((half, D), BF)],
         [
             rev_cols(D), rev_cols(D), rev_cols(D), rev_cols(1), rev_cols(3 * D), rev_rows(D),
             rev_rows(D), rev_cols(HEADS), whole((PAD_BLK, D)), whole((PAD_BLK, D)), whole((2, D)),
             whole((1, D)),
-        ] + [ANY] * 5,
+        ] + [ANY] * len(wqkv.flat()),
         [rev_rows(D), whole((half, D)), whole((half, D))],
+        attn_back_scratch() + [pltpu.VMEM((3 * D, TILE), F32)] + weight_scratch(wqkv),
+        (meta, gh, gatt, xh1, r1, qkv, krow, vrow, lse, ks, vs, gains, gln2, *wqkv.flat()),
+    )
+
+
+def whole_layer(meta, x, cotangent, gains, wqkv, wout, wup, wdown, layer):
+    weights = (wqkv, wout, wup, wdown)
+    tiled = lambda *shape: pltpu.VMEM((N_TILE,) + shape, BF)
+    sums = sds((16, PART_A + PART_B + PART_C, D), BF)
+    forth = lambda t: jnp.minimum(t, N_TILE - 1)
+    back = lambda t, *_: (jnp.where(t < N_TILE, N_TILE - 1, 2 * N_TILE - 1 - t), 0)
+    return call(
+        functools.partial(layer_kernel, layer=layer, weights=weights), (2 * N_TILE,),
+        [sds((MB_TOK, D), BF), sds((MB_TOK, D), BF), sums],
         [
-            pltpu.VMEM((3 * D, D), F32), pltpu.VMEM((D, SPAN), F32), pltpu.VMEM((D, PAD_BLK), F32),
-            pltpu.VMEM((D, PAD_BLK), F32), pltpu.VMEM((3 * D, TILE), F32),
-        ] + weight_scratch(wqkv),
-        LINEAR * 12 * D * 1.5,
-        (meta, gh, gatt, xh1, r1, qkv, krow, vrow, lse, ks, vs, gains, gln2, *wqkv),
-    )
-
-
-def finish_kernel(meta_ref, *refs, widths, flips):
-    pieces, refs = refs[:4], refs[4:]
+            pl.BlockSpec((TILE, D), lambda t, *_: (forth(t), 0)),
+            pl.BlockSpec((TILE, D), lambda t, m: (m[6] * N_TILE + forth(t), 0)),
+            whole((2, D)),
+        ] + [ANY] * len(flat(weights)),
+        [
+            pl.BlockSpec((TILE, D), lambda t, *_: (forth(t), 0)),
+            pl.BlockSpec((TILE, D), back), ANY,
+        ],
+        [
+            tiled(D, TILE), pltpu.VMEM((N_TILE, 1, TILE), F32), tiled(3 * D, TILE), tiled(TILE, D),
+            tiled(TILE, D), pltpu.VMEM((N_TILE, HEADS, TILE), F32), pltpu.VMEM((D, TILE), BF),
+            pltpu.VMEM((D, TILE), BF), pltpu.VMEM((1, TILE), F32), pltpu.VMEM((PAD_BLK, D), BF),
+            pltpu.VMEM((PAD_BLK, D), BF), pltpu.VMEM((N_TILE, D, TILE), F32), tiled(D, TILE),
+            pltpu.VMEM((FF, TILE), BF), pltpu.VMEM((FF, TILE), BF), pltpu.VMEM((D, TILE), BF),
+            pltpu.VMEM((3 * D, TILE), F32),
+        ] + mlp_scratch() + attn_back_scratch() + [
+            pltpu.VMEM((16, PART_A + PART_B, D), BF), pltpu.VMEM((16, PART_C, D), BF),
+        ] + weight_scratch(*weights) + [pltpu.SemaphoreType.DMA((2,))],
+        (meta, x, cotangent, gains, *flat(weights)),
+    )
+
+
+def finish_whole_kernel(held, *outs, widths, flips):
+    total = sum(widths)
+    for i, (width, flip) in enumerate(zip(widths, flips)):
+        start = sum(widths[:i])
+        places = [(s & 3) * 4 + ((s >> 2) & 1) * 2 + (s >> 3) for s in range(16)]
+        value = jnp.concatenate(
+            [held[pl.ds(p * total + start, width)] for p in places], axis=0
+        )
+        outs[i][...] = (value.T if flip else value).astype(F32)
+
+
+def finish_whole(value, widths, flips, shapes, specs):
+    return pl.pallas_call(
+        functools.partial(finish_whole_kernel, widths=widths, flips=flips),
+        out_shape=tuple(sds(shape, F32) for shape in shapes),
+        grid=(1,), in_specs=[part_spec(value.shape, (0, 0))], out_specs=specs,
+        compiler_params=pltpu.CompilerParams(vmem_limit_bytes=VMEM_LIMIT),
+    )(value)
+
+
+def finish_kernel(meta_ref, *refs, widths, targets, extra):
+    pieces, refs = refs[:4], refs[4 + extra:]
     outs, held, sem = refs[:len(widths)], refs[-2], refs[-1]
     rows = held.shape[0] // 4
     for index, piece in enumerate(pieces):
@@ -645,27 +787,30 @@
     for index, piece in enumerate(pieces):
         pltpu.make_async_copy(piece, held.at[pl.ds(index * rows, rows)], sem).wait()
     total = sum(widths)
-    for i, (width, flip) in enumerate(zip(widths, flips)):
-        for s in range(16):
-            start = s * total + sum(widths[:i])
-            part = held[pl.ds(start, width)].astype(F32)
-            if flip:
-                outs[i][:, pl.ds(s * width, width)] = part.T
-            else:
-                outs[i][pl.ds(s * width, width)] = part
-
-
-def finish(meta, pieces, widths, flips):
+    for i, (width, flip) in enumerate(zip(widths, targets)):
+        start = sum(widths[:i])
+        value = jnp.concatenate(
+            [held[pl.ds(s * total + start, width)] for s in range(16)], axis=0
+        )
+        outs[i][...] = (value.T if flip else value).astype(F32)
+
+
+def finish(meta, pieces, widths, flips, shapes, specs, more=(), alias=None):
     rows = pieces[0].shape[0]
-    outs = [
-        sds((D, 16 * w), F32) if flip else sds((16 * w, D), F32) for w, flip in zip(widths, flips)
-    ]
-    return call(
-        functools.partial(finish_kernel, widths=widths, flips=flips), (1,),
-        outs, [ANY] * 4, [whole(o.shape) for o in outs],
-        [pltpu.VMEM((4 * rows, D), BF), pltpu.SemaphoreType.DMA],
-        0.0, (meta, *pieces),
-    )
+    return pl.pallas_call(
+        functools.partial(finish_kernel, widths=widths, targets=flips, extra=len(more)),
+        out_shape=tuple(sds(shape, F32) for shape in shapes),
+        grid_spec=pltpu.PrefetchScalarGridSpec(
+            num_scalar_prefetch=1, grid=(1,), in_specs=[ANY] * (4 + len(more)), out_specs=specs,
+            scratch_shapes=[pltpu.VMEM((4 * rows, D), BF), pltpu.SemaphoreType.DMA],
+        ),
+        input_output_aliases=alias or {},
+        compiler_params=pltpu.CompilerParams(vmem_limit_bytes=VMEM_LIMIT),
+    )(meta, *pieces, *more)
+
+
+def part_spec(shape, index):
+    return pl.BlockSpec(shape, lambda t, *_: index)
 
 
 def swap_xor(value, mask):
@@ -679,6 +824,15 @@
 
 def to_section(value, target):
     return lax.ppermute(value, "section", [(1 - target, target)])
+
+
+def exchange(value0, value1):
+    return swap_section(jnp.where(lax.axis_index("section") == 0, value1, value0))
+
+
+def low_groups():
+    size = lax.axis_size("dp")
+    return None if size == 16 else [list(range(i, i + 16)) for i in range(0, size, 16)]
 
 
 def added(*values):
@@ -756,18 +910,15 @@
     return jnp.concatenate(parts, axis=0)
 
 
-def gather_pieces(value):
+def gather_rest(value):
     for bit in reversed(rest_bits()):
         value = gather_bit(value, bit)
-    value = gather_quad(value, 2)
+    return value
+
+
+def spread_pieces(value):
     across = swap_xor(value, 2)
     return value, swap_xor(value, 1), across, swap_xor(across, 1)
-
-
-def fetch_pieces(value):
-    piece = swap_section(value)
-    across = swap_xor(piece, 2)
-    return piece, swap_xor(piece, 1), across, swap_xor(across, 1)
 
 
 def sum_rest(value):
@@ -789,97 +940,109 @@
     ])
     own = (w_qkv[0], w_out[0], w_up[0], w_down[0])
 
-    def quarter(weight):
-        rows = weight.shape[0] // 4
-        return lax.dynamic_slice_in_dim(weight, place * rows, rows, 0)
+    def part(weight, spot, count):
+        rows = weight.shape[0] // count
+        return lax.dynamic_slice_in_dim(weight, spot * rows, rows, 0)
 
     own_gains = jnp.concatenate([ln1_gain, ln2_gain], axis=0)
     other_gains = swap_section(own_gains)
-    wqkv = (own[0],) + fetch_pieces(quarter(own[0]))
-    wout = (own[1],) + fetch_pieces(quarter(own[1]))
-    up = swap_section(quarter(own[2]))
-    down = swap_section(quarter(own[3]))
+    attn = [
+        part(own[0][:, :2 * D], place, 4),
+        jnp.concatenate([part(own[0][:, 2 * D:], place, 4), part(own[1], place, 4)], axis=1),
+    ]
+    attn = [swap_section(value) for value in attn]
+    late = part(own[2], place, 4), part(own[3], place & 1, 2)
+    attn[1], other_gains, late = tie(attn[1], other_gains, late)
+    up, down = swap_section(late[0]), swap_section(late[1])
+    gains = [jnp.where(first, own_gains, other_gains), jnp.where(first, other_gains, own_gains)]
+    attn_x = [swap_xor(value, 2) for value in attn]
+    front, rest = [(v, swap_xor(v, 1), x, swap_xor(x, 1)) for v, x in zip(attn, attn_x)]
+    wqkv = Weight(own[0], (front, 0, 0, 2 * D), (rest, 0, 2 * D, D))
+    wout = Weight(own[1], (rest, D, 0, D))
     up_x, up_c = swap_xor(up, 2), swap_xor(up, 1)
-    gains = [jnp.where(first, own_gains, other_gains), jnp.where(first, other_gains, own_gains)]
 
     keep0, hidden, second = forward_attn(meta, tokens, gains[0], wqkv, wout, 0)
     keep0, hidden, second, up_x, up_c, down = tie(keep0, hidden, second, up_x, up_c, down)
-    down_x = swap_xor(down, 2)
-    wup = (own[2], up, up_c, up_x, swap_xor(up_x, 1))
-    wdown = (own[3], down, swap_xor(down, 1), down_x, swap_xor(down_x, 1))
+    wup = Weight(own[2], ((up, up_c, up_x, swap_xor(up_x, 1)), 0, 0, None))
+    wdown = Weight(own[3], ((down, swap_xor(down, 1)), 0, 0, None))
     act_out0, act0, gp0 = forward_mlp(meta, hidden, second, wup, wdown, 0)
-    half = MB_TOK // 2
-    out0_a = to_section(act_out0[:half], 0)
-    forward1 = forward(meta, act_out0, gains[1], wqkv, wout, wup, wdown, 1)
-    (keep1, (act_out1, act1, gp1)), out0_a, act_out0 = tie(forward1, out0_a, act_out0)
-    out0_b = to_section(act_out0[half:], 0)
-    out1_a = to_section(act_out1[:half], 1)
-
-    def back_mlp(layer, seed, keep, act, gp):
-        att, xh2, r2 = keep[6:9]
-        return mlp_back(meta, seed, act, gp, xh2, r2, att, gains[layer], wdown, wup, wout, layer)
-
-    def back_attn(layer, gh, gatt, keep, gln2):
-        xh1, r1, qkv, krow, vrow, lse = keep[:6]
-        return attn_back(
-            meta, gh, gatt, xh1, r1, qkv, krow, vrow, lse, keep[9], keep[10], gains[layer], gln2,
-            wqkv, layer,
+    act_out1, ig1, sums1 = whole_layer(
+        meta, act_out0, cotangent, gains[1], wqkv, wout, wup, wdown, 1
+    )
+    cut = 2 * MB_TOK // 3
+    acts_a = exchange(act_out0[:cut], act_out1[:cut])
+    sums1 = lax.psum_scatter(
+        sums1.reshape(-1, D), "dp", scatter_dimension=0, axis_index_groups=low_groups(), tiled=True
+    )
+    xh1, r1, qkv, krow, vrow, lse, att, xh2, r2, ks, vs = keep0
+    back = mlp_back(meta, ig1, act0, gp0, xh2, r2, att, gains[0], wdown, wup, wout, 0)
+    (send, kept, gln2, gh, gatt), acts_a, act_out0, act_out1 = tie(back, acts_a, act_out0, act_out1)
+    mlp0 = added(kept, swap_xor(send, 1))
+    a0, b0 = halves(mlp0[:8 * PART_A], 1), quarters(mlp0[8 * PART_A:], 2)
+    gh, a0, b0 = tie(gh, a0, b0)
+    acts_b = exchange(act_out0[cut:], act_out1[cut:])
+    a0_x, b0_z = swap_xor(a0[1], 2), swap_quarters(b0, 2)
+    back = attn_back(
+        meta, gh, gatt, xh1, r1, qkv, krow, vrow, lse, ks, vs, gains[0], gln2, wqkv, 0
+    )
+    (ig0, send, kept), a0_x, b0_z, acts_b = tie(back, a0_x, b0_z, acts_b)
+    acts_in = jnp.concatenate([acts_a, acts_b], axis=0)
+    grads_in = exchange(ig0, ig1)
+    c0 = swap_xor(send, 1)
+    a0 = quarters(added(a0[0], a0_x), 2)
+    a0, c0 = tie(a0, c0)
+    a0_z = swap_quarters(a0, 2)
+    c0 = halves(added(kept, c0), 1)
+    b0 = halves(added(b0[0], *b0_z), 1)
+    bc0_x = swap_xor(jnp.concatenate([b0[1], c0[1]], axis=0), 2)
+
+    def own_sum(grad0, grad1):
+        return added(jnp.where(first, grad0, grad1), swap_section(jnp.where(first, grad1, grad0)))
+
+    b0 = added(b0[0], bc0_x[:PART_B])
+    c0 = quarters(added(c0[0], bc0_x[PART_B:]), 2)
+    c0_z = swap_quarters(c0, 2)
+    a0_z, b0, c0_1, grads_in = tie(a0_z, b0, c0[1], grads_in)
+    a0 = added(a0[0], *a0_z)
+    spots = (0, PART_A, PART_A + PART_B, PART_A + PART_B + QKV_ROWS)
+    a1, b1, c1, gains1 = [sums1[i:j] for i, j in zip(spots, spots[1:] + (sums1.shape[0],))]
+    ab = own_sum(
+        jnp.concatenate([reduce_rest(a0), reduce_rest(b0)], axis=0),
+        jnp.concatenate([reduce_rest(a1), reduce_rest(b1)], axis=0),
+    )
+    a_rows = ab.shape[0] * PART_A // (PART_A + PART_B)
+    a_full = lax.all_gather(
+        gather_rest(ab[:a_rows]), "dp", axis=0, axis_index_groups=low_groups(), tiled=True
+    )
+    c0 = added(c0[0], *c0_z)
+    c_own = own_sum(
+        jnp.concatenate([reduce_rest(c0[:QKV_ROWS]), sum_rest(c0[QKV_ROWS:])], axis=0),
+        jnp.concatenate([reduce_rest(c1), sum_rest(gains1)], axis=0),
+    )
+    lns = c_own[-GAIN_ROWS:][:2].astype(F32)
+    bc_own = jnp.concatenate([gather_rest(ab[a_rows:]), gather_rest(c_own[:-GAIN_ROWS])], axis=0)
+    bc_pieces = spread_pieces(gather_quad(bc_own, 2))
+    grad_down, grad_up, grad_out = finish_whole(
+        a_full, (DOWN_ROWS, UP_A // 16, OUT_ROWS), (False, True, False),
+        [(FF, D), (D, FF), (D, D)],
+        [
+            part_spec((FF, D), (0, 0)), part_spec((D, UP_A), (0, UP_B // UP_A)),
+            part_spec((D, D), (0, 0)),
+        ],
+    )
+    grad_up, grad_qkv = finish(
+        meta, bc_pieces, (UP_B // 16, QKV_ROWS), (True, True), [(D, FF), (D, 3 * D)],
+        [part_spec((D, UP_B), (0, 0)), part_spec((D, 3 * D), (0, 0))],
+        (grad_up,), {5: 0},
+    )
+
+    def assemble(value0, value1, got):
+        return jnp.concatenate(
+            [jnp.where(first, value0, got), jnp.where(first, got, value1)], axis=0
         )
 
-    back = back_mlp(1, cotangent, keep1, act1, gp1)
-    (send, kept, gln2, gh, gatt), out0_b, out1_a, act_out1 = tie(back, out0_b, out1_a, act_out1)
-    mlp1 = halves(reduce_core((send, kept)), 1)
-    gh, mlp1 = tie(gh, mlp1)
-    mlp1_x = swap_xor(mlp1[1], 2)
-    out1_b = to_section(act_out1[half:], 1)
-    back = back_attn(1, gh, gatt, keep1, gln2)
-    (ig1, send, kept), mlp1_x, out1_b = tie(back, mlp1_x, out1_b)
-    qkv1 = halves(reduce_core((send, kept)), 1)
-    mlp1 = quarters(added(mlp1[0], mlp1_x), 2)
-    ig1, mlp1, qkv1 = tie(ig1, mlp1, qkv1)
-    mlp1_z = swap_quarters(mlp1, 2)
-    qkv1_x = swap_xor(qkv1[1], 2)
-    ig1_a = to_section(ig1[:half], 1)
-    back = back_mlp(0, ig1, keep0, act0, gp0)
-    (send, kept, gln2, gh, gatt), mlp1_z, qkv1_x, ig1_a, ig1 = tie(
-        back, mlp1_z, qkv1_x, ig1_a, ig1
-    )
-    mlp0 = halves(reduce_core((send, kept)), 1)
-    mlp1 = added(mlp1[0], *mlp1_z)
-    qkv1 = quarters(added(qkv1[0], qkv1_x), 2)
-    gh, mlp0, mlp1, qkv1 = tie(gh, mlp0, mlp1, qkv1)
-    mlp0_x = swap_xor(mlp0[1], 2)
-    qkv1_z = swap_quarters(qkv1, 2)
-    ig1_b = to_section(ig1[half:], 1)
-    back = back_attn(0, gh, gatt, keep0, gln2)
-    (ig0, send, kept), mlp0_x, qkv1_z, ig1_b = tie(back, mlp0_x, qkv1_z, ig1_b)
-    ig0_in = to_section(ig0, 0)
-    qkv0 = halves(reduce_core((send, kept)), 1)
-    mlp0 = quarter_sum(quarters(added(mlp0[0], mlp0_x), 2), 2)
-    qkv1 = added(qkv1[0], *qkv1_z)
-    qkv0 = quarter_sum(quarters(half_sum(qkv0, 1), 2), 2)
-
-    def own_sum(grad0, grad1):
-        got = swap_section(jnp.where(first, grad1, grad0))
-        return added(jnp.where(first, grad0, grad1), got)
-
-    mlp = gather_pieces(own_sum(reduce_rest(mlp0), reduce_rest(mlp1)))
-    cut = sum(QKV_SHARDS)
-    qkv = jnp.concatenate([reduce_rest(qkv0[:cut]), sum_rest(qkv0[cut:])], axis=0)
-    qkv = own_sum(qkv, jnp.concatenate([reduce_rest(qkv1[:cut]), sum_rest(qkv1[cut:])], axis=0))
-    lns = qkv[-GAIN_ROWS:][:2].astype(F32)
-    qkv = gather_pieces(qkv[:-GAIN_ROWS])
-    grad_down, grad_up, grad_out = finish(meta, mlp, MLP_SHARDS, (False, True, False))
-    (grad_qkv,) = finish(meta, qkv, QKV_SHARDS, (True,))
-    out0_in = jnp.concatenate([out0_a, out0_b], axis=0)
-    out1_in = jnp.concatenate([out1_a, out1_b], axis=0)
-    ig1_in = jnp.concatenate([ig1_a, ig1_b], axis=0)
-    activations = jnp.concatenate(
-        [jnp.where(first, act_out0, out1_in), jnp.where(first, out0_in, act_out1)], axis=0
-    )
-    input_grads = jnp.concatenate(
-        [jnp.where(first, ig0, ig1_in), jnp.where(first, ig0_in, ig1)], axis=0
-    )
+    activations = assemble(act_out0, act_out1, acts_in)
+    input_grads = assemble(ig0, ig1, grads_in)
     return (
         activations[None],
         input_grads[None],

time: 393 us -> 374 us (0.952)
  the two profiles are of different devices: /device:TPU:0 before, /device:TPU:17 now
where the time goes in v3:
time: 374 us; the launch traced here: 373 us
  Pallas kernels  159 us (43%)
  waiting for transfers between devices  102 us (27%)
  starting transfers between devices  47.6 us (13%)
  local copies, waits for them, and re-layouts  25.5 us (7%)
  other arithmetic  23.7 us (6%)
  between operations  14.8 us (4%)
    pallas_call x5, Pallas kernels, call(): pl.pallas_call(kernel, out_shape=tuple(outs), grid_spec=pltpu.PrefetchSca...  149 us
    ppermute x29, waiting for transfers between devices, swap_xor(): return lax.ppermute(value, 'dp', [(i, i ^ mask) for i in range(size)])  81.2 us
    ppermute x29, starting transfers between devices, swap_xor(): return lax.ppermute(value, 'dp', [(i, i ^ mask) for i in range(size)])  36.8 us
    ppermute x10, waiting for transfers between devices, swap_section(): return lax.ppermute(value, 'section', [(0, 1), (1, 0)])  20.7 us
    unnamed x67, local copies, waits for them, and re-layouts  11.3 us
    ppermute x10, starting transfers between devices, swap_section(): return lax.ppermute(value, 'section', [(0, 1), (1, 0)])  10.7 us
    convert_element_type x9, other arithmetic, added(): return total.astype(BF)  10.4 us
  transfers between devices with their start and end apart: 41, of which 17 were waited for; matrix products, arithmetic and copies ran while one was open for 9% of the time, Pallas kernels for 19%

profile of v3, /device:TPU:17, one launch (start us, length us, event | category | flops | bytes accessed | tf_op | source)
XLA Modules:
  0.0 372.6 jit_solution(9219746497254897073)
XLA Ops:
  18.9 4.1 %collective-permute-done.2.refs_1_ = bf16[128,1024]{1,0:T(8,128)(2,1)S(1)} collective-permute-done((bf16[128,1024]{1,0:T(8,128)(2,1)}, bf16[128,1024]{1,0:T(8,128)(2,1)S(1)}, u32[]{:S(2)}, u32[]{:S(2)}) %collective-permute-start.2) | collective-permute-done | bytes 262176 | tf_op jit(solution)/shard_map/ppermute | solution.py:822
  23.1 2.7 collective-permute-start.3
  28.3 6.1 %collective-permute-done.9.refs_1_.refs_15_.refs_4_ = bf16[128,2048]{1,0:T(8,128)(2,1)S(1)} collective-permute-done((bf16[128,2048]{1,0:T(8,128)(2,1)S(1)}, bf16[128,2048]{1,0:T(8,128)(2,1)S(1)}, u32[]{:S(2)}, u32[]{:S(2)}) %collective-permute-start.9) | collective-permute-done | bytes 524320 | tf_op jit(solution)/shard_map/ppermute | solution.py:822
  35.7 2.9 collective-permute-start.11
  42.5 16.1 %shard_map.161 = (bf16[512,1536]{1,0:T(8,128)(2,1)}, f32[1,1536]{1,0:T(1,128)}, bf16[1536,1536]{1,0:T(8,128)(2,1)}, bf16[1536,512]{1,0:T(8,128)(2,1)}, bf16[1536...) custom-call(s32[8]{0:T(128)} %pad_add_fusion.meta_ref, ...), custom_call_target="tpu_custom_call" | custom-call | tf_op jit(solution)/shard_map/pallas_call | solution.py:606
  59.2 2.9 collective-permute-done.13.refs_4_.refs_18_.refs_7_
  63.3 15.7 %shard_map.162 = (bf16[1536,512]{1,0:T(8,128)(2,1)}, bf16[2048,1536]{1,0:T(8,128)(2,1)}, bf16[2048,1536]{1,0:T(8,128)(2,1)}) custom-call(s32[8]{0:T(128)} %pad_add_fusion.meta_ref, f32[512,1536]{1,0:T(8,128)} %get-tuple-element.110.hid_ref, bf16[512,1536]{1,0:T(8,128)(2,1)} %get-tuple-element.111.sec_ref, bf16[512,2048]{1,0:T(8,128)(2,1)} %bitcast.33, ...), custom_call_target="tpu_custom_call" | custom-call | tf_op jit(solution)/shard_map/pallas_call | solution.py:606
  79.1 68.5 %shard_map.163 = (bf16[1536,512]{1,0:T(8,128)(2,1)}, bf16[1536,512]{1,0:T(8,128)(2,1)}, bf16[16,400,512]{2,1,0:T(8,128)(2,1)}) custom-call(s32[8]{0:T(128)} %pad_add_fusion.meta_ref, bf16[1536,512]{1,0:T(8,128)(2,1)} %get-tuple-element.128.x_ref, bf16[3072,512]{1,0:T(8,128)(2,1)} %cot_ref.1, f32[2,512]{1,0:T(2,128)} %get-tuple-element.200.gains_ref, ...), custom_call_target="tpu_custom_call" | custom-call | tf_op jit(solution)/shard_map/pallas_call | solution.py:606
  150.9 28.8 %shard_map.164 = (bf16[2304,512]{1,0:T(8,128)(2,1)}, bf16[2304,512]{1,0:T(8,128)(2,1)}, f32[1,512]{1,0:T(1,128)}, f32[512,1536]{1,0:T(8,128)}, bf16[512,1536]{1,0:T(8,128)(2,1)}) custom-call(s32[8]{0:T(128)} %pad_add_fusion.meta_ref, bf16[1536,512]{1,0:T(8,128)(2,1)} %get-tuple-element.116.seed_ref, bf16[2048,1536]{1,0:T(8,128)(2,1)} %get-tuple-element.117.act_ref, ...), custom_call_target="tpu_custom_call" | custom-call | tf_op jit(solution)/shard_map/pallas_call | solution.py:606
  180.3 4.5 %collective-permute-done.16 = bf16[2304,512]{1,0:T(8,128)(2,1)} collective-permute-done((bf16[2304,512]{1,0:T(8,128)(2,1)}, bf16[2304,512]{1,0:T(8,128)(2,1)}, u32[]{:S(2)}, u32[]{:S(2)}) %collective-permute-start.16) | collective-permute-done | bytes 2359328 | tf_op jit(solution)/shard_map/ppermute | solution.py:818
  184.8 3.0 add_convert_fusion
  197.0 19.5 %shard_map.165 = (bf16[1536,512]{1,0:T(8,128)(2,1)}, bf16[896,512]{1,0:T(8,128)(2,1)}, bf16[896,512]{1,0:T(8,128)(2,1)}) custom-call(s32[8]{0:T(128)} %pad_add_fusion.meta_ref, f32[512,1536]{1,0:T(8,128)} %get-tuple-element.133.gh_ref, bf16[512,1536]{1,0:T(8,128)(2,1)} %get-tuple-element.134.gatt_ref, bf16[512,1536]{1,0:T(8,128)(2,1)} %get-tuple-element.135.xh1_ref, ...), custom_call_target="tpu_custom_call" | custom-call | tf_op jit(solution)/shard_map/pallas_call | solution.py:606
  216.5 6.6 %collective-permute-done.20 = bf16[192,512]{1,0:T(8,128)(2,1)} collective-permute-done((bf16[192,512]{1,0:T(8,128)(2,1)S(1)}, bf16[192,512]{1,0:T(8,128)(2,1)}, u32[]{:S(2)}, u32[]{:S(2)}) %collective-permute-start.20) | collective-permute-done | bytes 196640 | tf_op jit(solution)/shard_map/ppermute | solution.py:818
  223.1 3.7 %collective-permute-start.22 = (bf16[896,512]{1,0:T(8,128)(2,1)}, bf16[896,512]{1,0:T(8,128)(2,1)S(1)}, u32[]{:S(2)}, u32[]{:S(2)}) collective-permute-start(bf16[896,512]{1,0:T(8,128)(2,1)} %get-tuple-element.156), channel_id=1, source_target_pairs={{0,1},{1,0},{2,3},{3,2},{4,5},{5,4},{6,7},{7,6},{8,9},{9,8},{10,11... | collective-permute-start | bytes 2752520 | tf_op jit(solution)/shard_map/ppermute | solution.py:818
  228.2 3.1 collective-permute-start.27
  240.3 11.6 %collective-permute-done.26 = bf16[544,512]{1,0:T(8,128)(2,1)} collective-permute-done((bf16[544,512]{1,0:T(8,128)(2,1)}, bf16[544,512]{1,0:T(8,128)(2,1)}, u32[]{:S(2)}, u32[]{:S(2)}) %collective-permute-start.26) | collective-permute-done | bytes 557088 | tf_op jit(solution)/shard_map/ppermute | solution.py:818
  255.6 9.5 %collective-permute-done.25 = bf16[192,512]{1,0:T(8,128)(2,1)S(1)} collective-permute-done((bf16[192,512]{1,0:T(8,128)(2,1)}, bf16[192,512]{1,0:T(8,128)(2,1)S(1)}, u32[]{:S(2)}, u32[]{:S(2)}) %collective-permute-start.25) | collective-permute-done | bytes 196640 | tf_op jit(solution)/shard_map/ppermute | solution.py:818
  269.8 6.7 %collective-permute-done.32 = bf16[288,512]{1,0:T(8,128)(2,1)S(1)} collective-permute-done((bf16[288,512]{1,0:T(8,128)(2,1)S(1)}, bf16[288,512]{1,0:T(8,128)(2,1)S(1)}, u32[]{:S(2)}, u32[]{:S(2)}) %collective-permute-start.32) | collective-permute-done | bytes 294944 | tf_op jit(solution)/shard_map/ppermute | solution.py:822
  279.3 3.3 collective-permute-start.29
  283.9 7.8 %collective-permute-done.29 = bf16[112,512]{1,0:T(8,128)(2,1)S(1)} collective-permute-done((bf16[112,512]{1,0:T(8,128)(2,1)}, bf16[112,512]{1,0:T(8,128)(2,1)S(1)}, u32[]{:S(2)}, u32[]{:S(2)}) %collective-permute-start.29) | collective-permute-done | bytes 114720 | tf_op jit(solution)/shard_map/ppermute | solution.py:818
  294.8 2.1 collective-permute-done.31
  297.9 3.4 collective-permute-start.33
  302.8 2.2 collective-permute-done.33
  305.0 3.1 collective-permute-done.34
  308.1 22.9 %collective-permute-done.35 = bf16[192,512]{1,0:T(8,128)(2,1)S(1)} collective-permute-done((bf16[192,512]{1,0:T(8,128)(2,1)S(1)}, bf16[192,512]{1,0:T(8,128)(2,1)S(1)}, u32[]{:S(2)}, u32[]{:S(2)}) %collective-permute-start.35) | collective-permute-done | bytes 196640 | tf_op jit(solution)/shard_map/ppermute | solution.py:818
  331.5 1.9 maximum_bitcast_fusion
  335.9 2.7 collective-permute-start.36
  338.6 9.2 %collective-permute-done.37.refs_2_ = bf16[768,512]{1,0:T(8,128)(2,1)S(1)} collective-permute-done((bf16[768,512]{1,0:T(8,128)(2,1)S(1)}, bf16[768,512]{1,0:T(8,128)(2,1)S(1)}, u32[]{:S(2)}, u32[]{:S(2)}) %collective-permute-start.37) | collective-permute-done | bytes 786464 | tf_op jit(solution)/shard_map/ppermute | solution.py:818
  347.8 3.6 collective-permute-start.38
  351.4 1.9 maximum_bitcast_fusion.1
  353.9 4.8 %shard_map.166 = (f32[2048,512]{1,0:T(8,128)}, f32[512,2048]{1,0:T(8,128)}, f32[512,512]{1,0:T(8,128)}) custom-call(bf16[3072,512]{1,0:T(8,128)(2,1)} %all-gather.2.cloned.1.call-done.held), custom_call_target="tpu_custom_call" | custom-call | tf_op jit(solution)/shard_map/pallas_call | solution.py:769
  359.9 5.7 %shard_map.167 = (f32[512,2048]{1,0:T(8,128)}, f32[512,1536]{1,0:T(8,128)}) custom-call(s32[8]{0:T(128)} %pad_add_fusion.meta_ref, bf16[768,512]{1,0:T(8,128)(2,1)} %copy-done.18, bf16[768,512]{1,0:T(8,128)(2,1)} %copy-done.27, bf16[768,512]{1,0:T(8,128)(2,1)} %copy-done.26, bf16[768,512]{1,0:T(8,128)(2,1)} %copy-done.28, ...), custom_call_target="tpu_custom_call", output_to_operand_aliasing={{0}: (5, {})} | custom-call | tf_op jit(solution)/shard_map/pallas_call | solution.py:800
  (176 shorter events, 66.9 us)
Async XLA Ops:
  7.2 260.2 %reduce-scatter.2.cloned.1.call-start = ((), (), s32[]{:S(2)}) async-start(), calls=%async_computation.1 | async-start | bytes 6963200 | tf_op jit(solution)/shard_map/reduce_scatter | solution.py:974
  10.0 7.5 %collective-permute-start = (bf16[128,1024]{1,0:T(8,128)(2,1)}, bf16[128,1024]{1,0:T(8,128)(2,1)S(1)}, u32[]{:S(2)}, u32[]{:S(2)}) collective-permute-start(bf16[128,1024]{1,0:T(8,128)(2,1)} %pad_maximum_fusion.3), channel_id=1, source_target_pairs={{0,16},{16,0},{1,17},{17,1},{2,18},{18,2},{3,19},{19,3},{4,20},{20... | collective-permute-start | bytes 786440 | tf_op jit(solution)/shard_map/ppermute | solution.py:822
  13.7 9.4 %collective-permute-start.2 = (bf16[128,1024]{1,0:T(8,128)(2,1)}, bf16[128,1024]{1,0:T(8,128)(2,1)S(1)}, u32[]{:S(2)}, u32[]{:S(2)}) collective-permute-start(bf16[128,1024]{1,0:T(8,128)(2,1)} %constant_dynamic-slice_fusion.15), channel_id=1, source_target_pairs={{0,16},{16,0},{1,17},{17,1},{2,18},{18,2},{3,19},{19,3},{4,20},{20... | collective-permute-start | bytes 786440 | tf_op jit(solution)/shard_map/ppermute | solution.py:822
  17.5 17.0 %collective-permute-start.9 = (bf16[128,2048]{1,0:T(8,128)(2,1)S(1)}, bf16[128,2048]{1,0:T(8,128)(2,1)S(1)}, u32[]{:S(2)}, u32[]{:S(2)}) collective-permute-start(bf16[128,2048]{1,0:T(8,128)(2,1)S(1)} %dynamic-slice_bitcast_fusion.1), channel_id=1, source_target_pairs={{0,16},{16,0},{1,17},{17,1},{2,18},{18,2},{3,19},{19,3},{4,20},{20... | collective-permute-start | bytes 1572872 | tf_op jit(solution)/shard_map/ppermute | solution.py:822
  18.7 39.9 %collective-permute-start.12 = (bf16[1024,512]{1,0:T(8,128)(2,1)}, bf16[1024,512]{1,0:T(8,128)(2,1)S(1)}, u32[]{:S(2)}, u32[]{:S(2)}) collective-permute-start(bf16[1024,512]{1,0:T(8,128)(2,1)} %dynamic-slice_bitcast_fusion), channel_id=1, source_target_pairs={{0,16},{16,0},{1,17},{17,1},{2,18},{18,2},{3,19},{19,3},{4,20},{20... | collective-permute-start | bytes 3145736 | tf_op jit(solution)/shard_map/ppermute | solution.py:822
  25.8 9.9 %collective-permute-start.4 = (bf16[128,1024]{1,0:T(8,128)(2,1)S(1)}, bf16[128,1024]{1,0:T(8,128)(2,1)}, u32[]{:S(2)}, u32[]{:S(2)}) collective-permute-start(bf16[128,1024]{1,0:T(8,128)(2,1)S(1)} %collective-permute-done.2.refs_1_), channel_id=1, source_target_pairs={{0,2},{1,3},{2,0},{3,1},{4,6},{5,7},{6,4},{7,5},{8,10},{9,11},{10,... | collective-permute-start | bytes 786440 | tf_op jit(solution)/shard_map/ppermute | solution.py:818
  27.0 11.5 %collective-permute-start.6 = (bf16[128,1024]{1,0:T(8,128)(2,1)S(1)}, bf16[128,1024]{1,0:T(8,128)(2,1)S(1)}, u32[]{:S(2)}, u32[]{:S(2)}) collective-permute-start(bf16[128,1024]{1,0:T(8,128)(2,1)S(1)} %collective-permute-done.refs_5_.refs_10_.refs_9_), channel_id=1, source_target_pairs={{0,1},{1,0},{2,3},{3,2},{4,5},{5,4},{6,7},{7,6},{8,9},{9,8},{10,11... | collective-permute-start | bytes 786440 | tf_op jit(solution)/shard_map/ppermute | solution.py:818
  27.3 12.1 %collective-permute-start.7 = (bf16[128,1024]{1,0:T(8,128)(2,1)S(1)}, bf16[128,1024]{1,0:T(8,128)(2,1)S(1)}, u32[]{:S(2)}, u32[]{:S(2)}) collective-permute-start(bf16[128,1024]{1,0:T(8,128)(2,1)S(1)} %collective-permute-done.refs_5_.refs_10_.refs_9_), channel_id=1, source_target_pairs={{0,2},{1,3},{2,0},{3,1},{4,6},{5,7},{6,4},{7,5},{8,10},{9,11},{10,... | collective-permute-start | bytes 786440 | tf_op jit(solution)/shard_map/ppermute | solution.py:818
  34.4 24.2 %collective-permute-start.10 = (bf16[128,2048]{1,0:T(8,128)(2,1)S(1)}, bf16[128,2048]{1,0:T(8,128)(2,1)S(1)}, u32[]{:S(2)}, u32[]{:S(2)}) collective-permute-start(bf16[128,2048]{1,0:T(8,128)(2,1)S(1)} %collective-permute-done.9.refs_1_.refs_15_.refs_4_), channel_id=1, source_target_pairs={{0,2},{1,3},{2,0},{3,1},{4,6},{5,7},{6,4},{7,5},{8,10},{9,11},{10,... | collective-permute-start | bytes 1572872 | tf_op jit(solution)/shard_map/ppermute | solution.py:818
  35.7 23.0 %collective-permute-start.11 = (bf16[128,2048]{1,0:T(8,128)(2,1)S(1)}, bf16[128,2048]{1,0:T(8,128)(2,1)}, u32[]{:S(2)}, u32[]{:S(2)}) collective-permute-start(bf16[128,2048]{1,0:T(8,128)(2,1)S(1)} %collective-permute-done.9.refs_1_.refs_15_.refs_4_), channel_id=1, source_target_pairs={{0,1},{1,0},{2,3},{3,2},{4,5},{5,4},{6,7},{7,6},{8,9},{9,8},{10,11... | collective-permute-start | bytes 1572872 | tf_op jit(solution)/shard_map/ppermute | solution.py:818
  147.7 206.2 %all-gather.2.cloned.1.call-start = ((), (), s32[]{:S(2)}) async-start(), calls=%async_computation.2 | async-start | bytes 3342336 | tf_op jit(solution)/shard_map/all_gather | solution.py:1014
  149.6 30.0 %collective-permute-start.15 = (bf16[1024,512]{1,0:T(8,128)(2,1)S(1)}, bf16[1024,512]{1,0:T(8,128)(2,1)}, u32[]{:S(2)}, u32[]{:S(2)}) collective-permute-start(bf16[1024,512]{1,0:T(8,128)(2,1)S(1)} %slice_select_fusion), channel_id=1, source_target_pairs={{0,16},{16,0},{1,17},{17,1},{2,18},{18,2},{3,19},{19,3},{4,20},{20... | collective-permute-start | bytes 3145736 | tf_op jit(solution)/shard_map/ppermute | solution.py:822
  192.1 31.0 %collective-permute-start.17 = (bf16[768,512]{1,0:T(8,128)(2,1)}, bf16[768,512]{1,0:T(8,128)(2,1)}, u32[]{:S(2)}, u32[]{:S(2)}) collective-permute-start(bf16[768,512]{1,0:T(8,128)(2,1)} %get-tuple-element.147), channel_id=1, source_target_pairs={{0,2},{1,3},{2,0},{3,1},{4,6},{5,7},{6,4},{7,5},{8,10},{9,11},{10,... | collective-permute-start | bytes 2359304 | tf_op jit(solution)/shard_map/ppermute | solution.py:818
  194.3 22.1 %collective-permute-start.21 = (bf16[512,512]{1,0:T(8,128)(2,1)}, bf16[512,512]{1,0:T(8,128)(2,1)}, u32[]{:S(2)}, u32[]{:S(2)}) collective-permute-start(bf16[512,512]{1,0:T(8,128)(2,1)} %slice_select_fusion.1), channel_id=1, source_target_pairs={{0,16},{16,0},{1,17},{17,1},{2,18},{18,2},{3,19},{19,3},{4,20},{20... | collective-permute-start | bytes 1572872 | tf_op jit(solution)/shard_map/ppermute | solution.py:822
  194.3 22.1 %collective-permute-start.18 = (bf16[192,512]{1,0:T(8,128)(2,1)}, bf16[192,512]{1,0:T(8,128)(2,1)}, u32[]{:S(2)}, u32[]{:S(2)}) collective-permute-start(bf16[192,512]{1,0:T(8,128)(2,1)} %get-tuple-element.148), channel_id=1, source_target_pairs={{0,4},{1,5},{2,6},{3,7},{4,0},{5,1},{6,2},{7,3},{8,12},{9,13},{10,... | collective-permute-start | bytes 589832 | tf_op jit(solution)/shard_map/ppermute | solution.py:818
  195.6 20.8 %collective-permute-start.19 = (bf16[192,512]{1,0:T(8,128)(2,1)}, bf16[192,512]{1,0:T(8,128)(2,1)}, u32[]{:S(2)}, u32[]{:S(2)}) collective-permute-start(bf16[192,512]{1,0:T(8,128)(2,1)} %get-tuple-element.149), channel_id=1, source_target_pairs={{0,8},{1,9},{2,10},{3,11},{4,12},{5,13},{6,14},{7,15},{8,0},{9,1},... | collective-permute-start | bytes 589832 | tf_op jit(solution)/shard_map/ppermute | solution.py:818
  195.7 27.4 %collective-permute-start.20 = (bf16[192,512]{1,0:T(8,128)(2,1)S(1)}, bf16[192,512]{1,0:T(8,128)(2,1)}, u32[]{:S(2)}, u32[]{:S(2)}) collective-permute-start(bf16[192,512]{1,0:T(8,128)(2,1)S(1)} %get-tuple-element.150), channel_id=1, source_target_pairs={{0,12},{1,13},{2,14},{3,15},{4,8},{5,9},{6,10},{7,11},{8,4},{9,5},... | collective-permute-start | bytes 589832 | tf_op jit(solution)/shard_map/ppermute | solution.py:818
  223.1 12.5 %collective-permute-start.22 = (bf16[896,512]{1,0:T(8,128)(2,1)}, bf16[896,512]{1,0:T(8,128)(2,1)S(1)}, u32[]{:S(2)}, u32[]{:S(2)}) collective-permute-start(bf16[896,512]{1,0:T(8,128)(2,1)} %get-tuple-element.156), channel_id=1, source_target_pairs={{0,1},{1,0},{2,3},{3,2},{4,5},{5,4},{6,7},{7,6},{8,9},{9,8},{10,11... | collective-permute-start | bytes 2752520 | tf_op jit(solution)/shard_map/ppermute | solution.py:818
  228.2 38.2 %collective-permute-start.27 = (bf16[1536,512]{1,0:T(8,128)(2,1)}, bf16[1536,512]{1,0:T(8,128)(2,1)}, u32[]{:S(2)}, u32[]{:S(2)}) collective-permute-start(bf16[1536,512]{1,0:T(8,128)(2,1)} %broadcast_select_fusion.2), channel_id=1, source_target_pairs={{0,16},{16,0},{1,17},{17,1},{2,18},{18,2},{3,19},{19,3},{4,20},{20... | collective-permute-start | bytes 4718600 | tf_op jit(solution)/shard_map/ppermute | solution.py:822
  237.7 14.2 %collective-permute-start.26 = (bf16[544,512]{1,0:T(8,128)(2,1)}, bf16[544,512]{1,0:T(8,128)(2,1)}, u32[]{:S(2)}, u32[]{:S(2)}) collective-permute-start(bf16[544,512]{1,0:T(8,128)(2,1)} %pad_maximum_fusion.1), channel_id=1, source_target_pairs={{0,2},{1,3},{2,0},{3,1},{4,6},{5,7},{6,4},{7,5},{8,10},{9,11},{10,... | collective-permute-start | bytes 1671176 | tf_op jit(solution)/shard_map/ppermute | solution.py:818
  237.7 17.9 %collective-permute-start.23 = (bf16[192,512]{1,0:T(8,128)(2,1)}, bf16[192,512]{1,0:T(8,128)(2,1)S(1)}, u32[]{:S(2)}, u32[]{:S(2)}) collective-permute-start(bf16[192,512]{1,0:T(8,128)(2,1)} %get-tuple-element.157), channel_id=1, source_target_pairs={{0,4},{1,5},{2,6},{3,7},{4,0},{5,1},{6,2},{7,3},{8,12},{9,13},{10,... | collective-permute-start | bytes 589832 | tf_op jit(solution)/shard_map/ppermute | solution.py:818
  237.7 17.9 %collective-permute-start.24 = (bf16[192,512]{1,0:T(8,128)(2,1)}, bf16[192,512]{1,0:T(8,128)(2,1)S(1)}, u32[]{:S(2)}, u32[]{:S(2)}) collective-permute-start(bf16[192,512]{1,0:T(8,128)(2,1)} %get-tuple-element.158), channel_id=1, source_target_pairs={{0,8},{1,9},{2,10},{3,11},{4,12},{5,13},{6,14},{7,15},{8,0},{9,1},... | collective-permute-start | bytes 589832 | tf_op jit(solution)/shard_map/ppermute | solution.py:818
  239.0 26.1 %collective-permute-start.25 = (bf16[192,512]{1,0:T(8,128)(2,1)}, bf16[192,512]{1,0:T(8,128)(2,1)S(1)}, u32[]{:S(2)}, u32[]{:S(2)}) collective-permute-start(bf16[192,512]{1,0:T(8,128)(2,1)} %get-tuple-element.159), channel_id=1, source_target_pairs={{0,12},{1,13},{2,14},{3,15},{4,8},{5,9},{6,10},{7,11},{8,4},{9,5},... | collective-permute-start | bytes 589832 | tf_op jit(solution)/shard_map/ppermute | solution.py:818
  268.4 8.0 %collective-permute-start.32 = (bf16[288,512]{1,0:T(8,128)(2,1)S(1)}, bf16[288,512]{1,0:T(8,128)(2,1)S(1)}, u32[]{:S(2)}, u32[]{:S(2)}) collective-permute-start(bf16[288,512]{1,0:T(8,128)(2,1)S(1)} %broadcast_select_fusion.5), channel_id=1, source_target_pairs={{0,16},{16,0},{1,17},{17,1},{2,18},{18,2},{3,19},{19,3},{4,20},{20... | collective-permute-start | bytes 884744 | tf_op jit(solution)/shard_map/ppermute | solution.py:822
  279.0 12.8 %collective-permute-start.28 = (bf16[112,512]{1,0:T(8,128)(2,1)}, bf16[112,512]{1,0:T(8,128)(2,1)S(1)}, u32[]{:S(2)}, u32[]{:S(2)}) collective-permute-start(bf16[112,512]{1,0:T(8,128)(2,1)} %get-tuple-element.199), channel_id=1, source_target_pairs={{0,4},{1,5},{2,6},{3,7},{4,0},{5,1},{6,2},{7,3},{8,12},{9,13},{10,... | collective-permute-start | bytes 344072 | tf_op jit(solution)/shard_map/ppermute | solution.py:818
  279.3 12.4 %collective-permute-start.29 = (bf16[112,512]{1,0:T(8,128)(2,1)}, bf16[112,512]{1,0:T(8,128)(2,1)S(1)}, u32[]{:S(2)}, u32[]{:S(2)}) collective-permute-start(bf16[112,512]{1,0:T(8,128)(2,1)} %get-tuple-element.197), channel_id=1, source_target_pairs={{0,8},{1,9},{2,10},{3,11},{4,12},{5,13},{6,14},{7,15},{8,0},{9,1},... | collective-permute-start | bytes 344072 | tf_op jit(solution)/shard_map/ppermute | solution.py:818
  297.9 7.2 %collective-permute-start.33 = (bf16[192,512]{1,0:T(8,128)(2,1)S(1)}, bf16[192,512]{1,0:T(8,128)(2,1)S(1)}, u32[]{:S(2)}, u32[]{:S(2)}) collective-permute-start(bf16[192,512]{1,0:T(8,128)(2,1)S(1)} %pad_maximum_fusion.4), channel_id=1, source_target_pairs={{0,4},{1,5},{2,6},{3,7},{4,0},{5,1},{6,2},{7,3},{8,12},{9,13},{10,... | collective-permute-start | bytes 589832 | tf_op jit(solution)/shard_map/ppermute | solution.py:818
  301.3 6.9 %collective-permute-start.34 = (bf16[192,512]{1,0:T(8,128)(2,1)S(1)}, bf16[192,512]{1,0:T(8,128)(2,1)S(1)}, u32[]{:S(2)}, u32[]{:S(2)}) collective-permute-start(bf16[192,512]{1,0:T(8,128)(2,1)S(1)} %pad_maximum_fusion.4), channel_id=1, source_target_pairs={{0,8},{1,9},{2,10},{3,11},{4,12},{5,13},{6,14},{7,15},{8,0},{9,1},... | collective-permute-start | bytes 589832 | tf_op jit(solution)/shard_map/ppermute | solution.py:818
  301.3 29.8 %collective-permute-start.35 = (bf16[192,512]{1,0:T(8,128)(2,1)S(1)}, bf16[192,512]{1,0:T(8,128)(2,1)S(1)}, u32[]{:S(2)}, u32[]{:S(2)}) collective-permute-start(bf16[192,512]{1,0:T(8,128)(2,1)S(1)} %pad_maximum_fusion.4), channel_id=1, source_target_pairs={{0,12},{1,13},{2,14},{3,15},{4,8},{5,9},{6,10},{7,11},{8,4},{9,5},... | collective-permute-start | bytes 589832 | tf_op jit(solution)/shard_map/ppermute | solution.py:818
  331.4 16.4 %collective-permute-start.37 = (bf16[768,512]{1,0:T(8,128)(2,1)S(1)}, bf16[768,512]{1,0:T(8,128)(2,1)S(1)}, u32[]{:S(2)}, u32[]{:S(2)}) collective-permute-start(bf16[768,512]{1,0:T(8,128)(2,1)S(1)} %pad_maximum_fusion.refs_0_), channel_id=1, source_target_pairs={{0,2},{1,3},{2,0},{3,1},{4,6},{5,7},{6,4},{7,5},{8,10},{9,11},{10,... | collective-permute-start | bytes 2359304 | tf_op jit(solution)/shard_map/ppermute | solution.py:818
  335.9 22.8 %collective-permute-start.36 = (bf16[768,512]{1,0:T(8,128)(2,1)S(1)}, bf16[768,512]{1,0:T(8,128)(2,1)S(1)}, u32[]{:S(2)}, u32[]{:S(2)}) collective-permute-start(bf16[768,512]{1,0:T(8,128)(2,1)S(1)} %pad_maximum_fusion.refs_0_), channel_id=1, source_target_pairs={{0,1},{1,0},{2,3},{3,2},{4,5},{5,4},{6,7},{7,6},{8,9},{9,8},{10,11... | collective-permute-start | bytes 2359304 | tf_op jit(solution)/shard_map/ppermute | solution.py:818
  347.8 10.9 %collective-permute-start.38 = (bf16[768,512]{1,0:T(8,128)(2,1)S(1)}, bf16[768,512]{1,0:T(8,128)(2,1)S(1)}, u32[]{:S(2)}, u32[]{:S(2)}) collective-permute-start(bf16[768,512]{1,0:T(8,128)(2,1)S(1)} %collective-permute-done.37.refs_2_), channel_id=1, source_target_pairs={{0,1},{1,0},{2,3},{3,2},{4,5},{5,4},{6,7},{7,6},{8,9},{9,8},{10,11... | collective-permute-start | bytes 2359304 | tf_op jit(solution)/shard_map/ppermute | solution.py:818
  (43 other events, 294.5 us)
Sparse Core Ops, SparseCore 0:
  147.8 111.9 reduce-scatter.1
  279.1 53.8 all-gather.1

commit v4 on v3

--- a/solution.py
+++ b/solution.py
@@ -321,7 +321,7 @@
 
 
 DOWN_ROWS, OUT_ROWS, QKV_ROWS, GAIN_ROWS = FF // 16, D // 16, 3 * D // 16, 16
-UP_A = FF // 4
+UP_A = FF // 2
 UP_B = FF - UP_A
 PART_A, PART_B = DOWN_ROWS + UP_A // 16 + OUT_ROWS, UP_B // 16
 PART_C = QKV_ROWS + GAIN_ROWS
@@ -754,24 +754,66 @@
     )
 
 
-def finish_whole_kernel(held, *outs, widths, flips):
+def combine_kernel(meta_ref, *refs, count, cuts):
+    values, outs = refs[:count], refs[count:]
+    x, z = (meta_ref[7] >> 1) & 1, meta_ref[8]
+    for out, (start, kind, k) in zip(outs, cuts):
+        rows = out.shape[0]
+        spot = {"x": x ^ k, "z": z ^ k, "all": 0}[kind]
+        part = pl.ds(pl.multiple_of(start + spot * rows, 16), rows)
+        total = values[0][part].astype(F32)
+        for value in values[1:]:
+            total = total + value[part].astype(F32)
+        out[...] = total.astype(BF)
+
+
+def combine(meta, values, cuts):
+    return pl.pallas_call(
+        functools.partial(
+            combine_kernel, count=len(values), cuts=tuple((c[0],) + c[2:] for c in cuts)
+        ),
+        out_shape=tuple(sds((c[1], D), BF) for c in cuts),
+        grid_spec=pltpu.PrefetchScalarGridSpec(
+            num_scalar_prefetch=1, grid=(1,),
+            in_specs=[part_spec(v.shape, (0, 0)) for v in values],
+            out_specs=[part_spec((c[1], D), (0, 0)) for c in cuts],
+        ),
+        cost_estimate=pl.CostEstimate(flops=10**10, bytes_accessed=10**7, transcendentals=0),
+        compiler_params=pltpu.CompilerParams(vmem_limit_bytes=VMEM_LIMIT // 4),
+    )(meta, *values)
+
+
+def by_x(start, rows):
+    return [(start, rows, "x", 0), (start, rows, "x", 1)]
+
+
+def by_z(start, rows):
+    return [(start, rows, "z", k) for k in range(4)]
+
+
+def finish_whole_kernel(held, _, up_ref, down_ref, out_ref, *, widths):
     total = sum(widths)
-    for i, (width, flip) in enumerate(zip(widths, flips)):
-        start = sum(widths[:i])
-        places = [(s & 3) * 4 + ((s >> 2) & 1) * 2 + (s >> 3) for s in range(16)]
-        value = jnp.concatenate(
-            [held[pl.ds(p * total + start, width)] for p in places], axis=0
+    places = [(s & 3) * 4 + ((s >> 2) & 1) * 2 + (s >> 3) for s in range(16)]
+
+    def take(i):
+        start = (widths[1], 0, widths[1] + widths[0])[i]
+        return jnp.concatenate(
+            [held[pl.ds(p * total + start, widths[i])] for p in places], axis=0
         )
-        outs[i][...] = (value.T if flip else value).astype(F32)
-
-
-def finish_whole(value, widths, flips, shapes, specs):
+
+    up_ref[...] = take(0).T.astype(F32)
+    down_ref[...] = take(1).astype(F32)
+    out_ref[...] = take(2).astype(F32)
+
+
+def finish_whole(value, widths, shapes, specs, up):
     return pl.pallas_call(
-        functools.partial(finish_whole_kernel, widths=widths, flips=flips),
+        functools.partial(finish_whole_kernel, widths=widths),
         out_shape=tuple(sds(shape, F32) for shape in shapes),
-        grid=(1,), in_specs=[part_spec(value.shape, (0, 0))], out_specs=specs,
+        grid=(1,), in_specs=[part_spec(value.shape, (0, 0)), ANY], out_specs=specs,
+        input_output_aliases={1: 0},
         compiler_params=pltpu.CompilerParams(vmem_limit_bytes=VMEM_LIMIT),
-    )(value)
+    )(value, up)
 
 
 def finish_kernel(meta_ref, *refs, widths, targets, extra):
@@ -937,6 +979,7 @@
         lax.dynamic_index_in_dim(span_counts, section, 0, keepdims=False),
         lax.dynamic_index_in_dim(tail_lens, section, 0, keepdims=False),
         section.astype(jnp.int32)[None], place.astype(jnp.int32)[None],
+        ((lax.axis_index("dp") >> 2) & 3).astype(jnp.int32)[None],
     ])
     own = (w_qkv[0], w_out[0], w_up[0], w_down[0])
 
@@ -945,20 +988,17 @@
         return lax.dynamic_slice_in_dim(weight, spot * rows, rows, 0)
 
     own_gains = jnp.concatenate([ln1_gain, ln2_gain], axis=0)
+    attn = swap_section(
+        jnp.concatenate([part(own[0], place, 4), part(own[1], place, 4)], axis=1)
+    )
     other_gains = swap_section(own_gains)
-    attn = [
-        part(own[0][:, :2 * D], place, 4),
-        jnp.concatenate([part(own[0][:, 2 * D:], place, 4), part(own[1], place, 4)], axis=1),
-    ]
-    attn = [swap_section(value) for value in attn]
-    late = part(own[2], place, 4), part(own[3], place & 1, 2)
-    attn[1], other_gains, late = tie(attn[1], other_gains, late)
-    up, down = swap_section(late[0]), swap_section(late[1])
+    attn, other_gains = tie(attn, other_gains)
     gains = [jnp.where(first, own_gains, other_gains), jnp.where(first, other_gains, own_gains)]
-    attn_x = [swap_xor(value, 2) for value in attn]
-    front, rest = [(v, swap_xor(v, 1), x, swap_xor(x, 1)) for v, x in zip(attn, attn_x)]
-    wqkv = Weight(own[0], (front, 0, 0, 2 * D), (rest, 0, 2 * D, D))
-    wout = Weight(own[1], (rest, D, 0, D))
+    attn_x = swap_xor(attn, 2)
+    attn = (attn, swap_xor(attn, 1), attn_x, swap_xor(attn_x, 1))
+    wqkv, wout = Weight(own[0], (attn, 0, 0, None)), Weight(own[1], (attn, 3 * D, 0, None))
+    up = swap_section(part(own[2], place, 4))
+    down = swap_section(part(own[3], place & 1, 2))
     up_x, up_c = swap_xor(up, 2), swap_xor(up, 1)
 
     keep0, hidden, second = forward_attn(meta, tokens, gains[0], wqkv, wout, 0)
@@ -977,8 +1017,10 @@
     xh1, r1, qkv, krow, vrow, lse, att, xh2, r2, ks, vs = keep0
     back = mlp_back(meta, ig1, act0, gp0, xh2, r2, att, gains[0], wdown, wup, wout, 0)
     (send, kept, gln2, gh, gatt), acts_a, act_out0, act_out1 = tie(back, acts_a, act_out0, act_out1)
-    mlp0 = added(kept, swap_xor(send, 1))
-    a0, b0 = halves(mlp0[:8 * PART_A], 1), quarters(mlp0[8 * PART_A:], 2)
+    mlp0 = combine(
+        meta, (kept, swap_xor(send, 1)), by_x(0, 4 * PART_A) + by_z(8 * PART_A, 2 * PART_B)
+    )
+    a0, b0 = mlp0[:2], mlp0[2:]
     gh, a0, b0 = tie(gh, a0, b0)
     acts_b = exchange(act_out0[cut:], act_out1[cut:])
     a0_x, b0_z = swap_xor(a0[1], 2), swap_quarters(b0, 2)
@@ -987,12 +1029,11 @@
     )
     (ig0, send, kept), a0_x, b0_z, acts_b = tie(back, a0_x, b0_z, acts_b)
     acts_in = jnp.concatenate([acts_a, acts_b], axis=0)
-    grads_in = exchange(ig0, ig1)
     c0 = swap_xor(send, 1)
-    a0 = quarters(added(a0[0], a0_x), 2)
+    a0 = [added(*pair) for pair in zip(quarters(a0[0], 2), quarters(a0_x, 2))]
     a0, c0 = tie(a0, c0)
     a0_z = swap_quarters(a0, 2)
-    c0 = halves(added(kept, c0), 1)
+    c0 = combine(meta, (kept, c0), by_x(0, 4 * PART_C))
     b0 = halves(added(b0[0], *b0_z), 1)
     bc0_x = swap_xor(jnp.concatenate([b0[1], c0[1]], axis=0), 2)
 
@@ -1002,14 +1043,15 @@
     b0 = added(b0[0], bc0_x[:PART_B])
     c0 = quarters(added(c0[0], bc0_x[PART_B:]), 2)
     c0_z = swap_quarters(c0, 2)
-    a0_z, b0, c0_1, grads_in = tie(a0_z, b0, c0[1], grads_in)
-    a0 = added(a0[0], *a0_z)
+    a0_z, b0, c0_1 = tie(a0_z, b0, c0[1])
+    (a0,) = combine(meta, (a0[0], *a0_z), [(0, PART_A, "all", 0)])
     spots = (0, PART_A, PART_A + PART_B, PART_A + PART_B + QKV_ROWS)
     a1, b1, c1, gains1 = [sums1[i:j] for i, j in zip(spots, spots[1:] + (sums1.shape[0],))]
     ab = own_sum(
         jnp.concatenate([reduce_rest(a0), reduce_rest(b0)], axis=0),
         jnp.concatenate([reduce_rest(a1), reduce_rest(b1)], axis=0),
     )
+    ab, c0_z = tie(ab, c0_z)
     a_rows = ab.shape[0] * PART_A // (PART_A + PART_B)
     a_full = lax.all_gather(
         gather_rest(ab[:a_rows]), "dp", axis=0, axis_index_groups=low_groups(), tiled=True
@@ -1019,21 +1061,23 @@
         jnp.concatenate([reduce_rest(c0[:QKV_ROWS]), sum_rest(c0[QKV_ROWS:])], axis=0),
         jnp.concatenate([reduce_rest(c1), sum_rest(gains1)], axis=0),
     )
+    c_own, ig0 = tie(c_own, ig0)
+    grads_in = exchange(ig0, ig1)
     lns = c_own[-GAIN_ROWS:][:2].astype(F32)
     bc_own = jnp.concatenate([gather_rest(ab[a_rows:]), gather_rest(c_own[:-GAIN_ROWS])], axis=0)
     bc_pieces = spread_pieces(gather_quad(bc_own, 2))
-    grad_down, grad_up, grad_out = finish_whole(
-        a_full, (DOWN_ROWS, UP_A // 16, OUT_ROWS), (False, True, False),
-        [(FF, D), (D, FF), (D, D)],
-        [
-            part_spec((FF, D), (0, 0)), part_spec((D, UP_A), (0, UP_B // UP_A)),
-            part_spec((D, D), (0, 0)),
-        ],
-    )
     grad_up, grad_qkv = finish(
         meta, bc_pieces, (UP_B // 16, QKV_ROWS), (True, True), [(D, FF), (D, 3 * D)],
         [part_spec((D, UP_B), (0, 0)), part_spec((D, 3 * D), (0, 0))],
-        (grad_up,), {5: 0},
+    )
+    grad_up, a_full = tie(grad_up, a_full)
+    grad_up, grad_down, grad_out = finish_whole(
+        a_full, (UP_A // 16, DOWN_ROWS, OUT_ROWS), [(D, FF), (FF, D), (D, D)],
+        [
+            part_spec((D, UP_A), (0, UP_B // UP_A)), part_spec((FF, D), (0, 0)),
+            part_spec((D, D), (0, 0)),
+        ],
+        grad_up,
     )
 
     def assemble(value0, value1, got):

time: 374 us -> 352 us (0.941)
  the two profiles are of different devices: /device:TPU:17 before, /device:TPU:0 now
where the time goes in v4:
time: 352 us; the launch traced here: 347 us
  Pallas kernels  158 us (45%)
  waiting for transfers between devices  108 us (31%)
  starting transfers between devices  36.5 us (10%)
  between operations  14.9 us (4%)
  local copies, waits for them, and re-layouts  14.8 us (4%)
  other arithmetic  13.9 us (4%)
    pallas_call x5, Pallas kernels, call(): pl.pallas_call(kernel, out_shape=tuple(outs), grid_spec=pltpu.PrefetchSca...  145 us
    ppermute x26, waiting for transfers between devices, swap_xor(): return lax.ppermute(value, 'dp', [(i, i ^ mask) for i in range(size)])  81.6 us
    ppermute x26, starting transfers between devices, swap_xor(): return lax.ppermute(value, 'dp', [(i, i ^ mask) for i in range(size)])  25.4 us
    ppermute x9, waiting for transfers between devices, swap_section(): return lax.ppermute(value, 'section', [(0, 1), (1, 0)])  16.5 us
    ppermute x9, starting transfers between devices, swap_section(): return lax.ppermute(value, 'section', [(0, 1), (1, 0)])  11 us
  transfers between devices with their start and end apart: 37, of which 17 were waited for; matrix products, arithmetic and copies ran while one was open for 5% of the time, Pallas kernels for 21%

profile of v4, /device:TPU:0, one launch (start us, length us, event | category | flops | bytes accessed | tf_op | source)
XLA Modules:
  0.0 346.8 jit_solution(1664822698047759744)
XLA Ops:
  9.4 3.0 collective-permute-start
  12.6 1.9 dynamic-slice_bitcast_fusion.1
  14.5 2.0 collective-permute-start.5
  16.5 8.8 %collective-permute-done.1 = f32[2,512]{1,0:T(2,128)S(1)} collective-permute-done((f32[2,512]{1,0:T(2,128)S(1)}, f32[2,512]{1,0:T(2,128)S(1)}, u32[]{:S(2)}, u32[]{:S(2)}) %collective-permute-start.1) | collective-permute-done | bytes 4128 | tf_op jit(solution)/shard_map/ppermute | solution.py:864
  25.3 2.0 collective-permute-start.3
  29.9 7.7 %collective-permute-done.3.refs_3_.refs_8_.refs_11_ = bf16[128,2048]{1,0:T(8,128)(2,1)S(1)} collective-permute-done((bf16[128,2048]{1,0:T(8,128)(2,1)S(1)}, bf16[128,2048]{1,0:T(8,128)(2,1)S(1)}, u32[]{:S(2)}, u32[]{:S(2)}) %collective-permute-start.3) | collective-permute-done | bytes 524320 | tf_op jit(solution)/shard_map/ppermute | solution.py:860
  41.5 16.4 %shard_map.161 = (bf16[512,1536]{1,0:T(8,128)(2,1)}, f32[1,1536]{1,0:T(1,128)}, bf16[1536,1536]{1,0:T(8,128)(2,1)}, bf16[1536,512]{1,0:T(8,128)(2,1)}, bf16[1536...) custom-call(s32[9]{0:T(128)} %concatenate.37.meta_ref, ...), custom_call_target="tpu_custom_call" | custom-call | tf_op jit(solution)/shard_map/pallas_call | solution.py:606
  58.7 3.1 collective-permute-done.9.refs_4_.refs_14_.refs_7_
  62.9 15.8 %shard_map.162 = (bf16[1536,512]{1,0:T(8,128)(2,1)}, bf16[2048,1536]{1,0:T(8,128)(2,1)}, bf16[2048,1536]{1,0:T(8,128)(2,1)}) custom-call(s32[9]{0:T(128)} %concatenate.37.meta_ref, f32[512,1536]{1,0:T(8,128)} %get-tuple-element.121.hid_ref, bf16[512,1536]{1,0:T(8,128)(2,1)} %get-tuple-element.122.sec_ref, bf16[512,2048]{1,0:T(8,128)(2,1)} %bitcast.31, ...), custom_call_target="tpu_custom_call" | custom-call | tf_op jit(solution)/shard_map/pallas_call | solution.py:606
  78.8 64.2 %shard_map.163 = (bf16[1536,512]{1,0:T(8,128)(2,1)}, bf16[1536,512]{1,0:T(8,128)(2,1)}, bf16[16,400,512]{2,1,0:T(8,128)(2,1)}) custom-call(s32[9]{0:T(128)} %concatenate.37.meta_ref, bf16[1536,512]{1,0:T(8,128)(2,1)} %get-tuple-element.139.x_ref, bf16[3072,512]{1,0:T(8,128)(2,1)} %cot_ref.1, f32[2,512]{1,0:T(2,128)} %get-tuple-element.220.gains_ref, ...), custom_call_target="tpu_custom_call" | custom-call | tf_op jit(solution)/shard_map/pallas_call | solution.py:606
  147.2 29.4 %shard_map.164 = (bf16[2304,512]{1,0:T(8,128)(2,1)}, bf16[2304,512]{1,0:T(8,128)(2,1)}, f32[1,512]{1,0:T(1,128)}, f32[512,1536]{1,0:T(8,128)}, bf16[512,1536]{1,0:T(8,128)(2,1)}) custom-call(s32[9]{0:T(128)} %concatenate.37.meta_ref, bf16[1536,512]{1,0:T(8,128)(2,1)} %get-tuple-element.127.seed_ref, bf16[2048,1536]{1,0:T(8,128)(2,1)} %get-tuple-element.128.act_ref, ...), custom_call_target="tpu_custom_call" | custom-call | tf_op jit(solution)/shard_map/pallas_call | solution.py:606
  177.6 3.9 %collective-permute-done.12.refs_1_ = bf16[2304,512]{1,0:T(8,128)(2,1)S(1)} collective-permute-done((bf16[2304,512]{1,0:T(8,128)(2,1)}, bf16[2304,512]{1,0:T(8,128)(2,1)S(1)}, u32[]{:S(2)}, u32[]{:S(2)}) %collective-permute-start.12) | collective-permute-done | bytes 2359328 | tf_op jit(solution)/shard_map/ppermute | solution.py:860
  188.6 2.6 collective-permute-start.15
  191.4 19.5 %shard_map.166 = (bf16[1536,512]{1,0:T(8,128)(2,1)}, bf16[896,512]{1,0:T(8,128)(2,1)}, bf16[896,512]{1,0:T(8,128)(2,1)}) custom-call(s32[9]{0:T(128)} %concatenate.37.meta_ref, f32[512,1536]{1,0:T(8,128)} %get-tuple-element.150.gh_ref, bf16[512,1536]{1,0:T(8,128)(2,1)} %get-tuple-element.151.gatt_ref, bf16[512,1536]{1,0:T(8,128)(2,1)} %get-tuple-element.152.xh1_ref, ...), custom_call_target="tpu_custom_call" | custom-call | tf_op jit(solution)/shard_map/pallas_call | solution.py:606
  210.9 3.3 collective-permute-done.13
  219.9 2.4 collective-permute-start.21
  222.5 13.6 %collective-permute-done.19 = bf16[512,512]{1,0:T(8,128)(2,1)S(1)} collective-permute-done((bf16[512,512]{1,0:T(8,128)(2,1)S(1)}, bf16[512,512]{1,0:T(8,128)(2,1)S(1)}, u32[]{:S(2)}, u32[]{:S(2)}) %collective-permute-start.19) | collective-permute-done | bytes 524320 | tf_op jit(solution)/shard_map/ppermute | solution.py:860
  237.0 11.5 %collective-permute-done.21.refs_2_ = bf16[224,512]{1,0:T(8,128)(2,1)S(1)} collective-permute-done((bf16[224,512]{1,0:T(8,128)(2,1)S(1)}, bf16[224,512]{1,0:T(8,128)(2,1)S(1)}, u32[]{:S(2)}, u32[]{:S(2)}) %collective-permute-start.21) | collective-permute-done | bytes 229408 | tf_op jit(solution)/shard_map/ppermute | solution.py:860
  249.2 6.5 %reduce-scatter.2.cloned.1.call-done = bf16[400,512]{1,0:T(8,128)(2,1)} async-done(((bf16[6400,512]{1,0:T(8,128)(2,1)}), bf16[400,512]{1,0:T(8,128)(2,1)}) %reduce-scatter.2.cloned.1.call-update) | async-done | bytes 409616 | tf_op jit(solution)/shard_map/reduce_scatter | solution.py:1014
  260.7 1.9 collective-permute-start.26
  262.7 3.2 collective-permute-done.23
  267.0 3.4 collective-permute-done.25
  273.2 4.2 %collective-permute-done.27 = bf16[112,512]{1,0:T(8,128)(2,1)S(1)} collective-permute-done((bf16[112,512]{1,0:T(8,128)(2,1)S(1)}, bf16[112,512]{1,0:T(8,128)(2,1)S(1)}, u32[]{:S(2)}, u32[]{:S(2)}) %collective-permute-start.27) | collective-permute-done | bytes 114720 | tf_op jit(solution)/shard_map/ppermute | solution.py:864
  277.5 1.9 collective-permute-start.29
  282.7 7.6 %collective-permute-done.29 = bf16[160,512]{1,0:T(8,128)(2,1)S(1)} collective-permute-done((bf16[160,512]{1,0:T(8,128)(2,1)S(1)}, bf16[160,512]{1,0:T(8,128)(2,1)S(1)}, u32[]{:S(2)}, u32[]{:S(2)}) %collective-permute-start.29) | collective-permute-done | bytes 163872 | tf_op jit(solution)/shard_map/ppermute | solution.py:860
  290.3 8.5 %collective-permute-done.30 = bf16[160,512]{1,0:T(8,128)(2,1)S(1)} collective-permute-done((bf16[160,512]{1,0:T(8,128)(2,1)S(1)}, bf16[160,512]{1,0:T(8,128)(2,1)S(1)}, u32[]{:S(2)}, u32[]{:S(2)}) %collective-permute-start.30) | collective-permute-done | bytes 163872 | tf_op jit(solution)/shard_map/ppermute | solution.py:860
  301.0 17.5 %collective-permute-done.33.refs_2_ = bf16[640,512]{1,0:T(8,128)(2,1)S(1)} collective-permute-done((bf16[640,512]{1,0:T(8,128)(2,1)S(1)}, bf16[640,512]{1,0:T(8,128)(2,1)S(1)}, u32[]{:S(2)}, u32[]{:S(2)}) %collective-permute-start.33) | collective-permute-done | bytes 655392 | tf_op jit(solution)/shard_map/ppermute | solution.py:860
  318.6 1.9 maximum_bitcast_fusion
  321.9 5.1 %shard_map.169 = (f32[512,2048]{1,0:T(8,128)}, f32[512,1536]{1,0:T(8,128)}) custom-call(s32[9]{0:T(128)} %concatenate.37.meta_ref, bf16[640,512]{1,0:T(8,128)(2,1)} %copy-done.17, bf16[640,512]{1,0:T(8,128)(2,1)} %copy-done.22, bf16[640,512]{1,0:T(8,128)(2,1)} %copy-done.21, bf16[640,512]{1,0:T(8,128)(2,1)} %collective-permute-done.34.refs_3_), custom_call_target="tpu_custom_call" | custom-call | tf_op jit(solution)/shard_map/pallas_call | solution.py:842
  328.6 1.9 maximum_bitcast_fusion.1
  330.5 3.7 %all-gather.2.cloned.1.call-done.held = bf16[3584,512]{1,0:T(8,128)(2,1)} async-done(((bf16[224,512]{1,0:T(8,128)(2,1)}), bf16[3584,512]{1,0:T(8,128)(2,1)}) %all-gather.2.cloned.1.call-update) | async-done | bytes 3670032 | tf_op jit(solution)/shard_map/all_gather | solution.py:1056
  334.2 5.5 %shard_map.170 = (f32[512,2048]{1,0:T(8,128)}, f32[2048,512]{1,0:T(8,128)}, f32[512,512]{1,0:T(8,128)}) custom-call(bf16[3584,512]{1,0:T(8,128)(2,1)} %all-gather.2.cloned.1.call-done.held, f32[512,2048]{1,0:T(8,128)} %get-tuple-element.200._), custom_call_target="tpu_custom_call", output_to_operand_aliasing={{0}: (1, {})} | custom-call | tf_op jit(solution)/shard_map/pallas_call | solution.py:810
  (164 shorter events, 48.1 us)
Async XLA Ops:
  7.2 248.5 %reduce-scatter.2.cloned.1.call-start = ((), (), s32[]{:S(2)}) async-start(), calls=%async_computation.1 | async-start | bytes 6963200 | tf_op jit(solution)/shard_map/reduce_scatter | solution.py:1014
  9.4 15.9 %collective-permute-start = (bf16[128,2048]{1,0:T(8,128)(2,1)S(1)}, bf16[128,2048]{1,0:T(8,128)(2,1)S(1)}, u32[]{:S(2)}, u32[]{:S(2)}) collective-permute-start(bf16[128,2048]{1,0:T(8,128)(2,1)S(1)} %pad_maximum_fusion.1), channel_id=1, source_target_pairs={{0,16},{16,0},{1,17},{17,1},{2,18},{18,2},{3,19},{19,3},{4,20},{20... | collective-permute-start | bytes 1572872 | tf_op jit(solution)/shard_map/ppermute | solution.py:864
  12.5 12.8 %collective-permute-start.1 = (f32[2,512]{1,0:T(2,128)S(1)}, f32[2,512]{1,0:T(2,128)S(1)}, u32[]{:S(2)}, u32[]{:S(2)}) collective-permute-start(f32[2,512]{1,0:T(2,128)S(1)} %pad_maximum_fusion.5), channel_id=1, source_target_pairs={{0,16},{16,0},{1,17},{17,1},{2,18},{18,2},{3,19},{19,3},{4,20},{20... | collective-permute-start | bytes 12296 | tf_op jit(solution)/shard_map/ppermute | solution.py:864
  14.5 23.1 %collective-permute-start.5 = (bf16[128,2048]{1,0:T(8,128)(2,1)}, bf16[128,2048]{1,0:T(8,128)(2,1)}, u32[]{:S(2)}, u32[]{:S(2)}) collective-permute-start(bf16[128,2048]{1,0:T(8,128)(2,1)} %dynamic-slice_bitcast_fusion.1), channel_id=1, source_target_pairs={{0,16},{16,0},{1,17},{17,1},{2,18},{18,2},{3,19},{19,3},{4,20},{20... | collective-permute-start | bytes 1572872 | tf_op jit(solution)/shard_map/ppermute | solution.py:864
  25.3 12.3 %collective-permute-start.3 = (bf16[128,2048]{1,0:T(8,128)(2,1)S(1)}, bf16[128,2048]{1,0:T(8,128)(2,1)S(1)}, u32[]{:S(2)}, u32[]{:S(2)}) collective-permute-start(bf16[128,2048]{1,0:T(8,128)(2,1)S(1)} %collective-permute-done.refs_1_.refs_6_.refs_9_), channel_id=1, source_target_pairs={{0,2},{1,3},{2,0},{3,1},{4,6},{5,7},{6,4},{7,5},{8,10},{9,11},{10,... | collective-permute-start | bytes 1572872 | tf_op jit(solution)/shard_map/ppermute | solution.py:860
  28.4 29.8 %collective-permute-start.8 = (bf16[1024,512]{1,0:T(8,128)(2,1)}, bf16[1024,512]{1,0:T(8,128)(2,1)S(1)}, u32[]{:S(2)}, u32[]{:S(2)}) collective-permute-start(bf16[1024,512]{1,0:T(8,128)(2,1)} %dynamic-slice_bitcast_fusion), channel_id=1, source_target_pairs={{0,16},{16,0},{1,17},{17,1},{2,18},{18,2},{3,19},{19,3},{4,20},{20... | collective-permute-start | bytes 3145736 | tf_op jit(solution)/shard_map/ppermute | solution.py:864
  29.9 10.6 %collective-permute-start.2 = (bf16[128,2048]{1,0:T(8,128)(2,1)S(1)}, bf16[128,2048]{1,0:T(8,128)(2,1)S(1)}, u32[]{:S(2)}, u32[]{:S(2)}) collective-permute-start(bf16[128,2048]{1,0:T(8,128)(2,1)S(1)} %collective-permute-done.refs_1_.refs_6_.refs_9_), channel_id=1, source_target_pairs={{0,1},{1,0},{2,3},{3,2},{4,5},{5,4},{6,7},{7,6},{8,9},{9,8},{10,11... | collective-permute-start | bytes 1572872 | tf_op jit(solution)/shard_map/ppermute | solution.py:860
  37.6 20.3 %collective-permute-start.6 = (bf16[128,2048]{1,0:T(8,128)(2,1)}, bf16[128,2048]{1,0:T(8,128)(2,1)}, u32[]{:S(2)}, u32[]{:S(2)}) collective-permute-start(bf16[128,2048]{1,0:T(8,128)(2,1)} %collective-permute-done.5.refs_1_.refs_11_.refs_4_), channel_id=1, source_target_pairs={{0,2},{1,3},{2,0},{3,1},{4,6},{5,7},{6,4},{7,5},{8,10},{9,11},{10,... | collective-permute-start | bytes 1572872 | tf_op jit(solution)/shard_map/ppermute | solution.py:860
  39.0 18.8 %collective-permute-start.7 = (bf16[128,2048]{1,0:T(8,128)(2,1)}, bf16[128,2048]{1,0:T(8,128)(2,1)}, u32[]{:S(2)}, u32[]{:S(2)}) collective-permute-start(bf16[128,2048]{1,0:T(8,128)(2,1)} %collective-permute-done.5.refs_1_.refs_11_.refs_4_), channel_id=1, source_target_pairs={{0,1},{1,0},{2,3},{3,2},{4,5},{5,4},{6,7},{7,6},{8,9},{9,8},{10,11... | collective-permute-start | bytes 1572872 | tf_op jit(solution)/shard_map/ppermute | solution.py:860
  143.1 191.1 %all-gather.2.cloned.1.call-start = ((), (), s32[]{:S(2)}) async-start(), calls=%async_computation.2 | async-start | bytes 3899392 | tf_op jit(solution)/shard_map/all_gather | solution.py:1056
  145.8 30.8 %collective-permute-start.11 = (bf16[1024,512]{1,0:T(8,128)(2,1)S(1)}, bf16[1024,512]{1,0:T(8,128)(2,1)S(1)}, u32[]{:S(2)}, u32[]{:S(2)}) collective-permute-start(bf16[1024,512]{1,0:T(8,128)(2,1)S(1)} %slice_select_fusion), channel_id=1, source_target_pairs={{0,16},{16,0},{1,17},{17,1},{2,18},{18,2},{3,19},{19,3},{4,20},{20... | collective-permute-start | bytes 3145736 | tf_op jit(solution)/shard_map/ppermute | solution.py:864
  176.6 4.8 %collective-permute-start.12 = (bf16[2304,512]{1,0:T(8,128)(2,1)}, bf16[2304,512]{1,0:T(8,128)(2,1)S(1)}, u32[]{:S(2)}, u32[]{:S(2)}) collective-permute-start(bf16[2304,512]{1,0:T(8,128)(2,1)} %get-tuple-element.143), channel_id=1, source_target_pairs={{0,1},{1,0},{2,3},{3,2},{4,5},{5,4},{6,7},{7,6},{8,9},{9,8},{10,11... | collective-permute-start | bytes 7077896 | tf_op jit(solution)/shard_map/ppermute | solution.py:860
  184.2 30.0 %collective-permute-start.13 = (bf16[896,512]{1,0:T(8,128)(2,1)S(1)}, bf16[896,512]{1,0:T(8,128)(2,1)S(1)}, u32[]{:S(2)}, u32[]{:S(2)}) collective-permute-start(bf16[896,512]{1,0:T(8,128)(2,1)S(1)} %get-tuple-element.164), channel_id=1, source_target_pairs={{0,2},{1,3},{2,0},{3,1},{4,6},{5,7},{6,4},{7,5},{8,10},{9,11},{10,... | collective-permute-start | bytes 2752520 | tf_op jit(solution)/shard_map/ppermute | solution.py:860
  186.8 24.1 %collective-permute-start.17 = (bf16[512,512]{1,0:T(8,128)(2,1)S(1)}, bf16[512,512]{1,0:T(8,128)(2,1)S(1)}, u32[]{:S(2)}, u32[]{:S(2)}) collective-permute-start(bf16[512,512]{1,0:T(8,128)(2,1)S(1)} %slice_select_fusion.1), channel_id=1, source_target_pairs={{0,16},{16,0},{1,17},{17,1},{2,18},{18,2},{3,19},{19,3},{4,20},{20... | collective-permute-start | bytes 1572872 | tf_op jit(solution)/shard_map/ppermute | solution.py:864
  186.9 24.0 %collective-permute-start.14 = (bf16[128,512]{1,0:T(8,128)(2,1)S(1)}, bf16[128,512]{1,0:T(8,128)(2,1)S(1)}, u32[]{:S(2)}, u32[]{:S(2)}) collective-permute-start(bf16[128,512]{1,0:T(8,128)(2,1)S(1)} %get-tuple-element.165), channel_id=1, source_target_pairs={{0,4},{1,5},{2,6},{3,7},{4,0},{5,1},{6,2},{7,3},{8,12},{9,13},{10,... | collective-permute-start | bytes 393224 | tf_op jit(solution)/shard_map/ppermute | solution.py:860
  188.6 22.3 %collective-permute-start.15 = (bf16[128,512]{1,0:T(8,128)(2,1)S(1)}, bf16[128,512]{1,0:T(8,128)(2,1)S(1)}, u32[]{:S(2)}, u32[]{:S(2)}) collective-permute-start(bf16[128,512]{1,0:T(8,128)(2,1)S(1)} %get-tuple-element.166), channel_id=1, source_target_pairs={{0,8},{1,9},{2,10},{3,11},{4,12},{5,13},{6,14},{7,15},{8,0},{9,1},... | collective-permute-start | bytes 393224 | tf_op jit(solution)/shard_map/ppermute | solution.py:860
  191.2 19.7 %collective-permute-start.16 = (bf16[128,512]{1,0:T(8,128)(2,1)S(1)}, bf16[128,512]{1,0:T(8,128)(2,1)S(1)}, u32[]{:S(2)}, u32[]{:S(2)}) collective-permute-start(bf16[128,512]{1,0:T(8,128)(2,1)S(1)} %get-tuple-element.167), channel_id=1, source_target_pairs={{0,12},{1,13},{2,14},{3,15},{4,8},{5,9},{6,10},{7,11},{8,4},{9,5},... | collective-permute-start | bytes 393224 | tf_op jit(solution)/shard_map/ppermute | solution.py:860
  217.8 18.4 %collective-permute-start.19 = (bf16[512,512]{1,0:T(8,128)(2,1)S(1)}, bf16[512,512]{1,0:T(8,128)(2,1)S(1)}, u32[]{:S(2)}, u32[]{:S(2)}) collective-permute-start(bf16[512,512]{1,0:T(8,128)(2,1)S(1)} %pad_maximum_fusion.2), channel_id=1, source_target_pairs={{0,2},{1,3},{2,0},{3,1},{4,6},{5,7},{6,4},{7,5},{8,10},{9,11},{10,... | collective-permute-start | bytes 1572872 | tf_op jit(solution)/shard_map/ppermute | solution.py:860
  218.1 18.9 %collective-permute-start.20 = (bf16[224,512]{1,0:T(8,128)(2,1)S(1)}, bf16[224,512]{1,0:T(8,128)(2,1)S(1)}, u32[]{:S(2)}, u32[]{:S(2)}) collective-permute-start(bf16[224,512]{1,0:T(8,128)(2,1)S(1)} %copy-done.27), channel_id=1, source_target_pairs={{0,4},{1,5},{2,6},{3,7},{4,0},{5,1},{6,2},{7,3},{8,12},{9,13},{10,... | collective-permute-start | bytes 688136 | tf_op jit(solution)/shard_map/ppermute | solution.py:860
  219.9 28.7 %collective-permute-start.21 = (bf16[224,512]{1,0:T(8,128)(2,1)S(1)}, bf16[224,512]{1,0:T(8,128)(2,1)S(1)}, u32[]{:S(2)}, u32[]{:S(2)}) collective-permute-start(bf16[224,512]{1,0:T(8,128)(2,1)S(1)} %copy-done.26), channel_id=1, source_target_pairs={{0,8},{1,9},{2,10},{3,11},{4,12},{5,13},{6,14},{7,15},{8,0},{9,1},... | collective-permute-start | bytes 688136 | tf_op jit(solution)/shard_map/ppermute | solution.py:860
  222.3 26.3 %collective-permute-start.22 = (bf16[224,512]{1,0:T(8,128)(2,1)S(1)}, bf16[224,512]{1,0:T(8,128)(2,1)S(1)}, u32[]{:S(2)}, u32[]{:S(2)}) collective-permute-start(bf16[224,512]{1,0:T(8,128)(2,1)S(1)} %copy-done.25), channel_id=1, source_target_pairs={{0,12},{1,13},{2,14},{3,15},{4,8},{5,9},{6,10},{7,11},{8,4},{9,5},... | collective-permute-start | bytes 688136 | tf_op jit(solution)/shard_map/ppermute | solution.py:860
  256.7 9.1 %collective-permute-start.23 = (bf16[288,512]{1,0:T(8,128)(2,1)S(1)}, bf16[288,512]{1,0:T(8,128)(2,1)S(1)}, u32[]{:S(2)}, u32[]{:S(2)}) collective-permute-start(bf16[288,512]{1,0:T(8,128)(2,1)S(1)} %broadcast_select_fusion.5), channel_id=1, source_target_pairs={{0,16},{16,0},{1,17},{17,1},{2,18},{18,2},{3,19},{19,3},{4,20},{20... | collective-permute-start | bytes 884744 | tf_op jit(solution)/shard_map/ppermute | solution.py:864
  258.3 8.7 %collective-permute-start.24 = (bf16[112,512]{1,0:T(8,128)(2,1)S(1)}, bf16[112,512]{1,0:T(8,128)(2,1)S(1)}, u32[]{:S(2)}, u32[]{:S(2)}) collective-permute-start(bf16[112,512]{1,0:T(8,128)(2,1)S(1)} %copy-done.31), channel_id=1, source_target_pairs={{0,4},{1,5},{2,6},{3,7},{4,0},{5,1},{6,2},{7,3},{8,12},{9,13},{10,... | collective-permute-start | bytes 344072 | tf_op jit(solution)/shard_map/ppermute | solution.py:860
  259.7 10.6 %collective-permute-start.25 = (bf16[112,512]{1,0:T(8,128)(2,1)S(1)}, bf16[112,512]{1,0:T(8,128)(2,1)S(1)}, u32[]{:S(2)}, u32[]{:S(2)}) collective-permute-start(bf16[112,512]{1,0:T(8,128)(2,1)S(1)} %copy-done.30), channel_id=1, source_target_pairs={{0,8},{1,9},{2,10},{3,11},{4,12},{5,13},{6,14},{7,15},{8,0},{9,1},... | collective-permute-start | bytes 344072 | tf_op jit(solution)/shard_map/ppermute | solution.py:860
  260.7 9.6 %collective-permute-start.26 = (bf16[112,512]{1,0:T(8,128)(2,1)S(1)}, bf16[112,512]{1,0:T(8,128)(2,1)}, u32[]{:S(2)}, u32[]{:S(2)}) collective-permute-start(bf16[112,512]{1,0:T(8,128)(2,1)S(1)} %get-tuple-element.217), channel_id=1, source_target_pairs={{0,12},{1,13},{2,14},{3,15},{4,8},{5,9},{6,10},{7,11},{8,4},{9,5},... | collective-permute-start | bytes 344072 | tf_op jit(solution)/shard_map/ppermute | solution.py:860
  272.5 4.9 %collective-permute-start.27 = (bf16[112,512]{1,0:T(8,128)(2,1)S(1)}, bf16[112,512]{1,0:T(8,128)(2,1)S(1)}, u32[]{:S(2)}, u32[]{:S(2)}) collective-permute-start(bf16[112,512]{1,0:T(8,128)(2,1)S(1)} %get-tuple-element.204), channel_id=1, source_target_pairs={{0,16},{16,0},{1,17},{17,1},{2,18},{18,2},{3,19},{19,3},{4,20},{20... | collective-permute-start | bytes 344072 | tf_op jit(solution)/shard_map/ppermute | solution.py:864
  277.5 12.9 %collective-permute-start.29 = (bf16[160,512]{1,0:T(8,128)(2,1)S(1)}, bf16[160,512]{1,0:T(8,128)(2,1)S(1)}, u32[]{:S(2)}, u32[]{:S(2)}) collective-permute-start(bf16[160,512]{1,0:T(8,128)(2,1)S(1)} %pad_maximum_fusion.4), channel_id=1, source_target_pairs={{0,4},{1,5},{2,6},{3,7},{4,0},{5,1},{6,2},{7,3},{8,12},{9,13},{10,... | collective-permute-start | bytes 491528 | tf_op jit(solution)/shard_map/ppermute | solution.py:860
  279.4 19.4 %collective-permute-start.30 = (bf16[160,512]{1,0:T(8,128)(2,1)S(1)}, bf16[160,512]{1,0:T(8,128)(2,1)S(1)}, u32[]{:S(2)}, u32[]{:S(2)}) collective-permute-start(bf16[160,512]{1,0:T(8,128)(2,1)S(1)} %pad_maximum_fusion.4), channel_id=1, source_target_pairs={{0,8},{1,9},{2,10},{3,11},{4,12},{5,13},{6,14},{7,15},{8,0},{9,1},... | collective-permute-start | bytes 491528 | tf_op jit(solution)/shard_map/ppermute | solution.py:860
  280.1 18.7 %collective-permute-start.31 = (bf16[160,512]{1,0:T(8,128)(2,1)S(1)}, bf16[160,512]{1,0:T(8,128)(2,1)S(1)}, u32[]{:S(2)}, u32[]{:S(2)}) collective-permute-start(bf16[160,512]{1,0:T(8,128)(2,1)S(1)} %pad_maximum_fusion.4), channel_id=1, source_target_pairs={{0,12},{1,13},{2,14},{3,15},{4,8},{5,9},{6,10},{7,11},{8,4},{9,5},... | collective-permute-start | bytes 491528 | tf_op jit(solution)/shard_map/ppermute | solution.py:860
  282.1 44.8 %collective-permute-start.28 = (bf16[1536,512]{1,0:T(8,128)(2,1)S(1)}, bf16[1536,512]{1,0:T(8,128)(2,1)}, u32[]{:S(2)}, u32[]{:S(2)}) collective-permute-start(bf16[1536,512]{1,0:T(8,128)(2,1)S(1)} %broadcast_select_fusion.2), channel_id=1, source_target_pairs={{0,16},{16,0},{1,17},{17,1},{2,18},{18,2},{3,19},{19,3},{4,20},{20... | collective-permute-start | bytes 4718600 | tf_op jit(solution)/shard_map/ppermute | solution.py:864
  299.1 19.4 %collective-permute-start.33 = (bf16[640,512]{1,0:T(8,128)(2,1)S(1)}, bf16[640,512]{1,0:T(8,128)(2,1)S(1)}, u32[]{:S(2)}, u32[]{:S(2)}) collective-permute-start(bf16[640,512]{1,0:T(8,128)(2,1)S(1)} %pad_maximum_fusion.refs_0_), channel_id=1, source_target_pairs={{0,2},{1,3},{2,0},{3,1},{4,6},{5,7},{6,4},{7,5},{8,10},{9,11},{10,... | collective-permute-start | bytes 1966088 | tf_op jit(solution)/shard_map/ppermute | solution.py:860
  300.9 20.1 %collective-permute-start.32 = (bf16[640,512]{1,0:T(8,128)(2,1)S(1)}, bf16[640,512]{1,0:T(8,128)(2,1)S(1)}, u32[]{:S(2)}, u32[]{:S(2)}) collective-permute-start(bf16[640,512]{1,0:T(8,128)(2,1)S(1)} %pad_maximum_fusion.refs_0_), channel_id=1, source_target_pairs={{0,1},{1,0},{2,3},{3,2},{4,5},{5,4},{6,7},{7,6},{8,9},{9,8},{10,11... | collective-permute-start | bytes 1966088 | tf_op jit(solution)/shard_map/ppermute | solution.py:860
  (41 other events, 299.3 us)
Sparse Core Ops, SparseCore 0:
  143.2 112.4 reduce-scatter.1
  271.2 62.9 all-gather.1

commit v5 on v4

--- a/solution.py
+++ b/solution.py
@@ -325,6 +325,7 @@
 UP_B = FF - UP_A
 PART_A, PART_B = DOWN_ROWS + UP_A // 16 + OUT_ROWS, UP_B // 16
 PART_C = QKV_ROWS + GAIN_ROWS
+OVERLAPPED = 4 * 10**9
 
 
 def norm_back(grad, gain, xhat, factor, gln_acc):
@@ -510,19 +511,17 @@
 
 def layer_kernel(meta_ref, x_ref, cot_ref, gains_ref, *refs, layer, weights):
     weights, refs = bound(weights, refs)
-    out_ref, gin_ref, sums_ref, *refs = refs
+    out_ref, gin_ref, sums_ref, send_ref, keep_ref, *refs = refs
     keep, refs = refs[:13], refs[13:]
     (xh1, r1, qkv, krow, vrow, lse, att_ref, xh2_ref, r2_ref, ks_ref, vs_ref, gh, gatt) = keep
     act_ref, gp_ref, attf_ref, rows_ref, *refs = refs
     mlp_accs, attn_accs, refs = refs[:4], refs[4:8], refs[8:]
-    held_mlp, held_qkv, *refs = refs
-    targets, sems, copies = refs[:4], refs[4], refs[5]
+    held_mlp, *refs = refs
+    targets, sems, copied = refs[:4], refs[4], refs[5]
     wqkv_ref, wout_ref, wup_ref, wdown_ref = targets
     step = pl.program_id(0)
     wait = weight_waits(meta_ref, layer, weights, targets, sems)
-    mlp_rows = PART_A + PART_B
-    mlp_copy = pltpu.make_async_copy(held_mlp, sums_ref.at[:, pl.ds(0, mlp_rows)], copies.at[0])
-    qkv_copy = pltpu.make_async_copy(held_qkv, sums_ref.at[:, pl.ds(mlp_rows, PART_C)], copies.at[1])
+    copy = pltpu.make_async_copy(held_mlp, sums_ref, copied)
 
     @pl.when(step == 0)
     def _():
@@ -552,7 +551,7 @@
     def _():
         part_a, part_b = mlp_parts(*mlp_accs[:3])
         write_shards(part_a + part_b, held_mlp)
-        mlp_copy.start()
+        copy.start()
 
     @pl.when(step >= N_TILE)
     def _():
@@ -572,10 +571,8 @@
         parts = (
             (attn_accs[0], 0, QKV_ROWS), (gain_rows(attn_accs[1], gln2), 0, GAIN_ROWS)
         )
-        write_shards(parts, held_qkv)
-        qkv_copy.start()
-        mlp_copy.wait()
-        qkv_copy.wait()
+        write_halves(meta_ref, parts, send_ref, keep_ref)
+        copy.wait()
 
 
 ANY = pl.BlockSpec(memory_space=pl.ANY)
@@ -725,12 +722,15 @@
 def whole_layer(meta, x, cotangent, gains, wqkv, wout, wup, wdown, layer):
     weights = (wqkv, wout, wup, wdown)
     tiled = lambda *shape: pltpu.VMEM((N_TILE,) + shape, BF)
-    sums = sds((16, PART_A + PART_B + PART_C, D), BF)
+    sums, half = sds((16, PART_A + PART_B, D), BF), 8 * PART_C
     forth = lambda t: jnp.minimum(t, N_TILE - 1)
     back = lambda t, *_: (jnp.where(t < N_TILE, N_TILE - 1, 2 * N_TILE - 1 - t), 0)
     return call(
         functools.partial(layer_kernel, layer=layer, weights=weights), (2 * N_TILE,),
-        [sds((MB_TOK, D), BF), sds((MB_TOK, D), BF), sums],
+        [
+            sds((MB_TOK, D), BF), sds((MB_TOK, D), BF), sums, sds((half, D), BF),
+            sds((half, D), BF),
+        ],
         [
             pl.BlockSpec((TILE, D), lambda t, *_: (forth(t), 0)),
             pl.BlockSpec((TILE, D), lambda t, m: (m[6] * N_TILE + forth(t), 0)),
@@ -738,7 +738,7 @@
         ] + [ANY] * len(flat(weights)),
         [
             pl.BlockSpec((TILE, D), lambda t, *_: (forth(t), 0)),
-            pl.BlockSpec((TILE, D), back), ANY,
+            pl.BlockSpec((TILE, D), back), ANY, whole((half, D)), whole((half, D)),
         ],
         [
             tiled(D, TILE), pltpu.VMEM((N_TILE, 1, TILE), F32), tiled(3 * D, TILE), tiled(TILE, D),
@@ -748,8 +748,8 @@
             pltpu.VMEM((FF, TILE), BF), pltpu.VMEM((FF, TILE), BF), pltpu.VMEM((D, TILE), BF),
             pltpu.VMEM((3 * D, TILE), F32),
         ] + mlp_scratch() + attn_back_scratch() + [
-            pltpu.VMEM((16, PART_A + PART_B, D), BF), pltpu.VMEM((16, PART_C, D), BF),
-        ] + weight_scratch(*weights) + [pltpu.SemaphoreType.DMA((2,))],
+            pltpu.VMEM((16, PART_A + PART_B, D), BF),
+        ] + weight_scratch(*weights) + [pltpu.SemaphoreType.DMA],
         (meta, x, cotangent, gains, *flat(weights)),
     )
 
@@ -767,7 +767,7 @@
         out[...] = total.astype(BF)
 
 
-def combine(meta, values, cuts):
+def combine(meta, values, cuts, work=0):
     return pl.pallas_call(
         functools.partial(
             combine_kernel, count=len(values), cuts=tuple((c[0],) + c[2:] for c in cuts)
@@ -778,7 +778,7 @@
             in_specs=[part_spec(v.shape, (0, 0)) for v in values],
             out_specs=[part_spec((c[1], D), (0, 0)) for c in cuts],
         ),
-        cost_estimate=pl.CostEstimate(flops=10**10, bytes_accessed=10**7, transcendentals=0),
+        cost_estimate=pl.CostEstimate(flops=work, bytes_accessed=0, transcendentals=0),
         compiler_params=pltpu.CompilerParams(vmem_limit_bytes=VMEM_LIMIT // 4),
     )(meta, *values)
 
@@ -789,31 +789,6 @@
 
 def by_z(start, rows):
     return [(start, rows, "z", k) for k in range(4)]
-
-
-def finish_whole_kernel(held, _, up_ref, down_ref, out_ref, *, widths):
-    total = sum(widths)
-    places = [(s & 3) * 4 + ((s >> 2) & 1) * 2 + (s >> 3) for s in range(16)]
-
-    def take(i):
-        start = (widths[1], 0, widths[1] + widths[0])[i]
-        return jnp.concatenate(
-            [held[pl.ds(p * total + start, widths[i])] for p in places], axis=0
-        )
-
-    up_ref[...] = take(0).T.astype(F32)
-    down_ref[...] = take(1).astype(F32)
-    out_ref[...] = take(2).astype(F32)
-
-
-def finish_whole(value, widths, shapes, specs, up):
-    return pl.pallas_call(
-        functools.partial(finish_whole_kernel, widths=widths),
-        out_shape=tuple(sds(shape, F32) for shape in shapes),
-        grid=(1,), in_specs=[part_spec(value.shape, (0, 0)), ANY], out_specs=specs,
-        input_output_aliases={1: 0},
-        compiler_params=pltpu.CompilerParams(vmem_limit_bytes=VMEM_LIMIT),
-    )(value, up)
 
 
 def finish_kernel(meta_ref, *refs, widths, targets, extra):
@@ -1006,7 +981,7 @@
     wup = Weight(own[2], ((up, up_c, up_x, swap_xor(up_x, 1)), 0, 0, None))
     wdown = Weight(own[3], ((down, swap_xor(down, 1)), 0, 0, None))
     act_out0, act0, gp0 = forward_mlp(meta, hidden, second, wup, wdown, 0)
-    act_out1, ig1, sums1 = whole_layer(
+    act_out1, ig1, sums1, send1, kept1 = whole_layer(
         meta, act_out0, cotangent, gains[1], wqkv, wout, wup, wdown, 1
     )
     cut = 2 * MB_TOK // 3
@@ -1016,7 +991,10 @@
     )
     xh1, r1, qkv, krow, vrow, lse, att, xh2, r2, ks, vs = keep0
     back = mlp_back(meta, ig1, act0, gp0, xh2, r2, att, gains[0], wdown, wup, wout, 0)
-    (send, kept, gln2, gh, gatt), acts_a, act_out0, act_out1 = tie(back, acts_a, act_out0, act_out1)
+    c1 = swap_xor(send1, 1)
+    (send, kept, gln2, gh, gatt), acts_a, act_out0, act_out1, c1 = tie(
+        back, acts_a, act_out0, act_out1, c1
+    )
     mlp0 = combine(
         meta, (kept, swap_xor(send, 1)), by_x(0, 4 * PART_A) + by_z(8 * PART_A, 2 * PART_B)
     )
@@ -1033,53 +1011,46 @@
     a0 = [added(*pair) for pair in zip(quarters(a0[0], 2), quarters(a0_x, 2))]
     a0, c0 = tie(a0, c0)
     a0_z = swap_quarters(a0, 2)
-    c0 = combine(meta, (kept, c0), by_x(0, 4 * PART_C))
+    c0 = combine(meta, (kept, c0), by_x(0, 4 * PART_C), OVERLAPPED)
+    c1 = combine(meta, (kept1, c1), by_x(0, 4 * PART_C))
     b0 = halves(added(b0[0], *b0_z), 1)
-    bc0_x = swap_xor(jnp.concatenate([b0[1], c0[1]], axis=0), 2)
+    bc_x = swap_xor(jnp.concatenate([b0[1], c0[1], c1[1]], axis=0), 2)
 
     def own_sum(grad0, grad1):
         return added(jnp.where(first, grad0, grad1), swap_section(jnp.where(first, grad1, grad0)))
 
-    b0 = added(b0[0], bc0_x[:PART_B])
-    c0 = quarters(added(c0[0], bc0_x[PART_B:]), 2)
-    c0_z = swap_quarters(c0, 2)
-    a0_z, b0, c0_1 = tie(a0_z, b0, c0[1])
-    (a0,) = combine(meta, (a0[0], *a0_z), [(0, PART_A, "all", 0)])
-    spots = (0, PART_A, PART_A + PART_B, PART_A + PART_B + QKV_ROWS)
-    a1, b1, c1, gains1 = [sums1[i:j] for i, j in zip(spots, spots[1:] + (sums1.shape[0],))]
-    ab = own_sum(
-        jnp.concatenate([reduce_rest(a0), reduce_rest(b0)], axis=0),
-        jnp.concatenate([reduce_rest(a1), reduce_rest(b1)], axis=0),
-    )
-    ab, c0_z = tie(ab, c0_z)
-    a_rows = ab.shape[0] * PART_A // (PART_A + PART_B)
-    a_full = lax.all_gather(
-        gather_rest(ab[:a_rows]), "dp", axis=0, axis_index_groups=low_groups(), tiled=True
-    )
-    c0 = added(c0[0], *c0_z)
-    c_own = own_sum(
-        jnp.concatenate([reduce_rest(c0[:QKV_ROWS]), sum_rest(c0[QKV_ROWS:])], axis=0),
-        jnp.concatenate([reduce_rest(c1), sum_rest(gains1)], axis=0),
-    )
+    bc_x, sums1 = tie(bc_x, sums1)
+    cut = PART_B + 4 * PART_C
+    b0 = added(b0[0], bc_x[:PART_B])
+    c0 = quarters(added(c0[0], bc_x[PART_B:cut]), 2)
+    c1 = quarters(added(c1[0], bc_x[cut:]), 2)
+    c = [jnp.concatenate(pair, axis=0) for pair in zip(c0, c1)]
+    c_z = swap_quarters(c, 2)
+    a0_z, b0, c_1 = tie(a0_z, b0, c[1])
+    (a0,) = combine(meta, (a0[0], *a0_z), [(0, PART_A, "all", 0)], OVERLAPPED)
+    a1, b1 = sums1[:PART_A], sums1[PART_A:]
+    ab0 = jnp.concatenate([reduce_rest(a0), reduce_rest(b0)], axis=0)
+    ab1 = jnp.concatenate([reduce_rest(a1), reduce_rest(b1)], axis=0)
+    ab = jnp.where(first, ab0, ab1), swap_section(jnp.where(first, ab1, ab0))
+    if rest_bits():
+        ab = added(*ab)
+        a_rows = ab.shape[0] * PART_A // (PART_A + PART_B)
+        a_own, b_own = ab[:a_rows], ab[a_rows:]
+    else:
+        a_own, b_own = combine(
+            meta, ab, [(0, PART_A, "all", 0), (PART_A, PART_B, "all", 0)], OVERLAPPED
+        )
+    a_own, b_own, c_z = tie(a_own, b_own, c_z)
+    a_full = gather_quad(gather_rest(a_own), 2)
+    c = added(c[0], *c_z)
+    c_own = own_sum(*[
+        jnp.concatenate([reduce_rest(v[:QKV_ROWS]), sum_rest(v[QKV_ROWS:])], axis=0)
+        for v in (c[:PART_C], c[PART_C:])
+    ])
     c_own, ig0 = tie(c_own, ig0)
     grads_in = exchange(ig0, ig1)
     lns = c_own[-GAIN_ROWS:][:2].astype(F32)
-    bc_own = jnp.concatenate([gather_rest(ab[a_rows:]), gather_rest(c_own[:-GAIN_ROWS])], axis=0)
-    bc_pieces = spread_pieces(gather_quad(bc_own, 2))
-    grad_up, grad_qkv = finish(
-        meta, bc_pieces, (UP_B // 16, QKV_ROWS), (True, True), [(D, FF), (D, 3 * D)],
-        [part_spec((D, UP_B), (0, 0)), part_spec((D, 3 * D), (0, 0))],
-    )
-    grad_up, a_full = tie(grad_up, a_full)
-    grad_up, grad_down, grad_out = finish_whole(
-        a_full, (UP_A // 16, DOWN_ROWS, OUT_ROWS), [(D, FF), (FF, D), (D, D)],
-        [
-            part_spec((D, UP_A), (0, UP_B // UP_A)), part_spec((FF, D), (0, 0)),
-            part_spec((D, D), (0, 0)),
-        ],
-        grad_up,
-    )
-
+    bc_own = jnp.concatenate([gather_rest(b_own), gather_rest(c_own[:-GAIN_ROWS])], axis=0)
     def assemble(value0, value1, got):
         return jnp.concatenate(
             [jnp.where(first, value0, got), jnp.where(first, got, value1)], axis=0
@@ -1087,6 +1058,28 @@
 
     activations = assemble(act_out0, act_out1, acts_in)
     input_grads = assemble(ig0, ig1, grads_in)
+    a_full, bc_own = tie(a_full, bc_own)
+    a_pieces = spread_pieces(a_full)
+    bc_full = gather_quad(bc_own, 2)
+    grads_a = finish(
+        meta, a_pieces, (DOWN_ROWS, UP_A // 16, OUT_ROWS), (False, True, False),
+        [(FF, D), (D, FF), (D, D)],
+        [
+            part_spec((FF, D), (0, 0)), part_spec((D, UP_A), (0, UP_B // UP_A)),
+            part_spec((D, D), (0, 0)),
+        ],
+    )
+    across, activations, input_grads, grads_a = tie(
+        swap_xor(bc_full, 2), activations, input_grads, grads_a
+    )
+    grad_down, grad_up, grad_out = grads_a
+    bc_pieces = (bc_full, swap_xor(bc_full, 1), across, swap_xor(across, 1))
+    grad_up, grad_qkv = finish(
+        meta, bc_pieces, (UP_B // 16, QKV_ROWS), (True, True), [(D, FF), (D, 3 * D)],
+        [part_spec((D, UP_B), (0, 0)), part_spec((D, 3 * D), (0, 0))],
+        (grad_up,), {5: 0},
+    )
+
     return (
         activations[None],
         input_grads[None],

time: 352 us -> 349 us (level)
  waiting for transfers between devices: 108 us -> 86.5 us
  starting transfers between devices: 36.5 us -> 50 us
  Pallas kernels: 158 us -> 165 us
    ppermute x26 -> x33, starting transfers between devices: 25.4 us -> 37.2 us  [swap_xor(): return lax.ppermute(value, 'dp', [(i, i ^ mask) for i in range(size)])]
    ppermute x9, waiting for transfers between devices: 16.5 us -> 9.74 us  [swap_section(): return lax.ppermute(value, 'section', [(0, 1), (1, 0)])]
    reduce_scatter x1, waiting for transfers between devices: 6.46 us -> 0.01 us  [per_device(): lax.psum_scatter(sums1.reshape(-1, D), 'dp', scatter_dimension=0, axis_in...]
    pallas_call x1 -> x2, Pallas kernels: 5.08 us -> 11.2 us  [finish(): pl.pallas_call(functools.partial(finish_kernel, widths=widths, targets=fl...]
    pallas_call x1 -> x0, Pallas kernels: 5.49 us -> none  [finish_whole(): pl.pallas_call(functools.partial(finish_whole_kernel, widths=widths), out...]
    ppermute x26 -> x33, waiting for transfers between devices: 81.6 us -> 76.8 us  [swap_xor(): return lax.ppermute(value, 'dp', [(i, i ^ mask) for i in range(size)])]
    concatenate x2 -> x7, other arithmetic: 0.05 us -> 3.87 us  [the longest x2 3.74 us: assemble(): jnp.concatenate([jnp.where(first, value0, got), jnp.where(first, got, val...]
    broadcast_in_dim x2 -> x0, other arithmetic: 3.74 us -> none  [the longest x1 1.87 us: per_device(): activations[None]]
  transfers between devices with their start and end apart: 37 -> 43, of which waited for: 17 -> 17; matrix products, arithmetic and copies ran while one was open for 5% -> 5% of each run, Pallas kernels for 21% -> 22%
where the time goes in v5:
time: 349 us; the launch traced here: 344 us
  Pallas kernels  165 us (47%)
  waiting for transfers between devices  86.5 us (25%)
  starting transfers between devices  50 us (14%)
  local copies, waits for them, and re-layouts  16.8 us (5%)
  between operations  14.9 us (4%)
  other arithmetic  11.4 us (3%)
    pallas_call x5, Pallas kernels, call(): pl.pallas_call(kernel, out_shape=tuple(outs), grid_spec=pltpu.PrefetchSca...  149 us
    ppermute x33, waiting for transfers between devices, swap_xor(): return lax.ppermute(value, 'dp', [(i, i ^ mask) for i in range(size)])  76.8 us
    ppermute x33, starting transfers between devices, swap_xor(): return lax.ppermute(value, 'dp', [(i, i ^ mask) for i in range(size)])  37.2 us
    ppermute x9, starting transfers between devices, swap_section(): return lax.ppermute(value, 'section', [(0, 1), (1, 0)])  12.7 us
    pallas_call x2, Pallas kernels, finish(): pl.pallas_call(functools.partial(finish_kernel, widths=widths, targets=fl...  11.2 us
    unnamed x87, local copies, waits for them, and re-layouts  10.3 us
    ppermute x9, waiting for transfers between devices, swap_section(): return lax.ppermute(value, 'section', [(0, 1), (1, 0)])  9.74 us
  transfers between devices with their start and end apart: 43, of which 17 were waited for; matrix products, arithmetic and copies ran while one was open for 5% of the time, Pallas kernels for 22%

profile of v5, /device:TPU:0, one launch (start us, length us, event | category | flops | bytes accessed | tf_op | source)
XLA Modules:
  0.0 344.5 jit_solution(128536530176497250)
XLA Ops:
  9.4 3.0 collective-permute-start
  12.6 1.9 dynamic-slice_bitcast_fusion.1
  14.5 2.0 collective-permute-start.5
  16.5 8.8 %collective-permute-done.1 = f32[2,512]{1,0:T(2,128)S(1)} collective-permute-done((f32[2,512]{1,0:T(2,128)S(1)}, f32[2,512]{1,0:T(2,128)S(1)}, u32[]{:S(2)}, u32[]{:S(2)}) %collective-permute-start.1) | collective-permute-done | bytes 4128 | tf_op jit(solution)/shard_map/ppermute | solution.py:839
  25.3 2.0 collective-permute-start.3
  29.9 7.7 %collective-permute-done.3.refs_3_.refs_8_.refs_11_ = bf16[128,2048]{1,0:T(8,128)(2,1)S(1)} collective-permute-done((bf16[128,2048]{1,0:T(8,128)(2,1)S(1)}, bf16[128,2048]{1,0:T(8,128)(2,1)S(1)}, u32[]{:S(2)}, u32[]{:S(2)}) %collective-permute-start.3) | collective-permute-done | bytes 524320 | tf_op jit(solution)/shard_map/ppermute | solution.py:835
  41.5 16.4 %shard_map.161 = (bf16[512,1536]{1,0:T(8,128)(2,1)}, f32[1,1536]{1,0:T(1,128)}, bf16[1536,1536]{1,0:T(8,128)(2,1)}, bf16[1536,512]{1,0:T(8,128)(2,1)}, bf16[1536...) custom-call(s32[9]{0:T(128)} %concatenate.52.meta_ref, ...), custom_call_target="tpu_custom_call" | custom-call | tf_op jit(solution)/shard_map/pallas_call | solution.py:603
  58.7 3.1 collective-permute-done.9.refs_4_.refs_14_.refs_7_
  63.0 15.8 %shard_map.162 = (bf16[1536,512]{1,0:T(8,128)(2,1)}, bf16[2048,1536]{1,0:T(8,128)(2,1)}, bf16[2048,1536]{1,0:T(8,128)(2,1)}) custom-call(s32[9]{0:T(128)} %concatenate.52.meta_ref, f32[512,1536]{1,0:T(8,128)} %get-tuple-element.137.hid_ref, bf16[512,1536]{1,0:T(8,128)(2,1)} %get-tuple-element.138.sec_ref, bf16[512,2048]{1,0:T(8,128)(2,1)} %bitcast.29, ...), custom_call_target="tpu_custom_call" | custom-call | tf_op jit(solution)/shard_map/pallas_call | solution.py:603
  78.8 68.2 %shard_map.163 = (bf16[1536,512]{1,0:T(8,128)(2,1)}, bf16[1536,512]{1,0:T(8,128)(2,1)}, bf16[16,288,512]{2,1,0:T(8,128)(2,1)}, bf16[896,512]{1,0:T(8,128)(2,1)}, bf16[896,512]{1,0:T(8,128)(2,1)}) custom-call(s32[9]{0:T(128)} %concatenate.52.meta_ref, bf16[1536,512]{1,0:T(8,128)(2,1)} %get-tuple-element.185.x_ref, bf16[3072,512]{1,0:T(8,128)(2,1)} %cot_ref.1, ...), custom_call_target="tpu_custom_call" | custom-call | tf_op jit(solution)/shard_map/pallas_call | solution.py:603
  150.5 28.8 %shard_map.164 = (bf16[2304,512]{1,0:T(8,128)(2,1)}, bf16[2304,512]{1,0:T(8,128)(2,1)}, f32[1,512]{1,0:T(1,128)}, f32[512,1536]{1,0:T(8,128)}, bf16[512,1536]{1,0:T(8,128)(2,1)}) custom-call(s32[9]{0:T(128)} %concatenate.52.meta_ref, bf16[1536,512]{1,0:T(8,128)(2,1)} %get-tuple-element.143.seed_ref, bf16[2048,1536]{1,0:T(8,128)(2,1)} %get-tuple-element.144.act_ref, ...), custom_call_target="tpu_custom_call" | custom-call | tf_op jit(solution)/shard_map/pallas_call | solution.py:603
  180.4 3.9 %collective-permute-done.13.refs_1_ = bf16[2304,512]{1,0:T(8,128)(2,1)S(1)} collective-permute-done((bf16[2304,512]{1,0:T(8,128)(2,1)}, bf16[2304,512]{1,0:T(8,128)(2,1)S(1)}, u32[]{:S(2)}, u32[]{:S(2)}) %collective-permute-start.13) | collective-permute-done | bytes 2359328 | tf_op jit(solution)/shard_map/ppermute | solution.py:835
  188.6 2.0 slice_select_fusion.1
  193.3 2.6 collective-permute-start.16
  196.1 19.4 %shard_map.166 = (bf16[1536,512]{1,0:T(8,128)(2,1)}, bf16[896,512]{1,0:T(8,128)(2,1)}, bf16[896,512]{1,0:T(8,128)(2,1)}) custom-call(s32[9]{0:T(128)} %concatenate.52.meta_ref, f32[512,1536]{1,0:T(8,128)} %get-tuple-element.166.gh_ref, bf16[512,1536]{1,0:T(8,128)(2,1)} %get-tuple-element.167.gatt_ref, bf16[512,1536]{1,0:T(8,128)(2,1)} %get-tuple-element.168.xh1_ref, ...), custom_call_target="tpu_custom_call" | custom-call | tf_op jit(solution)/shard_map/pallas_call | solution.py:603
  219.5 1.9 shard_map.167
  222.8 3.5 %collective-permute-start.21 = (bf16[224,512]{1,0:T(8,128)(2,1)}, bf16[224,512]{1,0:T(8,128)(2,1)S(1)}, u32[]{:S(2)}, u32[]{:S(2)}) collective-permute-start(bf16[224,512]{1,0:T(8,128)(2,1)} %get-tuple-element.190), channel_id=1, source_target_pairs={{0,8},{1,9},{2,10},{3,11},{4,12},{5,13},{6,14},{7,15},{8,0},{9,1},... | collective-permute-start | bytes 688136 | tf_op jit(solution)/shard_map/ppermute | solution.py:835
  226.4 19.9 %collective-permute-done.23 = bf16[960,512]{1,0:T(8,128)(2,1)} collective-permute-done((bf16[960,512]{1,0:T(8,128)(2,1)S(1)}, bf16[960,512]{1,0:T(8,128)(2,1)}, u32[]{:S(2)}, u32[]{:S(2)}) %collective-permute-start.23) | collective-permute-done | bytes 983072 | tf_op jit(solution)/shard_map/ppermute | solution.py:835
  251.4 4.1 %collective-permute-start.25 = (bf16[224,512]{1,0:T(8,128)(2,1)S(1)}, bf16[224,512]{1,0:T(8,128)(2,1)S(1)}, u32[]{:S(2)}, u32[]{:S(2)}) collective-permute-start(bf16[224,512]{1,0:T(8,128)(2,1)S(1)} %pad_maximum_fusion.7), channel_id=1, source_target_pairs={{0,4},{1,5},{2,6},{3,7},{4,0},{5,1},{6,2},{7,3},{8,12},{9,13},{10,... | collective-permute-start | bytes 688136 | tf_op jit(solution)/shard_map/ppermute | solution.py:835
  256.1 1.9 collective-permute-start.27
  259.2 5.2 %collective-permute-done.25 = bf16[224,512]{1,0:T(8,128)(2,1)S(1)} collective-permute-done((bf16[224,512]{1,0:T(8,128)(2,1)S(1)}, bf16[224,512]{1,0:T(8,128)(2,1)S(1)}, u32[]{:S(2)}, u32[]{:S(2)}) %collective-permute-start.25) | collective-permute-done | bytes 229408 | tf_op jit(solution)/shard_map/ppermute | solution.py:835
  264.4 10.4 %collective-permute-done.26 = bf16[224,512]{1,0:T(8,128)(2,1)S(1)} collective-permute-done((bf16[224,512]{1,0:T(8,128)(2,1)S(1)}, bf16[224,512]{1,0:T(8,128)(2,1)S(1)}, u32[]{:S(2)}, u32[]{:S(2)}) %collective-permute-start.26) | collective-permute-done | bytes 229408 | tf_op jit(solution)/shard_map/ppermute | solution.py:835
  276.1 3.8 %collective-permute-start.28 = (bf16[224,512]{1,0:T(8,128)(2,1)S(1)}, bf16[224,512]{1,0:T(8,128)(2,1)S(1)}, u32[]{:S(2)}, u32[]{:S(2)}) collective-permute-start(bf16[224,512]{1,0:T(8,128)(2,1)S(1)} %get-tuple-element.213), channel_id=1, source_target_pairs={{0,4},{1,5},{2,6},{3,7},{4,0},{5,1},{6,2},{7,3},{8,12},{9,13},{10,... | collective-permute-start | bytes 688136 | tf_op jit(solution)/shard_map/ppermute | solution.py:835
  283.6 3.2 collective-permute-done.28
  286.9 11.7 %collective-permute-done.29 = bf16[224,512]{1,0:T(8,128)(2,1)S(1)} collective-permute-done((bf16[224,512]{1,0:T(8,128)(2,1)S(1)}, bf16[224,512]{1,0:T(8,128)(2,1)S(1)}, u32[]{:S(2)}, u32[]{:S(2)}) %collective-permute-start.29) | collective-permute-done | bytes 229408 | tf_op jit(solution)/shard_map/ppermute | solution.py:835
  300.8 3.4 collective-permute-start.32
  304.5 2.1 collective-permute-start.34
  306.6 1.9 pad_maximum_fusion
  308.8 8.2 %collective-permute-done.33 = bf16[160,512]{1,0:T(8,128)(2,1)S(1)} collective-permute-done((bf16[160,512]{1,0:T(8,128)(2,1)S(1)}, bf16[160,512]{1,0:T(8,128)(2,1)S(1)}, u32[]{:S(2)}, u32[]{:S(2)}) %collective-permute-start.33) | collective-permute-done | bytes 163872 | tf_op jit(solution)/shard_map/ppermute | solution.py:835
  318.8 1.9 pad_maximum_fusion.1
  322.6 6.1 %shard_map.171 = (f32[2048,512]{1,0:T(8,128)}, f32[512,2048]{1,0:T(8,128)}, f32[512,512]{1,0:T(8,128)}) custom-call(s32[9]{0:T(128)} %concatenate.52.meta_ref, bf16[896,512]{1,0:T(8,128)(2,1)} %copy-done.19, bf16[896,512]{1,0:T(8,128)(2,1)} %copy-done.26, bf16[896,512]{1,0:T(8,128)(2,1)} %copy-done.25, bf16[896,512]{1,0:T(8,128)(2,1)} %copy-done.27), custom_call_target="tpu_custom_call" | custom-call | tf_op jit(solution)/shard_map/pallas_call | solution.py:817
  332.4 5.1 %shard_map.172 = (f32[512,2048]{1,0:T(8,128)}, f32[512,1536]{1,0:T(8,128)}) custom-call(s32[9]{0:T(128)} %concatenate.52.meta_ref, bf16[640,512]{1,0:T(8,128)(2,1)} %copy-done.20, bf16[640,512]{1,0:T(8,128)(2,1)} %copy-done.29, bf16[640,512]{1,0:T(8,128)(2,1)} %copy-done.28, bf16[640,512]{1,0:T(8,128)(2,1)} %copy-done.30, ...), custom_call_target="tpu_custom_call", output_to_operand_aliasing={{0}: (5, {})} | custom-call | tf_op jit(solution)/shard_map/pallas_call | solution.py:817
  (194 shorter events, 49.7 us)
Async XLA Ops:
  7.2 239.1 %reduce-scatter.2.cloned.1.call-start = ((), (), s32[]{:S(2)}) async-start(), calls=%async_computation.1 | async-start | bytes 5013504 | tf_op jit(solution)/shard_map/reduce_scatter | solution.py:989
  9.4 15.9 %collective-permute-start = (bf16[128,2048]{1,0:T(8,128)(2,1)S(1)}, bf16[128,2048]{1,0:T(8,128)(2,1)S(1)}, u32[]{:S(2)}, u32[]{:S(2)}) collective-permute-start(bf16[128,2048]{1,0:T(8,128)(2,1)S(1)} %pad_maximum_fusion.5), channel_id=1, source_target_pairs={{0,16},{16,0},{1,17},{17,1},{2,18},{18,2},{3,19},{19,3},{4,20},{20... | collective-permute-start | bytes 1572872 | tf_op jit(solution)/shard_map/ppermute | solution.py:839
  12.5 12.8 %collective-permute-start.1 = (f32[2,512]{1,0:T(2,128)S(1)}, f32[2,512]{1,0:T(2,128)S(1)}, u32[]{:S(2)}, u32[]{:S(2)}) collective-permute-start(f32[2,512]{1,0:T(2,128)S(1)} %pad_maximum_fusion.11), channel_id=1, source_target_pairs={{0,16},{16,0},{1,17},{17,1},{2,18},{18,2},{3,19},{19,3},{4,20},{20... | collective-permute-start | bytes 12296 | tf_op jit(solution)/shard_map/ppermute | solution.py:839
  14.5 23.1 %collective-permute-start.5 = (bf16[128,2048]{1,0:T(8,128)(2,1)}, bf16[128,2048]{1,0:T(8,128)(2,1)}, u32[]{:S(2)}, u32[]{:S(2)}) collective-permute-start(bf16[128,2048]{1,0:T(8,128)(2,1)} %dynamic-slice_bitcast_fusion.1), channel_id=1, source_target_pairs={{0,16},{16,0},{1,17},{17,1},{2,18},{18,2},{3,19},{19,3},{4,20},{20... | collective-permute-start | bytes 1572872 | tf_op jit(solution)/shard_map/ppermute | solution.py:839
  25.3 12.3 %collective-permute-start.3 = (bf16[128,2048]{1,0:T(8,128)(2,1)S(1)}, bf16[128,2048]{1,0:T(8,128)(2,1)S(1)}, u32[]{:S(2)}, u32[]{:S(2)}) collective-permute-start(bf16[128,2048]{1,0:T(8,128)(2,1)S(1)} %collective-permute-done.refs_1_.refs_6_.refs_9_), channel_id=1, source_target_pairs={{0,2},{1,3},{2,0},{3,1},{4,6},{5,7},{6,4},{7,5},{8,10},{9,11},{10,... | collective-permute-start | bytes 1572872 | tf_op jit(solution)/shard_map/ppermute | solution.py:835
  28.4 29.8 %collective-permute-start.8 = (bf16[1024,512]{1,0:T(8,128)(2,1)}, bf16[1024,512]{1,0:T(8,128)(2,1)S(1)}, u32[]{:S(2)}, u32[]{:S(2)}) collective-permute-start(bf16[1024,512]{1,0:T(8,128)(2,1)} %dynamic-slice_bitcast_fusion), channel_id=1, source_target_pairs={{0,16},{16,0},{1,17},{17,1},{2,18},{18,2},{3,19},{19,3},{4,20},{20... | collective-permute-start | bytes 3145736 | tf_op jit(solution)/shard_map/ppermute | solution.py:839
  37.6 20.2 %collective-permute-start.6 = (bf16[128,2048]{1,0:T(8,128)(2,1)}, bf16[128,2048]{1,0:T(8,128)(2,1)}, u32[]{:S(2)}, u32[]{:S(2)}) collective-permute-start(bf16[128,2048]{1,0:T(8,128)(2,1)} %collective-permute-done.5.refs_1_.refs_11_.refs_4_), channel_id=1, source_target_pairs={{0,2},{1,3},{2,0},{3,1},{4,6},{5,7},{6,4},{7,5},{8,10},{9,11},{10,... | collective-permute-start | bytes 1572872 | tf_op jit(solution)/shard_map/ppermute | solution.py:835
  39.0 18.8 %collective-permute-start.7 = (bf16[128,2048]{1,0:T(8,128)(2,1)}, bf16[128,2048]{1,0:T(8,128)(2,1)}, u32[]{:S(2)}, u32[]{:S(2)}) collective-permute-start(bf16[128,2048]{1,0:T(8,128)(2,1)} %collective-permute-done.5.refs_1_.refs_11_.refs_4_), channel_id=1, source_target_pairs={{0,1},{1,0},{2,3},{3,2},{4,5},{5,4},{6,7},{7,6},{8,9},{9,8},{10,11... | collective-permute-start | bytes 1572872 | tf_op jit(solution)/shard_map/ppermute | solution.py:835
  149.0 30.4 %collective-permute-start.11 = (bf16[1024,512]{1,0:T(8,128)(2,1)S(1)}, bf16[1024,512]{1,0:T(8,128)(2,1)S(1)}, u32[]{:S(2)}, u32[]{:S(2)}) collective-permute-start(bf16[1024,512]{1,0:T(8,128)(2,1)S(1)} %slice_select_fusion), channel_id=1, source_target_pairs={{0,16},{16,0},{1,17},{17,1},{2,18},{18,2},{3,19},{19,3},{4,20},{20... | collective-permute-start | bytes 3145736 | tf_op jit(solution)/shard_map/ppermute | solution.py:839
  150.4 28.9 %collective-permute-start.12 = (bf16[896,512]{1,0:T(8,128)(2,1)S(1)}, bf16[896,512]{1,0:T(8,128)(2,1)S(1)}, u32[]{:S(2)}, u32[]{:S(2)}) collective-permute-start(bf16[896,512]{1,0:T(8,128)(2,1)S(1)} %copy-done.42), channel_id=1, source_target_pairs={{0,1},{1,0},{2,3},{3,2},{4,5},{5,4},{6,7},{7,6},{8,9},{9,8},{10,11... | collective-permute-start | bytes 2752520 | tf_op jit(solution)/shard_map/ppermute | solution.py:835
  187.0 28.5 %collective-permute-start.14 = (bf16[896,512]{1,0:T(8,128)(2,1)S(1)}, bf16[896,512]{1,0:T(8,128)(2,1)S(1)}, u32[]{:S(2)}, u32[]{:S(2)}) collective-permute-start(bf16[896,512]{1,0:T(8,128)(2,1)S(1)} %get-tuple-element.180), channel_id=1, source_target_pairs={{0,2},{1,3},{2,0},{3,1},{4,6},{5,7},{6,4},{7,5},{8,10},{9,11},{10,... | collective-permute-start | bytes 2752520 | tf_op jit(solution)/shard_map/ppermute | solution.py:835
  190.6 24.9 %collective-permute-start.18 = (bf16[512,512]{1,0:T(8,128)(2,1)}, bf16[512,512]{1,0:T(8,128)(2,1)S(1)}, u32[]{:S(2)}, u32[]{:S(2)}) collective-permute-start(bf16[512,512]{1,0:T(8,128)(2,1)} %slice_select_fusion.1), channel_id=1, source_target_pairs={{0,16},{16,0},{1,17},{17,1},{2,18},{18,2},{3,19},{19,3},{4,20},{20... | collective-permute-start | bytes 1572872 | tf_op jit(solution)/shard_map/ppermute | solution.py:839
  191.7 23.8 %collective-permute-start.15 = (bf16[128,512]{1,0:T(8,128)(2,1)S(1)}, bf16[128,512]{1,0:T(8,128)(2,1)S(1)}, u32[]{:S(2)}, u32[]{:S(2)}) collective-permute-start(bf16[128,512]{1,0:T(8,128)(2,1)S(1)} %get-tuple-element.181), channel_id=1, source_target_pairs={{0,4},{1,5},{2,6},{3,7},{4,0},{5,1},{6,2},{7,3},{8,12},{9,13},{10,... | collective-permute-start | bytes 393224 | tf_op jit(solution)/shard_map/ppermute | solution.py:835
  193.3 22.3 %collective-permute-start.16 = (bf16[128,512]{1,0:T(8,128)(2,1)S(1)}, bf16[128,512]{1,0:T(8,128)(2,1)S(1)}, u32[]{:S(2)}, u32[]{:S(2)}) collective-permute-start(bf16[128,512]{1,0:T(8,128)(2,1)S(1)} %get-tuple-element.182), channel_id=1, source_target_pairs={{0,8},{1,9},{2,10},{3,11},{4,12},{5,13},{6,14},{7,15},{8,0},{9,1},... | collective-permute-start | bytes 393224 | tf_op jit(solution)/shard_map/ppermute | solution.py:835
  195.8 19.7 %collective-permute-start.17 = (bf16[128,512]{1,0:T(8,128)(2,1)S(1)}, bf16[128,512]{1,0:T(8,128)(2,1)S(1)}, u32[]{:S(2)}, u32[]{:S(2)}) collective-permute-start(bf16[128,512]{1,0:T(8,128)(2,1)S(1)} %get-tuple-element.183), channel_id=1, source_target_pairs={{0,12},{1,13},{2,14},{3,15},{4,8},{5,9},{6,10},{7,11},{8,4},{9,5},... | collective-permute-start | bytes 393224 | tf_op jit(solution)/shard_map/ppermute | solution.py:835
  221.5 24.8 %collective-permute-start.23 = (bf16[960,512]{1,0:T(8,128)(2,1)S(1)}, bf16[960,512]{1,0:T(8,128)(2,1)}, u32[]{:S(2)}, u32[]{:S(2)}) collective-permute-start(bf16[960,512]{1,0:T(8,128)(2,1)S(1)} %pad_maximum_fusion.2), channel_id=1, source_target_pairs={{0,2},{1,3},{2,0},{3,1},{4,6},{5,7},{6,4},{7,5},{8,10},{9,11},{10,... | collective-permute-start | bytes 2949128 | tf_op jit(solution)/shard_map/ppermute | solution.py:835
  222.0 26.7 %collective-permute-start.20 = (bf16[224,512]{1,0:T(8,128)(2,1)}, bf16[224,512]{1,0:T(8,128)(2,1)S(1)}, u32[]{:S(2)}, u32[]{:S(2)}) collective-permute-start(bf16[224,512]{1,0:T(8,128)(2,1)} %get-tuple-element.189), channel_id=1, source_target_pairs={{0,4},{1,5},{2,6},{3,7},{4,0},{5,1},{6,2},{7,3},{8,12},{9,13},{10,... | collective-permute-start | bytes 688136 | tf_op jit(solution)/shard_map/ppermute | solution.py:835
  222.8 25.9 %collective-permute-start.21 = (bf16[224,512]{1,0:T(8,128)(2,1)}, bf16[224,512]{1,0:T(8,128)(2,1)S(1)}, u32[]{:S(2)}, u32[]{:S(2)}) collective-permute-start(bf16[224,512]{1,0:T(8,128)(2,1)} %get-tuple-element.190), channel_id=1, source_target_pairs={{0,8},{1,9},{2,10},{3,11},{4,12},{5,13},{6,14},{7,15},{8,0},{9,1},... | collective-permute-start | bytes 688136 | tf_op jit(solution)/shard_map/ppermute | solution.py:835
  226.3 22.4 %collective-permute-start.22 = (bf16[224,512]{1,0:T(8,128)(2,1)}, bf16[224,512]{1,0:T(8,128)(2,1)S(1)}, u32[]{:S(2)}, u32[]{:S(2)}) collective-permute-start(bf16[224,512]{1,0:T(8,128)(2,1)} %get-tuple-element.191), channel_id=1, source_target_pairs={{0,12},{1,13},{2,14},{3,15},{4,8},{5,9},{6,10},{7,11},{8,4},{9,5},... | collective-permute-start | bytes 688136 | tf_op jit(solution)/shard_map/ppermute | solution.py:835
  251.4 13.0 %collective-permute-start.25 = (bf16[224,512]{1,0:T(8,128)(2,1)S(1)}, bf16[224,512]{1,0:T(8,128)(2,1)S(1)}, u32[]{:S(2)}, u32[]{:S(2)}) collective-permute-start(bf16[224,512]{1,0:T(8,128)(2,1)S(1)} %pad_maximum_fusion.7), channel_id=1, source_target_pairs={{0,4},{1,5},{2,6},{3,7},{4,0},{5,1},{6,2},{7,3},{8,12},{9,13},{10,... | collective-permute-start | bytes 688136 | tf_op jit(solution)/shard_map/ppermute | solution.py:835
  255.5 19.3 %collective-permute-start.26 = (bf16[224,512]{1,0:T(8,128)(2,1)S(1)}, bf16[224,512]{1,0:T(8,128)(2,1)S(1)}, u32[]{:S(2)}, u32[]{:S(2)}) collective-permute-start(bf16[224,512]{1,0:T(8,128)(2,1)S(1)} %pad_maximum_fusion.8), channel_id=1, source_target_pairs={{0,8},{1,9},{2,10},{3,11},{4,12},{5,13},{6,14},{7,15},{8,0},{9,1},... | collective-permute-start | bytes 688136 | tf_op jit(solution)/shard_map/ppermute | solution.py:835
  256.1 18.7 %collective-permute-start.27 = (bf16[224,512]{1,0:T(8,128)(2,1)S(1)}, bf16[224,512]{1,0:T(8,128)(2,1)S(1)}, u32[]{:S(2)}, u32[]{:S(2)}) collective-permute-start(bf16[224,512]{1,0:T(8,128)(2,1)S(1)} %pad_maximum_fusion.9), channel_id=1, source_target_pairs={{0,12},{1,13},{2,14},{3,15},{4,8},{5,9},{6,10},{7,11},{8,4},{9,5},... | collective-permute-start | bytes 688136 | tf_op jit(solution)/shard_map/ppermute | solution.py:835
  276.1 10.8 %collective-permute-start.28 = (bf16[224,512]{1,0:T(8,128)(2,1)S(1)}, bf16[224,512]{1,0:T(8,128)(2,1)S(1)}, u32[]{:S(2)}, u32[]{:S(2)}) collective-permute-start(bf16[224,512]{1,0:T(8,128)(2,1)S(1)} %get-tuple-element.213), channel_id=1, source_target_pairs={{0,4},{1,5},{2,6},{3,7},{4,0},{5,1},{6,2},{7,3},{8,12},{9,13},{10,... | collective-permute-start | bytes 688136 | tf_op jit(solution)/shard_map/ppermute | solution.py:835
  279.9 18.6 %collective-permute-start.29 = (bf16[224,512]{1,0:T(8,128)(2,1)S(1)}, bf16[224,512]{1,0:T(8,128)(2,1)S(1)}, u32[]{:S(2)}, u32[]{:S(2)}) collective-permute-start(bf16[224,512]{1,0:T(8,128)(2,1)S(1)} %get-tuple-element.213), channel_id=1, source_target_pairs={{0,8},{1,9},{2,10},{3,11},{4,12},{5,13},{6,14},{7,15},{8,0},{9,1},... | collective-permute-start | bytes 688136 | tf_op jit(solution)/shard_map/ppermute | solution.py:835
  280.7 17.8 %collective-permute-start.30 = (bf16[224,512]{1,0:T(8,128)(2,1)S(1)}, bf16[224,512]{1,0:T(8,128)(2,1)S(1)}, u32[]{:S(2)}, u32[]{:S(2)}) collective-permute-start(bf16[224,512]{1,0:T(8,128)(2,1)S(1)} %get-tuple-element.213), channel_id=1, source_target_pairs={{0,12},{1,13},{2,14},{3,15},{4,8},{5,9},{6,10},{7,11},{8,4},{9,5},... | collective-permute-start | bytes 688136 | tf_op jit(solution)/shard_map/ppermute | solution.py:835
  282.6 35.7 %collective-permute-start.36 = (bf16[1536,512]{1,0:T(8,128)(2,1)S(1)}, bf16[1536,512]{1,0:T(8,128)(2,1)S(1)}, u32[]{:S(2)}, u32[]{:S(2)}) collective-permute-start(bf16[1536,512]{1,0:T(8,128)(2,1)S(1)} %broadcast_select_fusion.2), channel_id=1, source_target_pairs={{0,16},{16,0},{1,17},{17,1},{2,18},{18,2},{3,19},{19,3},{4,20},{20... | collective-permute-start | bytes 4718600 | tf_op jit(solution)/shard_map/ppermute | solution.py:839
  298.7 19.1 %collective-permute-start.38 = (bf16[896,512]{1,0:T(8,128)(2,1)S(1)}, bf16[896,512]{1,0:T(8,128)(2,1)S(1)}, u32[]{:S(2)}, u32[]{:S(2)}) collective-permute-start(bf16[896,512]{1,0:T(8,128)(2,1)S(1)} %pad_maximum_fusion.3.refs_0_), channel_id=1, source_target_pairs={{0,2},{1,3},{2,0},{3,1},{4,6},{5,7},{6,4},{7,5},{8,10},{9,11},{10,... | collective-permute-start | bytes 2752520 | tf_op jit(solution)/shard_map/ppermute | solution.py:835
  304.2 12.8 %collective-permute-start.33 = (bf16[160,512]{1,0:T(8,128)(2,1)S(1)}, bf16[160,512]{1,0:T(8,128)(2,1)S(1)}, u32[]{:S(2)}, u32[]{:S(2)}) collective-permute-start(bf16[160,512]{1,0:T(8,128)(2,1)S(1)} %pad_maximum_fusion.10), channel_id=1, source_target_pairs={{0,8},{1,9},{2,10},{3,11},{4,12},{5,13},{6,14},{7,15},{8,0},{9,1},... | collective-permute-start | bytes 491528 | tf_op jit(solution)/shard_map/ppermute | solution.py:835
  304.5 12.4 %collective-permute-start.34 = (bf16[160,512]{1,0:T(8,128)(2,1)S(1)}, bf16[160,512]{1,0:T(8,128)(2,1)S(1)}, u32[]{:S(2)}, u32[]{:S(2)}) collective-permute-start(bf16[160,512]{1,0:T(8,128)(2,1)S(1)} %pad_maximum_fusion.10), channel_id=1, source_target_pairs={{0,12},{1,13},{2,14},{3,15},{4,8},{5,9},{6,10},{7,11},{8,4},{9,5},... | collective-permute-start | bytes 491528 | tf_op jit(solution)/shard_map/ppermute | solution.py:835
  308.8 11.9 %collective-permute-start.37 = (bf16[896,512]{1,0:T(8,128)(2,1)S(1)}, bf16[896,512]{1,0:T(8,128)(2,1)S(1)}, u32[]{:S(2)}, u32[]{:S(2)}) collective-permute-start(bf16[896,512]{1,0:T(8,128)(2,1)S(1)} %pad_maximum_fusion.3.refs_0_), channel_id=1, source_target_pairs={{0,1},{1,0},{2,3},{3,2},{4,5},{5,4},{6,7},{7,6},{8,9},{9,8},{10,11... | collective-permute-start | bytes 2752520 | tf_op jit(solution)/shard_map/ppermute | solution.py:835
  317.1 12.3 %collective-permute-start.35 = (bf16[640,512]{1,0:T(8,128)(2,1)S(1)}, bf16[640,512]{1,0:T(8,128)(2,1)S(1)}, u32[]{:S(2)}, u32[]{:S(2)}) collective-permute-start(bf16[640,512]{1,0:T(8,128)(2,1)S(1)} %pad_maximum_fusion.4.refs_0_), channel_id=1, source_target_pairs={{0,2},{1,3},{2,0},{3,1},{4,6},{5,7},{6,4},{7,5},{8,10},{9,11},{10,... | collective-permute-start | bytes 1966088 | tf_op jit(solution)/shard_map/ppermute | solution.py:835
  317.9 12.2 %collective-permute-start.40 = (bf16[640,512]{1,0:T(8,128)(2,1)S(1)}, bf16[640,512]{1,0:T(8,128)(2,1)S(1)}, u32[]{:S(2)}, u32[]{:S(2)}) collective-permute-start(bf16[640,512]{1,0:T(8,128)(2,1)S(1)} %pad_maximum_fusion.4.refs_0_), channel_id=1, source_target_pairs={{0,1},{1,0},{2,3},{3,2},{4,5},{5,4},{6,7},{7,6},{8,9},{9,8},{10,11... | collective-permute-start | bytes 1966088 | tf_op jit(solution)/shard_map/ppermute | solution.py:835
  (54 other events, 390.3 us)
Sparse Core Ops, SparseCore 0:
  147.2 94.2 reduce-scatter.1

commit v6 on v5

--- a/solution.py
+++ b/solution.py
@@ -599,7 +599,7 @@
     return pl.BlockSpec((height, TILE), lambda t, *_: (0, N_TILE - 1 - t))
 
 
-def call(kernel, grid, outs, in_specs, out_specs, scratch, args):
+def call(kernel, grid, outs, in_specs, out_specs, scratch, args, limit=VMEM_LIMIT):
     return pl.pallas_call(
         kernel,
         out_shape=tuple(outs),
@@ -608,7 +608,7 @@
             scratch_shapes=scratch,
         ),
         cost_estimate=pl.CostEstimate(flops=0, bytes_accessed=0, transcendentals=0),
-        compiler_params=pltpu.CompilerParams(vmem_limit_bytes=VMEM_LIMIT),
+        compiler_params=pltpu.CompilerParams(vmem_limit_bytes=limit),
     )(*args)
 
 
@@ -716,6 +716,7 @@
         [rev_rows(D), whole((half, D)), whole((half, D))],
         attn_back_scratch() + [pltpu.VMEM((3 * D, TILE), F32)] + weight_scratch(wqkv),
         (meta, gh, gatt, xh1, r1, qkv, krow, vrow, lse, ks, vs, gains, gln2, *wqkv.flat()),
+        VMEM_LIMIT * 3 // 4,
     )
 
 
@@ -822,7 +823,7 @@
             scratch_shapes=[pltpu.VMEM((4 * rows, D), BF), pltpu.SemaphoreType.DMA],
         ),
         input_output_aliases=alias or {},
-        compiler_params=pltpu.CompilerParams(vmem_limit_bytes=VMEM_LIMIT),
+        compiler_params=pltpu.CompilerParams(vmem_limit_bytes=VMEM_LIMIT * 5 // 8),
     )(meta, *pieces, *more)
 
 
@@ -1040,7 +1041,8 @@
         a_own, b_own = combine(
             meta, ab, [(0, PART_A, "all", 0), (PART_A, PART_B, "all", 0)], OVERLAPPED
         )
-    a_own, b_own, c_z = tie(a_own, b_own, c_z)
+    a_own, b_own, near = tie(a_own, b_own, c_z[0])
+    c_z = [near] + c_z[1:]
     a_full = gather_quad(gather_rest(a_own), 2)
     c = added(c[0], *c_z)
     c_own = own_sum(*[

time: 349 us -> 347 us (level)
  waiting for transfers between devices: 86.5 us -> 91.3 us
  starting transfers between devices: 50 us -> 45.3 us
    ppermute x33, starting transfers between devices: 37.2 us -> 32.8 us  [swap_xor(): return lax.ppermute(value, 'dp', [(i, i ^ mask) for i in range(size)])]
    unnamed x87 -> x99, local copies, waits for them, and re-layouts: 10.3 us -> 11.5 us
  transfers between devices with their start and end apart: 43 -> 43, of which waited for: 17 -> 17; matrix products, arithmetic and copies ran while one was open for 5% -> 5% of each run, Pallas kernels for 22% -> 21%
where the time goes in v6:
time: 347 us; the launch traced here: 343 us
  Pallas kernels  162 us (47%)
  waiting for transfers between devices  91.3 us (26%)
  starting transfers between devices  45.3 us (13%)
  local copies, waits for them, and re-layouts  17.9 us (5%)
  between operations  14.8 us (4%)
  other arithmetic  12.4 us (4%)
    pallas_call x5, Pallas kernels, call(): pl.pallas_call(kernel, out_shape=tuple(outs), grid_spec=pltpu.PrefetchSca...  148 us
    ppermute x33, waiting for transfers between devices, swap_xor(): return lax.ppermute(value, 'dp', [(i, i ^ mask) for i in range(size)])  79.9 us
    ppermute x33, starting transfers between devices, swap_xor(): return lax.ppermute(value, 'dp', [(i, i ^ mask) for i in range(size)])  32.8 us
    ppermute x9, starting transfers between devices, swap_section(): return lax.ppermute(value, 'section', [(0, 1), (1, 0)])  12.5 us
    unnamed x99, local copies, waits for them, and re-layouts  11.5 us
    ppermute x9, waiting for transfers between devices, swap_section(): return lax.ppermute(value, 'section', [(0, 1), (1, 0)])  11.4 us
    pallas_call x2, Pallas kernels, finish(): pl.pallas_call(functools.partial(finish_kernel, widths=widths, targets=fl...  9.04 us
  transfers between devices with their start and end apart: 43, of which 17 were waited for; matrix products, arithmetic and copies ran while one was open for 5% of the time, Pallas kernels for 21%

profile of v6, /device:TPU:0, one launch (start us, length us, event | category | flops | bytes accessed | tf_op | source)
XLA Modules:
  0.0 343.4 jit_solution(5574608912833761285)
XLA Ops:
  9.4 3.0 collective-permute-start
  12.6 1.9 dynamic-slice_bitcast_fusion.1
  14.5 2.0 collective-permute-start.5
  16.5 8.8 %collective-permute-done.1 = f32[2,512]{1,0:T(2,128)S(1)} collective-permute-done((f32[2,512]{1,0:T(2,128)S(1)}, f32[2,512]{1,0:T(2,128)S(1)}, u32[]{:S(2)}, u32[]{:S(2)}) %collective-permute-start.1) | collective-permute-done | bytes 4128 | tf_op jit(solution)/shard_map/ppermute | solution.py:840
  25.3 2.0 collective-permute-start.3
  29.9 7.7 %collective-permute-done.3.refs_3_.refs_8_.refs_11_ = bf16[128,2048]{1,0:T(8,128)(2,1)S(1)} collective-permute-done((bf16[128,2048]{1,0:T(8,128)(2,1)S(1)}, bf16[128,2048]{1,0:T(8,128)(2,1)S(1)}, u32[]{:S(2)}, u32[]{:S(2)}) %collective-permute-start.3) | collective-permute-done | bytes 524320 | tf_op jit(solution)/shard_map/ppermute | solution.py:836
  41.5 16.4 %shard_map.161 = (bf16[512,1536]{1,0:T(8,128)(2,1)}, f32[1,1536]{1,0:T(1,128)}, bf16[1536,1536]{1,0:T(8,128)(2,1)}, bf16[1536,512]{1,0:T(8,128)(2,1)}, bf16[1536...) custom-call(s32[9]{0:T(128)} %concatenate.52.meta_ref, ...), custom_call_target="tpu_custom_call" | custom-call | tf_op jit(solution)/shard_map/pallas_call | solution.py:603
  58.7 3.1 collective-permute-done.9.refs_4_.refs_14_.refs_7_
  62.9 15.8 %shard_map.162 = (bf16[1536,512]{1,0:T(8,128)(2,1)}, bf16[2048,1536]{1,0:T(8,128)(2,1)}, bf16[2048,1536]{1,0:T(8,128)(2,1)}) custom-call(s32[9]{0:T(128)} %concatenate.52.meta_ref, f32[512,1536]{1,0:T(8,128)} %get-tuple-element.135.hid_ref, bf16[512,1536]{1,0:T(8,128)(2,1)} %get-tuple-element.136.sec_ref, bf16[512,2048]{1,0:T(8,128)(2,1)} %bitcast.29, ...), custom_call_target="tpu_custom_call" | custom-call | tf_op jit(solution)/shard_map/pallas_call | solution.py:603
  78.8 68.5 %shard_map.163 = (bf16[1536,512]{1,0:T(8,128)(2,1)}, bf16[1536,512]{1,0:T(8,128)(2,1)}, bf16[16,288,512]{2,1,0:T(8,128)(2,1)}, bf16[896,512]{1,0:T(8,128)(2,1)}, bf16[896,512]{1,0:T(8,128)(2,1)}) custom-call(s32[9]{0:T(128)} %concatenate.52.meta_ref, bf16[1536,512]{1,0:T(8,128)(2,1)} %get-tuple-element.183.x_ref, bf16[3072,512]{1,0:T(8,128)(2,1)} %cot_ref.1, ...), custom_call_target="tpu_custom_call" | custom-call | tf_op jit(solution)/shard_map/pallas_call | solution.py:603
  150.8 28.8 %shard_map.164 = (bf16[2304,512]{1,0:T(8,128)(2,1)}, bf16[2304,512]{1,0:T(8,128)(2,1)}, f32[1,512]{1,0:T(1,128)}, f32[512,1536]{1,0:T(8,128)}, bf16[512,1536]{1,0:T(8,128)(2,1)}) custom-call(s32[9]{0:T(128)} %concatenate.52.meta_ref, bf16[1536,512]{1,0:T(8,128)(2,1)} %get-tuple-element.141.seed_ref, bf16[2048,1536]{1,0:T(8,128)(2,1)} %get-tuple-element.142.act_ref, ...), custom_call_target="tpu_custom_call" | custom-call | tf_op jit(solution)/shard_map/pallas_call | solution.py:603
  180.2 4.4 %collective-permute-done.13.refs_1_ = bf16[2304,512]{1,0:T(8,128)(2,1)S(1)} collective-permute-done((bf16[2304,512]{1,0:T(8,128)(2,1)}, bf16[2304,512]{1,0:T(8,128)(2,1)S(1)}, u32[]{:S(2)}, u32[]{:S(2)}) %collective-permute-start.13) | collective-permute-done | bytes 2359328 | tf_op jit(solution)/shard_map/ppermute | solution.py:836
  192.0 2.6 collective-permute-start.16
  196.3 18.1 %shard_map.166 = (bf16[1536,512]{1,0:T(8,128)(2,1)S(1)}, bf16[896,512]{1,0:T(8,128)(2,1)}, bf16[896,512]{1,0:T(8,128)(2,1)S(1)}) custom-call(s32[9]{0:T(128)S(1)} %copy-done.18, f32[512,1536]{1,0:T(8,128)} %get-tuple-element.164.gh_ref, bf16[512,1536]{1,0:T(8,128)(2,1)S(1)} %copy-done.11, bf16[512,1536]{1,0:T(8,128)(2,1)S(1)} %copy-done.9, ...), custom_call_target="tpu_custom_call" | custom-call | tf_op jit(solution)/shard_map/pallas_call | solution.py:603
  220.6 1.9 shard_map.167
  225.0 3.4 collective-permute-start.21
  228.6 19.5 %collective-permute-done.23 = bf16[960,512]{1,0:T(8,128)(2,1)} collective-permute-done((bf16[960,512]{1,0:T(8,128)(2,1)}, bf16[960,512]{1,0:T(8,128)(2,1)}, u32[]{:S(2)}, u32[]{:S(2)}) %collective-permute-start.23) | collective-permute-done | bytes 983072 | tf_op jit(solution)/shard_map/ppermute | solution.py:836
  252.3 1.9 collective-permute-start.24
  256.2 2.0 collective-permute-start.30
  258.8 2.3 collective-permute-done.24.refs_1_
  262.2 7.4 %collective-permute-done.30 = bf16[224,512]{1,0:T(8,128)(2,1)S(1)} collective-permute-done((bf16[224,512]{1,0:T(8,128)(2,1)S(1)}, bf16[224,512]{1,0:T(8,128)(2,1)S(1)}, u32[]{:S(2)}, u32[]{:S(2)}) %collective-permute-start.30) | collective-permute-done | bytes 229408 | tf_op jit(solution)/shard_map/ppermute | solution.py:836
  269.6 8.8 %collective-permute-done.29 = bf16[224,512]{1,0:T(8,128)(2,1)S(1)} collective-permute-done((bf16[224,512]{1,0:T(8,128)(2,1)S(1)}, bf16[224,512]{1,0:T(8,128)(2,1)S(1)}, u32[]{:S(2)}, u32[]{:S(2)}) %collective-permute-start.29) | collective-permute-done | bytes 229408 | tf_op jit(solution)/shard_map/ppermute | solution.py:836
  280.0 3.2 collective-permute-start.27
  285.5 4.7 %collective-permute-done.26 = bf16[224,512]{1,0:T(8,128)(2,1)S(1)} collective-permute-done((bf16[224,512]{1,0:T(8,128)(2,1)S(1)}, bf16[224,512]{1,0:T(8,128)(2,1)S(1)}, u32[]{:S(2)}, u32[]{:S(2)}) %collective-permute-start.26) | collective-permute-done | bytes 229408 | tf_op jit(solution)/shard_map/ppermute | solution.py:836
  290.1 9.1 %collective-permute-done.27 = bf16[224,512]{1,0:T(8,128)(2,1)S(1)} collective-permute-done((bf16[224,512]{1,0:T(8,128)(2,1)S(1)}, bf16[224,512]{1,0:T(8,128)(2,1)S(1)}, u32[]{:S(2)}, u32[]{:S(2)}) %collective-permute-start.27) | collective-permute-done | bytes 229408 | tf_op jit(solution)/shard_map/ppermute | solution.py:836
  300.6 3.2 collective-permute-start.32
  306.2 1.9 pad_maximum_fusion
  308.4 8.3 %collective-permute-done.33 = bf16[160,512]{1,0:T(8,128)(2,1)S(1)} collective-permute-done((bf16[160,512]{1,0:T(8,128)(2,1)S(1)}, bf16[160,512]{1,0:T(8,128)(2,1)S(1)}, u32[]{:S(2)}, u32[]{:S(2)}) %collective-permute-start.33) | collective-permute-done | bytes 163872 | tf_op jit(solution)/shard_map/ppermute | solution.py:836
  319.1 1.9 pad_maximum_fusion.1
  321.6 4.9 %shard_map.171 = (f32[2048,512]{1,0:T(8,128)}, f32[512,2048]{1,0:T(8,128)}, f32[512,512]{1,0:T(8,128)}) custom-call(s32[9]{0:T(128)S(1)} %copy-done.18, bf16[896,512]{1,0:T(8,128)(2,1)S(1)} %pad_maximum_fusion.3.refs_0_, bf16[896,512]{1,0:T(8,128)(2,1)S(1)} %collective-permute-done.37.refs_1_, bf16[896,512]{1,0:T(8,128)(2,1)S(1)} %collective-permute-done.38.refs_2_, ...), custom_call_target="tpu_custom_call" | custom-call | tf_op jit(solution)/shard_map/pallas_call | solution.py:818
  326.6 3.8 %collective-permute-done.35.refs_2_ = bf16[640,512]{1,0:T(8,128)(2,1)S(1)} collective-permute-done((bf16[640,512]{1,0:T(8,128)(2,1)S(1)}, bf16[640,512]{1,0:T(8,128)(2,1)S(1)}, u32[]{:S(2)}, u32[]{:S(2)}) %collective-permute-start.35) | collective-permute-done | bytes 655392 | tf_op jit(solution)/shard_map/ppermute | solution.py:836
  332.4 4.1 %shard_map.172 = (f32[512,2048]{1,0:T(8,128)}, f32[512,1536]{1,0:T(8,128)}) custom-call(s32[9]{0:T(128)S(1)} %copy-done.18, bf16[640,512]{1,0:T(8,128)(2,1)S(1)} %pad_maximum_fusion.4.refs_0_, bf16[640,512]{1,0:T(8,128)(2,1)S(1)} %collective-permute-done.40.refs_1_, ...), custom_call_target="tpu_custom_call", output_to_operand_aliasing={{0}: (5, {})} | custom-call | tf_op jit(solution)/shard_map/pallas_call | solution.py:818
  (206 shorter events, 53.2 us)
Async XLA Ops:
  7.2 240.9 %reduce-scatter.2.cloned.1.call-start = ((), (), s32[]{:S(2)}) async-start(), calls=%async_computation.1 | async-start | bytes 5013504 | tf_op jit(solution)/shard_map/reduce_scatter | solution.py:990
  9.4 15.9 %collective-permute-start = (bf16[128,2048]{1,0:T(8,128)(2,1)S(1)}, bf16[128,2048]{1,0:T(8,128)(2,1)S(1)}, u32[]{:S(2)}, u32[]{:S(2)}) collective-permute-start(bf16[128,2048]{1,0:T(8,128)(2,1)S(1)} %pad_maximum_fusion.5), channel_id=1, source_target_pairs={{0,16},{16,0},{1,17},{17,1},{2,18},{18,2},{3,19},{19,3},{4,20},{20... | collective-permute-start | bytes 1572872 | tf_op jit(solution)/shard_map/ppermute | solution.py:840
  12.5 12.8 %collective-permute-start.1 = (f32[2,512]{1,0:T(2,128)S(1)}, f32[2,512]{1,0:T(2,128)S(1)}, u32[]{:S(2)}, u32[]{:S(2)}) collective-permute-start(f32[2,512]{1,0:T(2,128)S(1)} %pad_maximum_fusion.11), channel_id=1, source_target_pairs={{0,16},{16,0},{1,17},{17,1},{2,18},{18,2},{3,19},{19,3},{4,20},{20... | collective-permute-start | bytes 12296 | tf_op jit(solution)/shard_map/ppermute | solution.py:840
  14.5 23.1 %collective-permute-start.5 = (bf16[128,2048]{1,0:T(8,128)(2,1)}, bf16[128,2048]{1,0:T(8,128)(2,1)}, u32[]{:S(2)}, u32[]{:S(2)}) collective-permute-start(bf16[128,2048]{1,0:T(8,128)(2,1)} %dynamic-slice_bitcast_fusion.1), channel_id=1, source_target_pairs={{0,16},{16,0},{1,17},{17,1},{2,18},{18,2},{3,19},{19,3},{4,20},{20... | collective-permute-start | bytes 1572872 | tf_op jit(solution)/shard_map/ppermute | solution.py:840
  25.3 12.3 %collective-permute-start.3 = (bf16[128,2048]{1,0:T(8,128)(2,1)S(1)}, bf16[128,2048]{1,0:T(8,128)(2,1)S(1)}, u32[]{:S(2)}, u32[]{:S(2)}) collective-permute-start(bf16[128,2048]{1,0:T(8,128)(2,1)S(1)} %collective-permute-done.refs_1_.refs_6_.refs_9_), channel_id=1, source_target_pairs={{0,2},{1,3},{2,0},{3,1},{4,6},{5,7},{6,4},{7,5},{8,10},{9,11},{10,... | collective-permute-start | bytes 1572872 | tf_op jit(solution)/shard_map/ppermute | solution.py:836
  28.4 29.8 %collective-permute-start.8 = (bf16[1024,512]{1,0:T(8,128)(2,1)}, bf16[1024,512]{1,0:T(8,128)(2,1)S(1)}, u32[]{:S(2)}, u32[]{:S(2)}) collective-permute-start(bf16[1024,512]{1,0:T(8,128)(2,1)} %dynamic-slice_bitcast_fusion), channel_id=1, source_target_pairs={{0,16},{16,0},{1,17},{17,1},{2,18},{18,2},{3,19},{19,3},{4,20},{20... | collective-permute-start | bytes 3145736 | tf_op jit(solution)/shard_map/ppermute | solution.py:840
  29.9 10.6 %collective-permute-start.2 = (bf16[128,2048]{1,0:T(8,128)(2,1)S(1)}, bf16[128,2048]{1,0:T(8,128)(2,1)S(1)}, u32[]{:S(2)}, u32[]{:S(2)}) collective-permute-start(bf16[128,2048]{1,0:T(8,128)(2,1)S(1)} %collective-permute-done.refs_1_.refs_6_.refs_9_), channel_id=1, source_target_pairs={{0,1},{1,0},{2,3},{3,2},{4,5},{5,4},{6,7},{7,6},{8,9},{9,8},{10,11... | collective-permute-start | bytes 1572872 | tf_op jit(solution)/shard_map/ppermute | solution.py:836
  37.6 20.2 %collective-permute-start.6 = (bf16[128,2048]{1,0:T(8,128)(2,1)}, bf16[128,2048]{1,0:T(8,128)(2,1)}, u32[]{:S(2)}, u32[]{:S(2)}) collective-permute-start(bf16[128,2048]{1,0:T(8,128)(2,1)} %collective-permute-done.5.refs_1_.refs_11_.refs_4_), channel_id=1, source_target_pairs={{0,2},{1,3},{2,0},{3,1},{4,6},{5,7},{6,4},{7,5},{8,10},{9,11},{10,... | collective-permute-start | bytes 1572872 | tf_op jit(solution)/shard_map/ppermute | solution.py:836
  39.0 18.8 %collective-permute-start.7 = (bf16[128,2048]{1,0:T(8,128)(2,1)}, bf16[128,2048]{1,0:T(8,128)(2,1)}, u32[]{:S(2)}, u32[]{:S(2)}) collective-permute-start(bf16[128,2048]{1,0:T(8,128)(2,1)} %collective-permute-done.5.refs_1_.refs_11_.refs_4_), channel_id=1, source_target_pairs={{0,1},{1,0},{2,3},{3,2},{4,5},{5,4},{6,7},{7,6},{8,9},{9,8},{10,11... | collective-permute-start | bytes 1572872 | tf_op jit(solution)/shard_map/ppermute | solution.py:836
  149.3 30.4 %collective-permute-start.11 = (bf16[1024,512]{1,0:T(8,128)(2,1)S(1)}, bf16[1024,512]{1,0:T(8,128)(2,1)S(1)}, u32[]{:S(2)}, u32[]{:S(2)}) collective-permute-start(bf16[1024,512]{1,0:T(8,128)(2,1)S(1)} %slice_select_fusion), channel_id=1, source_target_pairs={{0,16},{16,0},{1,17},{17,1},{2,18},{18,2},{3,19},{19,3},{4,20},{20... | collective-permute-start | bytes 3145736 | tf_op jit(solution)/shard_map/ppermute | solution.py:840
  150.7 28.9 %collective-permute-start.12 = (bf16[896,512]{1,0:T(8,128)(2,1)}, bf16[896,512]{1,0:T(8,128)(2,1)S(1)}, u32[]{:S(2)}, u32[]{:S(2)}) collective-permute-start(bf16[896,512]{1,0:T(8,128)(2,1)} %get-tuple-element.153), channel_id=1, source_target_pairs={{0,1},{1,0},{2,3},{3,2},{4,5},{5,4},{6,7},{7,6},{8,9},{9,8},{10,11... | collective-permute-start | bytes 2752520 | tf_op jit(solution)/shard_map/ppermute | solution.py:836
  187.5 27.9 %collective-permute-start.14 = (bf16[896,512]{1,0:T(8,128)(2,1)S(1)}, bf16[896,512]{1,0:T(8,128)(2,1)S(1)}, u32[]{:S(2)}, u32[]{:S(2)}) collective-permute-start(bf16[896,512]{1,0:T(8,128)(2,1)S(1)} %get-tuple-element.178), channel_id=1, source_target_pairs={{0,2},{1,3},{2,0},{3,1},{4,6},{5,7},{6,4},{7,5},{8,10},{9,11},{10,... | collective-permute-start | bytes 2752520 | tf_op jit(solution)/shard_map/ppermute | solution.py:836
  190.1 25.2 %collective-permute-start.18 = (bf16[512,512]{1,0:T(8,128)(2,1)S(1)}, bf16[512,512]{1,0:T(8,128)(2,1)S(1)}, u32[]{:S(2)}, u32[]{:S(2)}) collective-permute-start(bf16[512,512]{1,0:T(8,128)(2,1)S(1)} %slice_select_fusion.1), channel_id=1, source_target_pairs={{0,16},{16,0},{1,17},{17,1},{2,18},{18,2},{3,19},{19,3},{4,20},{20... | collective-permute-start | bytes 1572872 | tf_op jit(solution)/shard_map/ppermute | solution.py:840
  190.4 24.9 %collective-permute-start.15 = (bf16[128,512]{1,0:T(8,128)(2,1)S(1)}, bf16[128,512]{1,0:T(8,128)(2,1)}, u32[]{:S(2)}, u32[]{:S(2)}) collective-permute-start(bf16[128,512]{1,0:T(8,128)(2,1)S(1)} %get-tuple-element.179), channel_id=1, source_target_pairs={{0,4},{1,5},{2,6},{3,7},{4,0},{5,1},{6,2},{7,3},{8,12},{9,13},{10,... | collective-permute-start | bytes 393224 | tf_op jit(solution)/shard_map/ppermute | solution.py:836
  192.0 23.4 %collective-permute-start.16 = (bf16[128,512]{1,0:T(8,128)(2,1)S(1)}, bf16[128,512]{1,0:T(8,128)(2,1)}, u32[]{:S(2)}, u32[]{:S(2)}) collective-permute-start(bf16[128,512]{1,0:T(8,128)(2,1)S(1)} %get-tuple-element.180), channel_id=1, source_target_pairs={{0,8},{1,9},{2,10},{3,11},{4,12},{5,13},{6,14},{7,15},{8,0},{9,1},... | collective-permute-start | bytes 393224 | tf_op jit(solution)/shard_map/ppermute | solution.py:836
  194.6 20.7 %collective-permute-start.17 = (bf16[128,512]{1,0:T(8,128)(2,1)S(1)}, bf16[128,512]{1,0:T(8,128)(2,1)S(1)}, u32[]{:S(2)}, u32[]{:S(2)}) collective-permute-start(bf16[128,512]{1,0:T(8,128)(2,1)S(1)} %get-tuple-element.181), channel_id=1, source_target_pairs={{0,12},{1,13},{2,14},{3,15},{4,8},{5,9},{6,10},{7,11},{8,4},{9,5},... | collective-permute-start | bytes 393224 | tf_op jit(solution)/shard_map/ppermute | solution.py:836
  223.6 24.5 %collective-permute-start.23 = (bf16[960,512]{1,0:T(8,128)(2,1)}, bf16[960,512]{1,0:T(8,128)(2,1)}, u32[]{:S(2)}, u32[]{:S(2)}) collective-permute-start(bf16[960,512]{1,0:T(8,128)(2,1)} %pad_maximum_fusion.2), channel_id=1, source_target_pairs={{0,2},{1,3},{2,0},{3,1},{4,6},{5,7},{6,4},{7,5},{8,10},{9,11},{10,... | collective-permute-start | bytes 2949128 | tf_op jit(solution)/shard_map/ppermute | solution.py:836
  224.2 27.1 %collective-permute-start.20 = (bf16[224,512]{1,0:T(8,128)(2,1)}, bf16[224,512]{1,0:T(8,128)(2,1)S(1)}, u32[]{:S(2)}, u32[]{:S(2)}) collective-permute-start(bf16[224,512]{1,0:T(8,128)(2,1)} %get-tuple-element.187), channel_id=1, source_target_pairs={{0,4},{1,5},{2,6},{3,7},{4,0},{5,1},{6,2},{7,3},{8,12},{9,13},{10,... | collective-permute-start | bytes 688136 | tf_op jit(solution)/shard_map/ppermute | solution.py:836
  225.0 26.2 %collective-permute-start.21 = (bf16[224,512]{1,0:T(8,128)(2,1)}, bf16[224,512]{1,0:T(8,128)(2,1)S(1)}, u32[]{:S(2)}, u32[]{:S(2)}) collective-permute-start(bf16[224,512]{1,0:T(8,128)(2,1)} %get-tuple-element.188), channel_id=1, source_target_pairs={{0,8},{1,9},{2,10},{3,11},{4,12},{5,13},{6,14},{7,15},{8,0},{9,1},... | collective-permute-start | bytes 688136 | tf_op jit(solution)/shard_map/ppermute | solution.py:836
  228.4 22.9 %collective-permute-start.22 = (bf16[224,512]{1,0:T(8,128)(2,1)}, bf16[224,512]{1,0:T(8,128)(2,1)S(1)}, u32[]{:S(2)}, u32[]{:S(2)}) collective-permute-start(bf16[224,512]{1,0:T(8,128)(2,1)} %get-tuple-element.189), channel_id=1, source_target_pairs={{0,12},{1,13},{2,14},{3,15},{4,8},{5,9},{6,10},{7,11},{8,4},{9,5},... | collective-permute-start | bytes 688136 | tf_op jit(solution)/shard_map/ppermute | solution.py:836
  256.2 13.4 %collective-permute-start.30 = (bf16[224,512]{1,0:T(8,128)(2,1)S(1)}, bf16[224,512]{1,0:T(8,128)(2,1)S(1)}, u32[]{:S(2)}, u32[]{:S(2)}) collective-permute-start(bf16[224,512]{1,0:T(8,128)(2,1)S(1)} %pad_maximum_fusion.9), channel_id=1, source_target_pairs={{0,12},{1,13},{2,14},{3,15},{4,8},{5,9},{6,10},{7,11},{8,4},{9,5},... | collective-permute-start | bytes 688136 | tf_op jit(solution)/shard_map/ppermute | solution.py:836
  258.2 20.2 %collective-permute-start.29 = (bf16[224,512]{1,0:T(8,128)(2,1)S(1)}, bf16[224,512]{1,0:T(8,128)(2,1)S(1)}, u32[]{:S(2)}, u32[]{:S(2)}) collective-permute-start(bf16[224,512]{1,0:T(8,128)(2,1)S(1)} %pad_maximum_fusion.8), channel_id=1, source_target_pairs={{0,8},{1,9},{2,10},{3,11},{4,12},{5,13},{6,14},{7,15},{8,0},{9,1},... | collective-permute-start | bytes 688136 | tf_op jit(solution)/shard_map/ppermute | solution.py:836
  280.0 10.2 %collective-permute-start.26 = (bf16[224,512]{1,0:T(8,128)(2,1)S(1)}, bf16[224,512]{1,0:T(8,128)(2,1)S(1)}, u32[]{:S(2)}, u32[]{:S(2)}) collective-permute-start(bf16[224,512]{1,0:T(8,128)(2,1)S(1)} %get-tuple-element.211), channel_id=1, source_target_pairs={{0,4},{1,5},{2,6},{3,7},{4,0},{5,1},{6,2},{7,3},{8,12},{9,13},{10,... | collective-permute-start | bytes 688136 | tf_op jit(solution)/shard_map/ppermute | solution.py:836
  280.0 19.2 %collective-permute-start.27 = (bf16[224,512]{1,0:T(8,128)(2,1)S(1)}, bf16[224,512]{1,0:T(8,128)(2,1)S(1)}, u32[]{:S(2)}, u32[]{:S(2)}) collective-permute-start(bf16[224,512]{1,0:T(8,128)(2,1)S(1)} %get-tuple-element.211), channel_id=1, source_target_pairs={{0,8},{1,9},{2,10},{3,11},{4,12},{5,13},{6,14},{7,15},{8,0},{9,1},... | collective-permute-start | bytes 688136 | tf_op jit(solution)/shard_map/ppermute | solution.py:836
  283.2 16.0 %collective-permute-start.28 = (bf16[224,512]{1,0:T(8,128)(2,1)S(1)}, bf16[224,512]{1,0:T(8,128)(2,1)S(1)}, u32[]{:S(2)}, u32[]{:S(2)}) collective-permute-start(bf16[224,512]{1,0:T(8,128)(2,1)S(1)} %get-tuple-element.211), channel_id=1, source_target_pairs={{0,12},{1,13},{2,14},{3,15},{4,8},{5,9},{6,10},{7,11},{8,4},{9,5},... | collective-permute-start | bytes 688136 | tf_op jit(solution)/shard_map/ppermute | solution.py:836
  284.7 34.1 %collective-permute-start.36 = (bf16[1536,512]{1,0:T(8,128)(2,1)S(1)}, bf16[1536,512]{1,0:T(8,128)(2,1)S(1)}, u32[]{:S(2)}, u32[]{:S(2)}) collective-permute-start(bf16[1536,512]{1,0:T(8,128)(2,1)S(1)} %broadcast_select_fusion.2), channel_id=1, source_target_pairs={{0,16},{16,0},{1,17},{17,1},{2,18},{18,2},{3,19},{19,3},{4,20},{20... | collective-permute-start | bytes 4718600 | tf_op jit(solution)/shard_map/ppermute | solution.py:840
  299.5 18.8 %collective-permute-start.38 = (bf16[896,512]{1,0:T(8,128)(2,1)S(1)}, bf16[896,512]{1,0:T(8,128)(2,1)S(1)}, u32[]{:S(2)}, u32[]{:S(2)}) collective-permute-start(bf16[896,512]{1,0:T(8,128)(2,1)S(1)} %pad_maximum_fusion.3.refs_0_), channel_id=1, source_target_pairs={{0,2},{1,3},{2,0},{3,1},{4,6},{5,7},{6,4},{7,5},{8,10},{9,11},{10,... | collective-permute-start | bytes 2752520 | tf_op jit(solution)/shard_map/ppermute | solution.py:836
  303.8 13.0 %collective-permute-start.33 = (bf16[160,512]{1,0:T(8,128)(2,1)S(1)}, bf16[160,512]{1,0:T(8,128)(2,1)S(1)}, u32[]{:S(2)}, u32[]{:S(2)}) collective-permute-start(bf16[160,512]{1,0:T(8,128)(2,1)S(1)} %pad_maximum_fusion.10), channel_id=1, source_target_pairs={{0,8},{1,9},{2,10},{3,11},{4,12},{5,13},{6,14},{7,15},{8,0},{9,1},... | collective-permute-start | bytes 491528 | tf_op jit(solution)/shard_map/ppermute | solution.py:836
  304.7 12.1 %collective-permute-start.34 = (bf16[160,512]{1,0:T(8,128)(2,1)S(1)}, bf16[160,512]{1,0:T(8,128)(2,1)S(1)}, u32[]{:S(2)}, u32[]{:S(2)}) collective-permute-start(bf16[160,512]{1,0:T(8,128)(2,1)S(1)} %pad_maximum_fusion.10), channel_id=1, source_target_pairs={{0,12},{1,13},{2,14},{3,15},{4,8},{5,9},{6,10},{7,11},{8,4},{9,5},... | collective-permute-start | bytes 491528 | tf_op jit(solution)/shard_map/ppermute | solution.py:836
  308.4 12.5 %collective-permute-start.37 = (bf16[896,512]{1,0:T(8,128)(2,1)S(1)}, bf16[896,512]{1,0:T(8,128)(2,1)S(1)}, u32[]{:S(2)}, u32[]{:S(2)}) collective-permute-start(bf16[896,512]{1,0:T(8,128)(2,1)S(1)} %pad_maximum_fusion.3.refs_0_), channel_id=1, source_target_pairs={{0,1},{1,0},{2,3},{3,2},{4,5},{5,4},{6,7},{7,6},{8,9},{9,8},{10,11... | collective-permute-start | bytes 2752520 | tf_op jit(solution)/shard_map/ppermute | solution.py:836
  316.9 13.4 %collective-permute-start.35 = (bf16[640,512]{1,0:T(8,128)(2,1)S(1)}, bf16[640,512]{1,0:T(8,128)(2,1)S(1)}, u32[]{:S(2)}, u32[]{:S(2)}) collective-permute-start(bf16[640,512]{1,0:T(8,128)(2,1)S(1)} %pad_maximum_fusion.4.refs_0_), channel_id=1, source_target_pairs={{0,2},{1,3},{2,0},{3,1},{4,6},{5,7},{6,4},{7,5},{8,10},{9,11},{10,... | collective-permute-start | bytes 1966088 | tf_op jit(solution)/shard_map/ppermute | solution.py:836
  318.2 12.7 %collective-permute-start.40 = (bf16[640,512]{1,0:T(8,128)(2,1)S(1)}, bf16[640,512]{1,0:T(8,128)(2,1)S(1)}, u32[]{:S(2)}, u32[]{:S(2)}) collective-permute-start(bf16[640,512]{1,0:T(8,128)(2,1)S(1)} %pad_maximum_fusion.4.refs_0_), channel_id=1, source_target_pairs={{0,1},{1,0},{2,3},{3,2},{4,5},{5,4},{6,7},{7,6},{8,9},{9,8},{10,11... | collective-permute-start | bytes 1966088 | tf_op jit(solution)/shard_map/ppermute | solution.py:836
  (60 other events, 449.6 us)
Sparse Core Ops, SparseCore 0:
  147.4 93.9 reduce-scatter.1
